TPU v7x, 32 devices: a whole 2x2x4 slice. The times are simulated.
32 devices in a mesh: dp: 4 (over x, core), gx: 2 (over y), gy: 4 (over z).
Axes of the slice: x: 2, y: 2, z: 4, core: 2. Of those that a mesh axis runs over, the one named last changes fastest.
Arguments:
- field: bfloat16 [4, 32, 128, 128, 128], P('dp', None, 'gx', 'gy'), may hold values from -6 to 6
- cotangent: bfloat16 [4, 32, 128, 128, 128], P('dp', None, 'gx', 'gy'), may hold values from -6 to 6
- spectral_weight: float32 [16, 32, 16, 2, 1024], P('gy', 'gx'), may hold values from -8 to 8
Outputs:
- field_out: bfloat16 [4, 32, 128, 128, 128], P('dp', None, 'gx', 'gy')
- grad_field: bfloat16 [4, 32, 128, 128, 128], P('dp', None, 'gx', 'gy')
- weight_grad: float32 [16, 32, 16, 2, 1024], P('gy', 'gx', 'dp')
All inputs are finite; a program needn't handle non-finite values.
Results may differ from a plain program's by a relative error of at most 0.0057.
Values may be sent and summed in bfloat16 or wider, within the bound.
No kernel may reach another device: no remote copies, remote signals or barrier semaphores. Data moves between devices by JAX's collectives and lax.ppermute only.
A program may use at most 320 MiB of HBM per device.

v0:
```python
import math

import jax
import jax.numpy as jnp
from jax import lax
from jax.sharding import PartitionSpec as P

CHANNELS = 32
NX = 128
NY = 128
NZ = 128
MX = 16
MY = 16
MZ = 32


PRECISE = lax.Precision.HIGHEST


def mode_list(length, count):
    half_ids = jnp.arange(count // 2, dtype=jnp.int32)
    return jnp.concatenate([half_ids, length - count // 2 + half_ids])


def phase_tables(length, mode_ids):
    cell_ids = jnp.arange(length, dtype=jnp.int32)
    turn_ids = cell_ids[:, None] * mode_ids[None, :] % length
    angles = turn_ids.astype(jnp.float32) * (2.0 * math.pi / length)
    return (jnp.cos(angles), jnp.sin(angles))


def depth_scales():
    mode_ids = jnp.arange(MZ, dtype=jnp.int32)
    return jnp.where(mode_ids == 0, 1.0, 2.0).astype(jnp.float32) / float(NX * NY * NZ)


def depth_forward(scale_vec):
    cosine, sine_tab = phase_tables(NZ, jnp.arange(MZ, dtype=jnp.int32))
    table_in = jnp.stack([cosine, -sine_tab], axis=2) * scale_vec[None, :, None]
    return table_in.astype(jnp.bfloat16)


def depth_inverse(scale_vec):
    cosine, sine_tab = phase_tables(NZ, jnp.arange(MZ, dtype=jnp.int32))
    return jnp.stack([cosine.T, -sine_tab.T], axis=1) * scale_vec[:, None, None]


def spectral_lead(data_in, length, count):
    cosine, sine_tab = phase_tables(length, mode_list(length, count))
    part_c = jnp.einsum("lkpr,lm->mkpr", data_in, cosine, precision=PRECISE)
    part_s = jnp.einsum("lkpr,lm->mkpr", data_in, sine_tab, precision=PRECISE)
    real_part = part_c[:, :, 0] + part_s[:, :, 1]
    imag_part = part_c[:, :, 1] - part_s[:, :, 0]
    return jnp.stack([real_part, imag_part], axis=2)


def synthesis_lead(data_in, length, count):
    cosine, sine_tab = phase_tables(length, mode_list(length, count))
    part_c = jnp.einsum("mkpr,lm->lkpr", data_in, cosine, precision=PRECISE)
    part_s = jnp.einsum("mkpr,lm->lkpr", data_in, sine_tab, precision=PRECISE)
    real_part = part_c[:, :, 0] - part_s[:, :, 1]
    imag_part = part_s[:, :, 0] + part_c[:, :, 1]
    return jnp.stack([real_part, imag_part], axis=2)


def spectral_rows(data_in, length, count):
    cosine, sine_tab = phase_tables(length, mode_list(length, count))
    part_c = jnp.einsum("akplc,lm->akpmc", data_in, cosine, precision=PRECISE)
    part_s = jnp.einsum("akplc,lm->akpmc", data_in, sine_tab, precision=PRECISE)
    real_part = part_c[:, :, 0] + part_s[:, :, 1]
    imag_part = part_c[:, :, 1] - part_s[:, :, 0]
    return jnp.stack([real_part, imag_part], axis=2)


def synthesis_rows(data_in, length, count):
    cosine, sine_tab = phase_tables(length, mode_list(length, count))
    part_c = jnp.einsum("akpmc,lm->akplc", data_in, cosine, precision=PRECISE)
    part_s = jnp.einsum("akpmc,lm->akplc", data_in, sine_tab, precision=PRECISE)
    real_part = part_c[:, :, 0] - part_s[:, :, 1]
    imag_part = part_s[:, :, 0] + part_c[:, :, 1]
    return jnp.stack([real_part, imag_part], axis=2)


def channel_product(left_op, right_op):
    return jnp.einsum("akjc,akjco->akjo", left_op, right_op, precision=PRECISE)


def channel_adjoint(left_op, right_op):
    return jnp.einsum("akjo,akjco->akjc", left_op, right_op, precision=PRECISE)


def outer_sum(left_op, right_op):
    return jnp.einsum("akjc,akjo->akjco", left_op, right_op, precision=PRECISE)


def mix_modes(spectrum, weight):
    real_in, imag_in = (spectrum[:, :, 0], spectrum[:, :, 1])
    w_real, w_imag = (weight[:, :, :, 0], weight[:, :, :, 1])
    real_part = channel_product(real_in, w_real) - channel_product(imag_in, w_imag)
    imag_part = channel_product(imag_in, w_real) + channel_product(real_in, w_imag)
    return jnp.stack([real_part, imag_part], axis=2)


def mix_adjoint(spectrum, weight):
    real_in, imag_in = (spectrum[:, :, 0], spectrum[:, :, 1])
    w_real, w_imag = (weight[:, :, :, 0], weight[:, :, :, 1])
    real_part = channel_adjoint(real_in, w_real) + channel_adjoint(imag_in, w_imag)
    imag_part = channel_adjoint(imag_in, w_real) - channel_adjoint(real_in, w_imag)
    return jnp.stack([real_part, imag_part], axis=2)


def weight_terms(spec_u, spec_g):
    u_real, u_imag = (spec_u[:, :, 0], spec_u[:, :, 1])
    g_real, g_imag = (spec_g[:, :, 0], spec_g[:, :, 1])
    real_part = outer_sum(u_real, g_real) + outer_sum(u_imag, g_imag)
    imag_part = outer_sum(u_real, g_imag) - outer_sum(u_imag, g_real)
    stacked = jnp.stack([real_part, imag_part], axis=3)
    lead_len, mode_len, row_len, chan_len = u_real.shape
    return stacked.reshape(lead_len, mode_len, row_len, 2, chan_len * chan_len)


def gelu_parts(pre_act):
    normal_cdf = 0.5 * (1.0 + lax.erf(pre_act * 0.7071067811865476))
    density = jnp.exp(-0.5 * pre_act * pre_act) * 0.3989422804014327
    return (pre_act * normal_cdf, normal_cdf + pre_act * density)


def depth_analyze(sample_grid, table_in):
    return jnp.einsum("cxyz,zkp->xkpyc", sample_grid, table_in, preferred_element_type=jnp.float32)


def depth_synthesize(widened, table_in):
    return jnp.einsum("xkpyc,kpz->cxyz", widened, table_in, precision=PRECISE)


def along_rows(piece_in):
    lead_len, mode_len, _, merged_len = piece_in.shape
    row_len = merged_len // CHANNELS
    shaped = piece_in.reshape(lead_len, mode_len, 2, row_len, CHANNELS)
    return spectral_rows(shaped, row_len, MY)


def to_modes(spectrum):
    return along_rows(lax.all_to_all(spectrum, "gy", split_axis=0, concat_axis=3, tiled=True))


def from_modes(spectrum):
    widened = synthesis_rows(spectrum, NY, MY)
    lead_len, mode_len, _, row_len, chan_len = widened.shape
    widened = widened.reshape(lead_len, mode_len, 2, row_len * chan_len)
    return lax.all_to_all(widened, "gy", split_axis=3, concat_axis=0, tiled=True)


def lead_forward(piece_in):
    return spectral_lead(piece_in, piece_in.shape[0], MX)


def pencil_analyze(sample_grid, table_in):
    spectrum = depth_analyze(sample_grid, table_in)
    lead_len, mode_len, _, row_len, chan_len = spectrum.shape
    spectrum = spectrum.reshape(lead_len, mode_len, 2, row_len * chan_len)
    spectrum = lead_forward(lax.all_to_all(spectrum, "gx", split_axis=1, concat_axis=0, tiled=True))
    return to_modes(spectrum)


def pencil_synthesize(spectrum, table_in):
    merged = from_modes(spectrum)
    widened = synthesis_lead(merged, NX, MX)
    returned = lax.all_to_all(widened, "gx", split_axis=0, concat_axis=1, tiled=True)
    lead_len, mode_len, _, merged_len = returned.shape
    shaped = returned.reshape(lead_len, mode_len, 2, merged_len // CHANNELS, CHANNELS)
    return depth_synthesize(shaped, table_in)


def shards(field, cotangent, spectral_weight):
    sample_grid = field[0]
    grad_out = cotangent[0]
    lead_len, mode_len, row_len = (
        spectral_weight.shape[0],
        spectral_weight.shape[1],
        spectral_weight.shape[2],
    )
    weight = spectral_weight.reshape(lead_len, mode_len, row_len, 2, CHANNELS, CHANNELS)
    unit_scale = jnp.ones((MZ,), jnp.float32)
    depth_scale = depth_scales()
    forward_plain = depth_forward(unit_scale)
    forward_scaled = depth_forward(depth_scale)
    back_scaled = depth_inverse(depth_scale)
    back_plain = depth_inverse(unit_scale)
    spec_u = pencil_analyze(sample_grid, forward_plain)
    pre_act = pencil_synthesize(mix_modes(spec_u, weight), back_scaled)
    act_value, act_slope = gelu_parts(pre_act)
    grad_pre = (grad_out.astype(jnp.float32) * act_slope).astype(jnp.bfloat16)
    spec_g = pencil_analyze(grad_pre, forward_scaled)
    grad_grid = pencil_synthesize(mix_adjoint(spec_g, weight), back_plain).astype(jnp.bfloat16)
    out_grid = act_value.astype(jnp.bfloat16)
    grad_terms = weight_terms(spec_u, spec_g)
    summed_all = lax.psum(grad_terms, "dp")
    share_len = row_len // lax.axis_size("dp")
    weight_grad = lax.dynamic_slice_in_dim(
        summed_all, lax.axis_index("dp") * share_len, share_len, 2
    )
    return (out_grid[None], grad_grid[None], weight_grad)


def solution(mesh):
    placed = (
        P("dp", None, "gx", "gy", None),
        P("dp", None, "gx", "gy", None),
        P("gy", "gx", None, None, None),
    )
    return jax.shard_map(
        shards,
        mesh=mesh,
        in_specs=placed,
        out_specs=(
            P("dp", None, "gx", "gy", None),
            P("dp", None, "gx", "gy", None),
            P("gy", "gx", "dp", None, None),
        ),
        check_vma=False,
    )
```

profile of v0, /device:TPU:0, one launch (start us, length us, event | category | flops | bytes accessed | tf_op | source)
XLA Modules:
  0.0 1969.2 jit_solution(17008958331358228359)
XLA Ops:
  7.3 24.2 %convolution_bitcast_fusion.1 = f32[64,32,2,32,32]{0,1,3,4,2:T(8,128)} fusion(bf16[32,64,32,128]{3,2,1,0:T(8,128)(2,1)} %bitcast.293, f32[128,32,1]{0,1,2:T(8,128)S(1)} %get-tuple-element.32, f32[128,32,1]{0,1,2:T(8,128)S(1)} %get-tuple-element.33), kind=kOutput, calls=%fused_computation.15 | convolution fusion | flops 1073774592 | bytes 33587200 | tf_op jit(solution)/shard_map/cxyz,zkp->xkpyc/dot_general | solution.py:129
  31.5 31.8 %copy.42 = f32[64,32,2,32,32]{0,4,3,2,1:T(8,128)} copy(f32[64,32,2,32,32]{0,1,3,4,2:T(8,128)} %convolution_bitcast_fusion.1) | data formatting | bytes 33554432 | tf_op jit(solution)/shard_map/cxyz,zkp->xkpyc/transpose | solution.py:129
  63.3 24.5 %copy.43 = f32[64,32,2,1024]{3,0,2,1:T(8,128)} copy(f32[64,32,2,1024]{0,3,2,1:T(8,128)} %bitcast.285) | data formatting | bytes 33554432 | tf_op jit(solution)/shard_map/reshape | solution.py:161
  87.8 9.9 all-to-all-start
  97.9 183.6 %all-to-all-done = f32[64,32,2,1024]{3,0,2,1:T(8,128)} async-done(((f32[64,32,2,1024]{3,0,2,1:T(8,128)}), f32[64,32,2,1024]{3,0,2,1:T(8,128)}, u32[]{:S(2)}, u32[]{:S(2)}) %all-to-all-start) | async-done | bytes 16777248 | tf_op jit(solution)/shard_map/all_to_all | solution.py:162
  281.4 6.6 copy.45
  288.0 8.8 fusion.56
  296.9 8.8 fusion.68
  314.6 23.1 %reshape.203 = f32[4,16,16,2,32,32]{5,4,3,2,1,0:T(8,128)} reshape(f32[4,16,16,2,1024]{4,3,2,1,0:T(2,128)} %param.5) | data formatting | bytes 16777216 | tf_op jit(solution)/shard_map/reshape | solution.py:183
  337.7 24.2 %all-to-all-done.1 = f32[16,16,2,1024]{3,2,1,0:T(2,128)S(1)} async-done(((f32[16,16,2,1024]{3,2,1,0:T(2,128)}), f32[16,16,2,1024]{3,2,1,0:T(2,128)S(1)}, u32[]{:S(2)}, u32[]{:S(2)}) %all-to-all-start.1) | async-done | bytes 2097184 | tf_op jit(solution)/shard_map/all_to_all | solution.py:144
  371.0 6.7 convolution_bitcast_fusion.8
  377.6 7.3 convolution_bitcast_fusion.9
  385.1 16.8 fusion.22
  401.9 13.8 fusion.19
  415.7 14.0 fusion.18
  429.7 13.9 fusion.23
  465.9 10.7 copy.52
  476.6 14.7 reshape.233
  491.3 51.0 %all_to_all.132 = f32[4,1,131072]{2,1,0:T(1,128)} all-to-all(f32[4,1,131072]{2,1,0:T(1,128)S(1)} %reshape.233), channel_id=1, replica_groups=mesh['dp'=4,'gx'=2,'gy'=4] {'gy'}, dimensions={0} | all-to-all | bytes 4194304 | tf_op jit(solution)/shard_map/all_to_all | solution.py:151
  542.9 7.7 reduce
  550.6 18.1 reshape.234
  568.7 14.4 copy.54
  585.1 16.4 fusion.54
  601.5 16.4 fusion.66
  617.9 18.8 slice_subtract_fusion.1
  636.6 6.6 pad_maximum_fusion
  643.2 17.6 copy.55
  660.8 9.8 all-to-all-start.3
  671.4 180.5 %all-to-all-done.3 = f32[128,16,2,1024]{3,2,1,0:T(2,128)} async-done(((f32[128,16,2,1024]{3,2,1,0:T(2,128)}), f32[128,16,2,1024]{3,2,1,0:T(2,128)}, u32[]{:S(2)}, u32[]{:S(2)}) %all-to-all-start.3) | async-done | bytes 16777248 | tf_op jit(solution)/shard_map/all_to_all | solution.py:169
  851.9 33.1 %copy.56 = f32[2,64,16,2,1024]{1,2,0,3,4:T(8,128)} copy(f32[2,64,16,2,1024]{4,3,2,1,0:T(2,128)} %bitcast.53) | data formatting | bytes 33554432 | tf_op jit(solution)/shard_map/all_to_all | solution.py:169
  885.0 71.3 %fusion.5 = (bf16[32,64,32,128]{3,1,0,2:T(8,128)(2,1)}, bf16[1,32,64,32,128]{4,2,1,3,0:T(8,128)(2,1)}) fusion(bf16[1,32,64,32,128]{4,3,2,1,0:T(8,128)(2,1)} %param.4, f32[64,32,2,32,32]{0,1,2,4,3:T(8,128)} %bitcast.292, f32[32,2,128,1,1]{2,0,1,4,3:T(8,128)S(1)} %fusion.200), kind=kOutput, calls=%fused_computation.6 | convolution fusion | flops 6551502848 | bytes 67141632 | tf_op jit(solution)/shard_map/xkpyc,kpz->cxyz/dot_general | solution.py:133
  956.2 24.3 %convolution_bitcast_fusion = f32[64,32,2,32,32]{0,1,3,4,2:T(8,128)} fusion(bf16[32,64,32,128]{3,1,0,2:T(8,128)(2,1)} %get-tuple-element.14, f32[128,32,1]{0,1,2:T(8,128)S(1)} %copy-done.7, f32[128,32,1]{0,1,2:T(8,128)S(1)} %copy-done.9, f32[32]{0:T(128)S(1)} %fusion.97), kind=kOutput, calls=%fused_computation.14 | convolution fusion | flops 1073766400 | bytes 33587328 | tf_op jit(solution)/shard_map/cxyz,zkp->xkpyc/dot_general | solution.py:129
  980.5 32.0 %copy.59 = f32[64,32,2,32,32]{0,4,3,2,1:T(8,128)} copy(f32[64,32,2,32,32]{0,1,3,4,2:T(8,128)} %convolution_bitcast_fusion) | data formatting | bytes 33554432 | tf_op jit(solution)/shard_map/cxyz,zkp->xkpyc/transpose | solution.py:129
  1012.4 24.5 %copy.60 = f32[64,32,2,1024]{3,0,2,1:T(8,128)} copy(f32[64,32,2,1024]{0,3,2,1:T(8,128)} %bitcast.286) | data formatting | bytes 33554432 | tf_op jit(solution)/shard_map/reshape | solution.py:161
  1036.9 186.2 %all_to_all.133 = f32[64,32,2,1024]{3,0,2,1:T(8,128)S(1)} all-to-all(f32[64,32,2,1024]{3,0,2,1:T(8,128)} %copy.60), channel_id=1, replica_groups=mesh['dp'=4,'gx'=2,'gy'=4] {'gx'}, dimensions={1} | all-to-all | bytes 33554432 | tf_op jit(solution)/shard_map/all_to_all | solution.py:162
  1225.0 8.8 fusion.52
  1233.8 8.8 fusion.64
  1244.9 50.1 %all_to_all.134 = f32[16,16,2,1024]{3,2,1,0:T(2,128)S(1)} all-to-all(f32[16,16,2,1024]{3,2,1,0:T(2,128)S(1)} %copy.63), channel_id=1, replica_groups=mesh['dp'=4,'gx'=2,'gy'=4] {'gy'}, dimensions={0} | all-to-all | bytes 4194304 | tf_op jit(solution)/shard_map/all_to_all | solution.py:144
  1307.8 6.7 convolution_bitcast_fusion.7
  1314.6 28.8 %fusion.20 = f32[4,16,16,1,32]{4,3,2,1,0:T(1,128)S(1)} fusion(f32[4,16,16,32,1]{3,4,2,1,0:T(1,128)S(1)} %bitcast.300, f32[4,16,16,2,32,32]{5,4,3,2,1,0:T(8,128)} %reshape.203), kind=kOutput, calls=%fused_computation.32 | convolution fusion | flops 12582912 | bytes 17039360 | tf_op jit(solution)/shard_map/akjo,akjco->akjc/dot_general | solution.py:89
  1343.4 29.3 %fusion.17 = f32[4,16,16,1,32]{4,3,2,1,0:T(1,128)S(1)} fusion(f32[4,16,16,32,1]{3,4,2,1,0:T(1,128)S(1)} %bitcast.301, f32[4,16,16,2,32,32]{5,4,3,2,1,0:T(8,128)} %reshape.203), kind=kOutput, calls=%fused_computation.29 | convolution fusion | flops 12582912 | bytes 17039360 | tf_op jit(solution)/shard_map/akjo,akjco->akjc/dot_general | solution.py:89
  1372.7 28.8 %fusion.16 = f32[4,16,16,1,32]{4,3,2,1,0:T(1,128)S(1)} fusion(f32[4,16,16,32,1]{3,4,2,1,0:T(1,128)S(1)} %bitcast.303, f32[4,16,16,2,32,32]{5,4,3,2,1,0:T(8,128)} %reshape.203), kind=kOutput, calls=%fused_computation.28 | convolution fusion | flops 12582912 | bytes 17039360 | tf_op jit(solution)/shard_map/akjo,akjco->akjc/dot_general | solution.py:89
  1401.6 26.9 %fusion.21 = f32[4,16,16,1,32]{4,3,2,1,0:T(1,128)S(1)} fusion(f32[4,16,16,32,1]{3,4,2,1,0:T(1,128)S(1)} %bitcast.304, f32[4,16,16,2,32,32]{5,4,3,2,1,0:T(8,128)S(1)} %bitcast.279), kind=kOutput, calls=%fused_computation.33 | convolution fusion | flops 12582912 | bytes 17432576 | tf_op jit(solution)/shard_map/akjo,akjco->akjc/dot_general | solution.py:89
  1451.9 10.7 copy.69
  1462.7 14.7 reshape.235
  1477.4 49.8 %all_to_all.135 = f32[4,1,131072]{2,1,0:T(1,128)} all-to-all(f32[4,1,131072]{2,1,0:T(1,128)S(1)} %reshape.235), channel_id=1, replica_groups=mesh['dp'=4,'gx'=2,'gy'=4] {'gy'}, dimensions={0} | all-to-all | bytes 4194304 | tf_op jit(solution)/shard_map/all_to_all | solution.py:151
  1527.1 7.7 reduce.1
  1534.9 18.3 reshape.236
  1553.2 14.4 copy.71
  1569.6 16.4 fusion.50
  1586.0 16.4 fusion.62
  1602.4 18.8 slice_subtract_fusion
  1621.2 6.6 pad_maximum_fusion.1
  1627.8 17.6 copy.72
  1645.4 9.8 all-to-all-start.7
  1655.3 11.6 multiply_add_fusion
  1666.9 13.7 stack.100
  1680.6 13.7 stack.99
  1694.3 8.4 pad_maximum_fusion.2
  1702.8 18.9 copy.74
  1721.7 133.6 %all-reduce.2.cloned.1.call-done = f32[4,16,16,2,1024]{4,2,1,0,3:T(8,128)} async-done(((f32[4,16,16,2,1024]{4,2,1,0,3:T(8,128)}), f32[4,16,16,2,1024]{4,2,1,0,3:T(8,128)}) %all-reduce.2.cloned.1.call-update) | async-done | bytes 8388624 | tf_op jit(solution)/shard_map/psum | solution.py:198
  1861.3 32.8 %copy.73 = f32[2,64,16,2,1024]{1,2,0,3,4:T(8,128)} copy(f32[2,64,16,2,1024]{4,3,2,1,0:T(2,128)} %bitcast.100) | data formatting | bytes 33554432 | tf_op jit(solution)/shard_map/all_to_all | solution.py:169
  1894.0 56.0 %fusion.11 = bf16[1,32,64,32,128]{4,2,1,3,0:T(8,128)(2,1)S(1)} fusion(f32[64,32,2,32,32]{0,1,2,4,3:T(8,128)} %bitcast.280, f32[32,2,128,1,1]{2,0,1,4,3:T(8,128)S(1)} %fusion.202), kind=kOutput, calls=%fused_computation.17 | convolution fusion | flops 6450839552 | bytes 33587200 | tf_op jit(solution)/shard_map/xkpyc,kpz->cxyz/dot_general | solution.py:133
  1950.0 12.1 copy.75
  (100 shorter events, 92.2 us)
Async XLA Ops:
  7.3 24.3 %copy-start.6 = (f32[128,32,1]{0,1,2:T(8,128)}, f32[128,32,1]{0,1,2:T(8,128)S(1)}, u32[]{:S(2)}) copy-start(f32[128,32,1]{0,1,2:T(8,128)S(1)} %get-tuple-element.32) | copy-start | bytes 49156
  7.3 24.3 %copy-start.8 = (f32[128,32,1]{0,1,2:T(8,128)}, f32[128,32,1]{0,1,2:T(8,128)S(1)}, u32[]{:S(2)}) copy-start(f32[128,32,1]{0,1,2:T(8,128)S(1)} %get-tuple-element.33) | copy-start | bytes 49156
  87.8 193.6 %all-to-all-start = ((f32[64,32,2,1024]{3,0,2,1:T(8,128)}), f32[64,32,2,1024]{3,0,2,1:T(8,128)}, u32[]{:S(2)}, u32[]{:S(2)}) async-start(f32[64,32,2,1024]{3,0,2,1:T(8,128)} %copy.43), calls=%async_computation | async-start | bytes 33554432 | tf_op jit(solution)/shard_map/all_to_all | solution.py:162
  97.9 503.6 %copy-start.14 = (s32[16]{0:T(128)}, s32[16]{0:T(128)S(1)}, u32[]{:S(2)}) copy-start(s32[16]{0:T(128)S(1)} %pad_add_fusion) | copy-start | bytes 196
  309.3 52.6 %all-to-all-start.1 = ((f32[16,16,2,1024]{3,2,1,0:T(2,128)}), f32[16,16,2,1024]{3,2,1,0:T(2,128)S(1)}, u32[]{:S(2)}, u32[]{:S(2)}) async-start(f32[16,16,2,1024]{3,2,1,0:T(2,128)} %copy.46), calls=%async_computation.1 | async-start | bytes 4194304 | tf_op jit(solution)/shard_map/all_to_all | solution.py:144
  361.9 1.3 copy-start.5
  371.0 30.9 %copy-start = (f32[4,16,16,2,32,32]{5,4,3,2,1,0:T(8,128)S(1)}, f32[4,16,16,2,32,32]{5,4,3,2,1,0:T(8,128)}, u32[]{:S(2)}) copy-start(f32[4,16,16,2,32,32]{5,4,3,2,1,0:T(8,128)} %reshape.203) | copy-start | bytes 25165828
  385.1 30.6 %copy-start.1 = (f32[4,16,1,16,32]{4,3,2,1,0:T(8,128)}, f32[4,16,1,16,32]{4,3,2,1,0:T(8,128)S(1)}, u32[]{:S(2)}) copy-start(f32[4,16,1,16,32]{4,3,2,1,0:T(8,128)S(1)} %get-tuple-element.30) | copy-start | bytes 393220
  385.1 44.6 %copy-start.3 = (f32[4,16,1,16,32]{4,3,2,1,0:T(8,128)}, f32[4,16,1,16,32]{4,3,2,1,0:T(8,128)S(1)}, u32[]{:S(2)}) copy-start(f32[4,16,1,16,32]{4,3,2,1,0:T(8,128)S(1)} %get-tuple-element.31) | copy-start | bytes 393220
  660.8 191.0 %all-to-all-start.3 = ((f32[128,16,2,1024]{3,2,1,0:T(2,128)}), f32[128,16,2,1024]{3,2,1,0:T(2,128)}, u32[]{:S(2)}, u32[]{:S(2)}) async-start(f32[128,16,2,1024]{3,2,1,0:T(2,128)} %copy.55), calls=%async_computation.3 | async-start | bytes 33554432 | tf_op jit(solution)/shard_map/all_to_all | solution.py:169
  670.7 0.6 copy-start.10
  670.7 0.6 copy-start.12
  885.0 71.3 %copy-start.7 = (f32[128,32,1]{0,1,2:T(8,128)S(1)}, f32[128,32,1]{0,1,2:T(8,128)}, u32[]{:S(2)}) copy-start(f32[128,32,1]{0,1,2:T(8,128)} %copy-done.6) | copy-start | bytes 49156
  885.0 71.3 %copy-start.9 = (f32[128,32,1]{0,1,2:T(8,128)S(1)}, f32[128,32,1]{0,1,2:T(8,128)}, u32[]{:S(2)}) copy-start(f32[128,32,1]{0,1,2:T(8,128)} %copy-done.8) | copy-start | bytes 49156
  1223.1 1.9 copy-start.15
  1307.7 93.8 %slice-start = ((s8[33554432]{0:T(1024)(128)(4,1)}), s8[4194304]{0:T(1024)(128)(4,1)S(1)}, s32[]{:S(2)}) async-start(s8[33554432]{0:T(1024)(128)(4,1)} %bitcast.278), calls=%async_computation.9 | async-start | bytes 8388608
  1307.7 93.8 %slice-start.1 = ((s8[33554432]{0:T(1024)(128)(4,1)}), s8[4194304]{0:T(1024)(128)(4,1)S(1)}, s32[]{:S(2)}) async-start(s8[33554432]{0:T(1024)(128)(4,1)} %bitcast.278), calls=%async_computation.10 | async-start | bytes 8388608
  1314.6 87.0 %slice-start.2 = ((s8[33554432]{0:T(1024)(128)(4,1)}), s8[4194304]{0:T(1024)(128)(4,1)S(1)}, s32[]{:S(2)}) async-start(s8[33554432]{0:T(1024)(128)(4,1)} %bitcast.278), calls=%async_computation.11 | async-start | bytes 8388608
  1314.6 87.0 %slice-start.3 = ((s8[33554432]{0:T(1024)(128)(4,1)}), s8[4194304]{0:T(1024)(128)(4,1)S(1)}, s32[]{:S(2)}) async-start(s8[33554432]{0:T(1024)(128)(4,1)} %bitcast.278), calls=%async_computation.12 | async-start | bytes 8388608
  1343.4 58.2 %slice-start.4 = ((s8[33554432]{0:T(1024)(128)(4,1)}), s8[4194304]{0:T(1024)(128)(4,1)S(1)}, s32[]{:S(2)}) async-start(s8[33554432]{0:T(1024)(128)(4,1)} %bitcast.278), calls=%async_computation.13 | async-start | bytes 8388608
  1343.4 58.2 %slice-start.5 = ((s8[33554432]{0:T(1024)(128)(4,1)}), s8[4194304]{0:T(1024)(128)(4,1)S(1)}, s32[]{:S(2)}) async-start(s8[33554432]{0:T(1024)(128)(4,1)} %bitcast.278), calls=%async_computation.14 | async-start | bytes 8388608
  1372.7 28.9 %slice-start.6 = ((s8[33554432]{0:T(1024)(128)(4,1)}), s8[4194304]{0:T(1024)(128)(4,1)S(1)}, s32[]{:S(2)}) async-start(s8[33554432]{0:T(1024)(128)(4,1)} %bitcast.278), calls=%async_computation.15 | async-start | bytes 8388608
  1372.7 28.9 %slice-start.7 = ((s8[33554432]{0:T(1024)(128)(4,1)}), s8[4194304]{0:T(1024)(128)(4,1)S(1)}, s32[]{:S(2)}) async-start(s8[33554432]{0:T(1024)(128)(4,1)} %bitcast.278), calls=%async_computation.16 | async-start | bytes 8388608
  1645.4 9.9 copy-start.2
  1645.4 9.9 copy-start.4
  1645.4 215.9 %all-to-all-start.7 = ((f32[128,16,2,1024]{3,2,1,0:T(2,128)}), f32[128,16,2,1024]{3,2,1,0:T(2,128)}, u32[]{:S(2)}, u32[]{:S(2)}) async-start(f32[128,16,2,1024]{3,2,1,0:T(2,128)} %copy.72), calls=%async_computation.7 | async-start | bytes 33554432 | tf_op jit(solution)/shard_map/all_to_all | solution.py:169
  1655.3 200.0 %all-reduce.2.cloned.1.call-start = ((), (), s32[]{:S(2)}) async-start(), calls=%async_computation.8 | async-start | bytes 16777216 | tf_op jit(solution)/shard_map/psum | solution.py:198
  1694.3 8.5 copy-start.11
  1694.3 8.5 copy-start.13
Sparse Core Ops, SparseCore 0:
  1702.9 152.3 all-reduce.1
where the time goes:
time: 1980 us; the launch traced here: 1970 us
  waiting for transfers between devices  522 us (26%)
  matrix products  490 us (25%)
  local copies, waits for them, and re-layouts  478 us (24%)
  blocking collectives  337 us (17%)
  other arithmetic  92.3 us (5%)
  starting transfers between devices  34.9 us (2%)
    all_to_all x1, blocking collectives, pencil_analyze(): lax.all_to_all(spectrum, 'gx', split_axis=1, concat_axis=0, tiled=True)  186 us
    all_to_all x1, waiting for transfers between devices, pencil_analyze(): lax.all_to_all(spectrum, 'gx', split_axis=1, concat_axis=0, tiled=True)  184 us
    all_to_all x2, waiting for transfers between devices, pencil_synthesize(): lax.all_to_all(widened, 'gx', split_axis=0, concat_axis=1, tiled=True)  180 us
    psum x1, waiting for transfers between devices, shards(): summed_all = lax.psum(grad_terms, 'dp')  134 us
    dot_general x2, matrix products, depth_synthesize(): return jnp.einsum('xkpyc,kpz->cxyz', widened, table_in, precision=PRECISE)  127 us
    dot_general x4, matrix products, channel_adjoint(): return jnp.einsum('akjo,akjco->akjc', left_op, right_op, precision=PRECISE)  114 us
    unnamed x55, local copies, waits for them, and re-layouts  102 us
    all_to_all x2, blocking collectives, from_modes(): lax.all_to_all(widened, 'gy', split_axis=3, concat_axis=0, tiled=True)  101 us
  transfers between devices with their start and end apart: 5, of which 4 were waited for; matrix products, arithmetic and copies ran while one was open for 5% of the time, Pallas kernels for 0%

commit v1 on v0

v1 whole, which is shorter than its diff:
```python
import functools
import math

import jax
import jax.numpy as jnp
import ml_dtypes
import numpy as np
from jax import lax
from jax.experimental import pallas as pl
from jax.experimental.pallas import tpu as pltpu
from jax.sharding import PartitionSpec as P

CHANNELS = 32
NX = 128
NY = 128
NZ = 128
MX = 16
MY = 16
MZ = 32
SAMPLES = 4
PAIR = 2
VMEM_BYTES = 56 * 1024 * 1024

NT = (((1,), (1,)), ((), ()))
NN = (((1,), (0,)), ((), ()))


def f32_dot(left_op, right_op, dims=NN):
    return lax.dot_general(left_op, right_op, dims, preferred_element_type=jnp.float32)


def mode_list(length, count):
    half_ids = np.arange(count // 2)
    return np.concatenate([half_ids, length - count // 2 + half_ids])


def split_pair(table):
    high = table.astype(np.float32).astype(ml_dtypes.bfloat16)
    low = (table - high.astype(np.float64)).astype(np.float32).astype(ml_dtypes.bfloat16)
    return high, low


def depth_scales():
    return np.where(np.arange(MZ) == 0, 1.0, 2.0) / float(NX * NY * NZ)


def plane_angles(x_cells, y_cells, blocks):
    kx = mode_list(NX, MX)
    ky = mode_list(NY, MY)
    turns_x = (kx[:, None] * x_cells[None, :] % NX) / NX
    turns_y = (ky[:, None] * y_cells[None, :] % NY) / NY
    turns = turns_x[:, None, :, None] + turns_y[None, :, None, :]
    turns = turns.reshape(blocks, MX // blocks * MY, x_cells.size * y_cells.size)
    return 2.0 * math.pi * turns


def plane_table(x_len, y_len, blocks):
    angles = plane_angles(np.arange(x_len), np.arange(y_len), blocks)
    table = np.stack([np.cos(angles), -np.sin(angles)], axis=1)
    return split_pair(table.reshape(2 * MX * MY, x_len * y_len))


def shift_tables(x_len, y_len, x_parts, y_parts):
    angles = plane_angles(np.arange(x_parts) * x_len, np.arange(y_parts) * y_len, y_parts)
    angles = np.moveaxis(angles, 2, 0)
    cosine = np.stack([np.cos(angles), np.cos(angles)], axis=2)
    signed = np.stack([np.sin(angles), -np.sin(angles)], axis=2)
    shape = (x_parts * y_parts, 1, 2 * MX * MY)
    return cosine.reshape(shape).astype(np.float32), signed.reshape(shape).astype(np.float32)


def depth_angles():
    turns = (np.arange(MZ)[:, None] * np.arange(NZ)[None, :] % NZ) / NZ
    return 2.0 * math.pi * turns


def analysis_table(scale_vec):
    angles = depth_angles()
    table = np.concatenate([np.cos(angles), np.sin(angles)]) * np.tile(scale_vec, 2)[:, None]
    table = table.astype(np.float32).astype(ml_dtypes.bfloat16)
    return np.concatenate([table, table], axis=1)


def synthesis_table(scale_vec):
    angles = depth_angles()
    table = np.concatenate([np.cos(angles), np.sin(angles)]) * np.tile(scale_vec, 2)[:, None]
    high, low = split_pair(table.T)
    return np.concatenate([high, high, low], axis=1)


def spread_input():
    one = np.repeat(np.eye(CHANNELS), CHANNELS, axis=1)
    return np.concatenate([one, one]).astype(ml_dtypes.bfloat16)


def spread_output():
    one = np.tile(np.eye(CHANNELS), (1, CHANNELS))
    return np.concatenate([one, one]).astype(ml_dtypes.bfloat16)


def halves(value):
    high = value.astype(jnp.bfloat16)
    low = (value - high.astype(jnp.float32)).astype(jnp.bfloat16)
    return high, low


def swap_parts(value):
    width = value.shape[1]
    blocks = [
        pltpu.roll(value[:, at : at + 128], 64, 1) for at in range(0, width, 128)
    ]
    return jnp.concatenate(blocks, axis=1)


def part_signs(width):
    lane_ids = lax.broadcasted_iota(jnp.int32, (1, width), 1)
    return jnp.where(lane_ids % 128 < 64, 1.0, -1.0).astype(jnp.float32)


def analyze_pair(grids, high_ref, low_ref, depth_ref, cos_ref, sin_ref, out_ref, x_parts, y_parts):
    plane = f32_dot(high_ref[...], grids) + f32_dot(low_ref[...], grids)
    signs = part_signs(plane.shape[0])
    mode_len = MZ // x_parts
    for chan in range(PAIR):
        high, low = halves(plane[:, chan * NZ : (chan + 1) * NZ])
        both = f32_dot(depth_ref[...], jnp.concatenate([high, low], axis=1), NT)
        spectrum = both[:MZ] + signs * swap_parts(both[MZ:])
        spectrum = spectrum * cos_ref[...] + swap_parts(spectrum) * sin_ref[...]
        for gx in range(x_parts):
            for gy in range(y_parts):
                out_ref[gx * y_parts + gy, chan] = spectrum[
                    gx * mode_len : (gx + 1) * mode_len, gy * 128 : (gy + 1) * 128
                ].astype(jnp.bfloat16)


def depth_fields(spec_ref, depth_ref, cos_ref, sin_ref, x_parts, y_parts):
    fields = []
    for chan in range(PAIR):
        rows = [
            jnp.concatenate(
                [spec_ref[gx * y_parts + gy, chan].astype(jnp.float32) for gy in range(y_parts)],
                axis=1,
            )
            for gx in range(x_parts)
        ]
        spectrum = jnp.concatenate(rows, axis=0)
        spectrum = spectrum * cos_ref[...] - swap_parts(spectrum) * sin_ref[...]
        turned = -part_signs(spectrum.shape[1]) * swap_parts(spectrum)
        high, low = halves(jnp.concatenate([spectrum, turned], axis=0))
        fields.append(
            f32_dot(depth_ref[...], jnp.concatenate([high, low, high], axis=0)).astype(jnp.bfloat16)
        )
    return jnp.concatenate(fields, axis=0)


def gelu_parts(pre_act):
    size = jnp.abs(pre_act)
    bell = jnp.exp(pre_act * pre_act * -0.5)
    turn = pl.reciprocal(1.0 + (0.3275911 * 0.7071067811865476) * size, approx=False)
    poly = 0.5 * 1.061405429 * turn - 0.5 * 1.453152027
    poly = poly * turn + 0.5 * 1.421413741
    poly = poly * turn - 0.5 * 0.284496736
    poly = poly * turn + 0.5 * 0.254829592
    tail = poly * turn * bell
    value = jnp.maximum(pre_act, 0.0) - size * tail
    normal_cdf = jnp.where(pre_act > 0.0, 1.0 - tail, tail)
    return value, normal_cdf + pre_act * bell * 0.3989422804014327


def analyze_kernel(x_parts, y_parts, grid_ref, high_ref, low_ref, depth_ref, cos_ref, sin_ref, out_ref):
    cells = grid_ref.shape[1] * grid_ref.shape[2]
    grids = jnp.concatenate(
        [grid_ref[chan].reshape(cells, NZ) for chan in range(PAIR)], axis=1
    )
    analyze_pair(
        grids, high_ref, low_ref, depth_ref, cos_ref, sin_ref, out_ref, x_parts, y_parts
    )


def turn_kernel(
    x_parts,
    y_parts,
    spec_ref,
    cot_ref,
    back_high_ref,
    back_low_ref,
    back_depth_ref,
    high_ref,
    low_ref,
    depth_ref,
    cos_ref,
    sin_ref,
    value_ref,
    out_ref,
    grad_ref,
):
    fields = depth_fields(spec_ref, back_depth_ref, cos_ref, sin_ref, x_parts, y_parts)
    x_len, y_len = cot_ref.shape[1], cot_ref.shape[2]
    step = min(8, x_len)
    for x_at in range(0, x_len, step):
        rows = slice(x_at * y_len, (x_at + step) * y_len)
        pre_act = f32_dot(back_high_ref[rows], fields, NT) + f32_dot(back_low_ref[rows], fields, NT)
        for chan in range(PAIR):
            lanes = slice(chan * NZ, (chan + 1) * NZ)
            value, slope = gelu_parts(pre_act[:, lanes])
            value_ref[chan, x_at : x_at + step] = value.astype(jnp.bfloat16).reshape(step, y_len, NZ)
            cotangent = cot_ref[chan, x_at : x_at + step].reshape(step * y_len, NZ)
            grad_ref[rows, lanes] = (cotangent.astype(jnp.float32) * slope).astype(jnp.bfloat16)
    analyze_pair(
        grad_ref[...], high_ref, low_ref, depth_ref, cos_ref, sin_ref, out_ref, x_parts, y_parts
    )


def synthesize_kernel(
    x_parts, y_parts, spec_ref, high_ref, low_ref, depth_ref, cos_ref, sin_ref, out_ref
):
    fields = depth_fields(spec_ref, depth_ref, cos_ref, sin_ref, x_parts, y_parts)
    x_len, y_len = out_ref.shape[1], out_ref.shape[2]
    step = min(8, x_len)
    for x_at in range(0, x_len, step):
        rows = slice(x_at * y_len, (x_at + step) * y_len)
        grid = f32_dot(high_ref[rows], fields, NT) + f32_dot(low_ref[rows], fields, NT)
        for chan in range(PAIR):
            out_ref[chan, x_at : x_at + step] = (
                grid[:, chan * NZ : (chan + 1) * NZ].astype(jnp.bfloat16).reshape(step, y_len, NZ)
            )


def mode_rows(value, spread_ref):
    high = value.astype(jnp.bfloat16).astype(jnp.float32)
    both = jnp.concatenate([high, value - high], axis=0)
    return f32_dot(both.T.astype(jnp.bfloat16), spread_ref[...])


def mix_kernel(
    adjoint, mode_len, step_len, recv_ref, weight_ref, spread_ref, gather_ref, spec_ref, out_ref,
    taken_ref, mixed_ref
):
    step_at = pl.program_id(0)

    @pl.when(step_at == 0)
    def _():
        total = recv_ref[0].astype(jnp.float32)
        for source in range(1, recv_ref.shape[0]):
            total = total + recv_ref[source].astype(jnp.float32)
        spec_ref[...] = total
        taken_ref[...] = total.reshape(taken_ref.shape)

    half = 64
    for at in range(step_len):
        mode_at = step_at * step_len + at
        here = pl.ds(mode_at, CHANNELS, stride=mode_len) if mode_len > 1 else slice(None)
        spread = mode_rows(taken_ref[here, :], spread_ref)
        real_in, imag_in = spread[:half], spread[half:]
        w_real = weight_ref[:, at, :, 0, :].reshape(half, CHANNELS * CHANNELS)
        w_imag = weight_ref[:, at, :, 1, :].reshape(half, CHANNELS * CHANNELS)
        if adjoint:
            real_part = real_in * w_real + imag_in * w_imag
            imag_part = imag_in * w_real - real_in * w_imag
            terms = jnp.concatenate([real_part, imag_part], axis=0)
        else:
            real_part = real_in * w_real - imag_in * w_imag
            imag_part = imag_in * w_real + real_in * w_imag
            terms = jnp.concatenate([real_part, imag_part], axis=0)
            width = terms.shape[1]
            while width > 128:
                width //= 2
                terms = terms[:, :width] + terms[:, width:]
        high, low = halves(terms)
        mixed = f32_dot(jnp.concatenate([high, low], axis=1), gather_ref[...])
        mixed_ref[here, :] = mixed.T[:CHANNELS]

    @pl.when(step_at == pl.num_programs(0) - 1)
    def _():
        out_ref[...] = mixed_ref[...].reshape(out_ref.shape).astype(jnp.bfloat16)


def weight_kernel(
    mode_len, step_len, u_ref, g_ref, pick_ref, spread_u_ref, spread_g_ref, out_ref
):
    step_at = pl.program_id(0)
    kx_len, row_len = out_ref.shape[0], out_ref.shape[2]
    half = kx_len * row_len

    def spread_rows(ref, here, spread_ref):
        value = ref[here, :]
        picked = []
        for sample in range(SAMPLES):
            high, low = halves(value[sample * CHANNELS : (sample + 1) * CHANNELS])
            both = jnp.concatenate([high, low], axis=1)
            picked.append(f32_dot(pick_ref[...], both, NT))
        high, low = halves(jnp.concatenate(picked, axis=0))
        return f32_dot(jnp.concatenate([high, low], axis=1), spread_ref[...])

    for at in range(step_len):
        mode_at = step_at * step_len + at
        rows = SAMPLES * CHANNELS
        here = pl.ds(mode_at, rows, stride=mode_len) if mode_len > 1 else slice(None)
        spread_u = spread_rows(u_ref, here, spread_u_ref)
        spread_g = spread_rows(g_ref, here, spread_g_ref)
        real_part, imag_part = 0.0, 0.0
        for sample in range(SAMPLES):
            top = sample * 2 * half
            u_real, u_imag = spread_u[top : top + half], spread_u[top + half : top + 2 * half]
            g_real, g_imag = spread_g[top : top + half], spread_g[top + half : top + 2 * half]
            real_part = real_part + (u_real * g_real + u_imag * g_imag)
            imag_part = imag_part + (u_real * g_imag - u_imag * g_real)
        for kx in range(kx_len):
            out_ref[kx, at, :, 0, :] = real_part[kx * row_len : (kx + 1) * row_len]
            out_ref[kx, at, :, 1, :] = imag_part[kx * row_len : (kx + 1) * row_len]


def whole_spec(array):
    zeros = (0,) * array.ndim
    return pl.BlockSpec(array.shape, lambda *at: zeros)


def params():
    return pltpu.CompilerParams(vmem_limit_bytes=VMEM_BYTES)


def cost(flops, bytes_accessed):
    return pl.CostEstimate(
        flops=int(flops), bytes_accessed=int(bytes_accessed), transcendentals=0
    )


def shards(x_parts, y_parts, field, cotangent, spectral_weight):
    chan_len, x_len, y_len = field.shape[1:4]
    kx_len, mode_len, row_len = spectral_weight.shape[:3]
    parts = x_parts * y_parts
    dp_len = lax.axis_size("dp")
    share_len = row_len // dp_len
    step_len = min(4, mode_len)

    high, low = plane_table(x_len, y_len, y_parts)
    back_high, back_low = high.T.copy(), low.T.copy()
    forward_plain = analysis_table(np.ones(MZ))
    forward_scaled = analysis_table(depth_scales())
    back_scaled = synthesis_table(depth_scales())
    back_plain = synthesis_table(np.ones(MZ))
    cosines, sines = shift_tables(x_len, y_len, x_parts, y_parts)
    place = lax.axis_index("gx") * y_parts + lax.axis_index("gy")
    shift_cos = lax.dynamic_index_in_dim(jnp.asarray(cosines), place, 0, False)
    shift_sin = lax.dynamic_index_in_dim(jnp.asarray(sines), place, 0, False)
    high, low, back_high, back_low = map(jnp.asarray, (high, low, back_high, back_low))

    pair_grid = pl.BlockSpec((PAIR, x_len, y_len, NZ), lambda at: (at, 0, 0, 0))
    pair_spec = pl.BlockSpec((parts, PAIR, mode_len, 128), lambda at: (0, at, 0, 0))
    grid_shape = jax.ShapeDtypeStruct((chan_len, x_len, y_len, NZ), jnp.bfloat16)
    spec_shape = jax.ShapeDtypeStruct((parts, chan_len, mode_len, 128), jnp.bfloat16)
    grid_bytes = chan_len * x_len * y_len * NZ * 2
    plane_flops = 2 * 2 * MX * MY * x_len * y_len * NZ * chan_len * 2

    def call(body, name, operands, specs, out_shapes, out_specs, scratch, flops, moved):
        return pl.pallas_call(
            functools.partial(body, x_parts, y_parts),
            name=name,
            grid=(chan_len // PAIR,),
            in_specs=specs,
            out_specs=out_specs,
            out_shape=out_shapes,
            scratch_shapes=scratch,
            compiler_params=params(),
            cost_estimate=cost(flops, moved),
        )(*operands)

    def tables_of(*arrays):
        return [whole_spec(array) for array in arrays]

    def mix(name, received, spread, gather, adjoint):
        small = (chan_len * mode_len, 128)
        return pl.pallas_call(
            functools.partial(mix_kernel, adjoint, mode_len, step_len),
            name=name,
            grid=(mode_len // step_len,),
            in_specs=[
                whole_spec(received),
                pl.BlockSpec(
                    (kx_len, step_len, row_len, 2, chan_len * chan_len),
                    lambda at: (0, at, 0, 0, 0),
                ),
                whole_spec(spread),
                whole_spec(gather),
            ],
            out_specs=[
                pl.BlockSpec((chan_len, mode_len, 128), lambda at: (0, 0, 0)),
                pl.BlockSpec((chan_len, mode_len, 128), lambda at: (0, 0, 0)),
            ],
            out_shape=[
                jax.ShapeDtypeStruct((chan_len, mode_len, 128), jnp.float32),
                jax.ShapeDtypeStruct((chan_len, mode_len, 128), jnp.bfloat16),
            ],
            scratch_shapes=[pltpu.VMEM(small, jnp.float32), pltpu.VMEM(small, jnp.float32)],
            compiler_params=params(),
            cost_estimate=cost(mode_len * 2e8, spectral_weight.size * 4),
        )(received, spectral_weight, spread, gather)

    def exchange(partial_sums):
        return lax.all_to_all(partial_sums, ("gx", "gy"), 0, 0, tiled=True)

    def collect(spectrum):
        return lax.all_gather(spectrum, ("gx", "gy"), axis=0, tiled=False)

    spread_in, spread_out = jnp.asarray(spread_input()), jnp.asarray(spread_output())
    onto_out = np.zeros((128, 128))
    onto_out[np.arange(128), np.arange(128) % CHANNELS] = 1.0
    onto_out = jnp.asarray(np.concatenate([onto_out, onto_out]).astype(ml_dtypes.bfloat16))
    onto_in = np.zeros((chan_len * chan_len, 128))
    onto_in[np.arange(chan_len * chan_len), np.arange(chan_len * chan_len) // CHANNELS] = 1.0
    onto_in = jnp.asarray(np.concatenate([onto_in, onto_in]).astype(ml_dtypes.bfloat16))

    partial_u = call(
        analyze_kernel,
        "analyze_field",
        (field[0], high, low, jnp.asarray(forward_plain), shift_cos, shift_sin),
        [pair_grid] + tables_of(high, low, forward_plain, shift_cos, shift_sin),
        spec_shape,
        pair_spec,
        [],
        plane_flops,
        grid_bytes,
    )
    spec_u, spec_v = mix("mix_forward", exchange(partial_u), spread_in, onto_out, False)
    gathered_u = lax.all_gather(spec_u, "dp", axis=0, tiled=False)
    out_grid, partial_g = call(
        turn_kernel,
        "activate",
        (
            collect(spec_v),
            cotangent[0],
            back_high,
            back_low,
            jnp.asarray(back_scaled),
            high,
            low,
            jnp.asarray(forward_scaled),
            shift_cos,
            shift_sin,
        ),
        [pair_spec, pair_grid]
        + tables_of(
            back_high, back_low, back_scaled, high, low, forward_scaled, shift_cos, shift_sin
        ),
        [grid_shape, spec_shape],
        [pair_grid, pair_spec],
        [pltpu.VMEM((x_len * y_len, PAIR * NZ), jnp.bfloat16)],
        3 * plane_flops,
        2 * grid_bytes,
    )
    spec_g, spec_du = mix("mix_adjoint", exchange(partial_g), spread_out, onto_in, True)
    gathered_g = lax.all_gather(spec_g, "dp", axis=0, tiled=False)
    grad_grid = call(
        synthesize_kernel,
        "synthesize_grad",
        (collect(spec_du), back_high, back_low, jnp.asarray(back_plain), shift_cos, shift_sin),
        [pair_spec] + tables_of(back_high, back_low, back_plain, shift_cos, shift_sin),
        grid_shape,
        pair_grid,
        [],
        plane_flops,
        grid_bytes,
    )

    lane_ids = np.arange(128)
    picks = np.zeros((dp_len, 2 * kx_len * share_len, 128))
    for rank in range(dp_len):
        rows = np.arange(2 * kx_len * share_len)
        lanes = rows // share_len * row_len + rank * share_len + rows % share_len
        picks[rank] = lanes[:, None] == lane_ids[None, :]
    picks = jnp.asarray(np.concatenate([picks, picks], axis=2).astype(ml_dtypes.bfloat16))
    pick = lax.dynamic_index_in_dim(picks, lax.axis_index("dp"), 0, False)
    flat = (dp_len * chan_len * mode_len, 128)
    all_u, all_g = gathered_u.reshape(flat), gathered_g.reshape(flat)
    weight_grad = pl.pallas_call(
        functools.partial(weight_kernel, mode_len, step_len),
        name="weight_terms",
        grid=(mode_len // step_len,),
        in_specs=[whole_spec(part) for part in (all_u, all_g, pick, spread_in, spread_out)],
        out_specs=pl.BlockSpec(
            (kx_len, step_len, share_len, 2, chan_len * chan_len), lambda at: (0, at, 0, 0, 0)
        ),
        out_shape=jax.ShapeDtypeStruct(
            (kx_len, mode_len, share_len, 2, chan_len * chan_len), jnp.float32
        ),
        compiler_params=params(),
        cost_estimate=cost(mode_len * 2e8, mode_len * 2e6),
    )(all_u, all_g, pick, spread_in, spread_out)
    return (out_grid[None], grad_grid[None], weight_grad)


def solution(mesh):
    placed = (
        P("dp", None, "gx", "gy", None),
        P("dp", None, "gx", "gy", None),
        P("gy", "gx", None, None, None),
    )
    return jax.shard_map(
        functools.partial(shards, mesh.shape["gx"], mesh.shape["gy"]),
        mesh=mesh,
        in_specs=placed,
        out_specs=(
            P("dp", None, "gx", "gy", None),
            P("dp", None, "gx", "gy", None),
            P("gy", "gx", "dp", None, None),
        ),
        check_vma=False,
    )
```

time: 1980 us -> 339 us (0.17)
  matrix products: 490 us -> 0 us
  local copies, waits for them, and re-layouts: 478 us -> 3.58 us
  waiting for transfers between devices: 522 us -> 106 us
  blocking collectives: 337 us -> 34.1 us
  Pallas kernels: 0 us -> 175 us
  other arithmetic: 92.3 us -> 0 us
  starting transfers between devices: 34.9 us -> 3.73 us
    dot_general x28 -> x0, matrix products: 490 us -> none  [the longest x2 127 us: depth_synthesize(): return jnp.einsum('xkpyc,kpz->cxyz', widened, table_in, precision=PRECISE)]
    all_to_all x4 -> x1, waiting for transfers between devices: 388 us -> 25.2 us  [exchange(): return lax.all_to_all(partial_sums, ('gx', 'gy'), 0, 0, tiled=True)]
    all_to_all x4 -> x1, blocking collectives: 337 us -> 34.1 us  [exchange(): return lax.all_to_all(partial_sums, ('gx', 'gy'), 0, 0, tiled=True)]
    pallas_call x0 -> x6, Pallas kernels: none -> 175 us  [the longest x3 145 us: call(): pl.pallas_call(functools.partial(body, x_parts, y_parts), name=name, grid...]
    psum x1 -> x0, waiting for transfers between devices: 134 us -> none  [shards(): summed_all = lax.psum(grad_terms, 'dp')]
    all_to_all x11 -> x0, local copies, waits for them, and re-layouts: 112 us -> none  [the longest x2 65.9 us: pencil_synthesize(): lax.all_to_all(widened, 'gx', split_axis=0, concat_axis=1, tiled=True)]
    another operation x12 -> x0, local copies, waits for them, and re-layouts: 105 us -> none  [the longest x6 37.9 us: synthesis_rows(): return jnp.stack([real_part, imag_part], axis=2)]
    unnamed x55 -> x2, local copies, waits for them, and re-layouts: 102 us -> 0.97 us
  transfers between devices with their start and end apart: 5 -> 5, of which waited for: 4 -> 4; matrix products, arithmetic and copies ran while one was open for 5% -> 0% of each run, Pallas kernels for 0% -> 6%
where the time goes in v1:
time: 339 us
  Pallas kernels  175 us (52%)
  waiting for transfers between devices  106 us (31%)
  blocking collectives  34.1 us (10%)
  between operations  15.7 us (5%)
  starting transfers between devices  3.73 us (1%)
  local copies, waits for them, and re-layouts  3.58 us (1%)
    pallas_call x3, Pallas kernels, call(): pl.pallas_call(functools.partial(body, x_parts, y_parts), name=name, grid...  145 us
    all_gather x2, waiting for transfers between devices, collect(): return lax.all_gather(spectrum, ('gx', 'gy'), axis=0, tiled=False)  67.8 us
    all_to_all x1, blocking collectives, exchange(): return lax.all_to_all(partial_sums, ('gx', 'gy'), 0, 0, tiled=True)  34.1 us
    all_to_all x1, waiting for transfers between devices, exchange(): return lax.all_to_all(partial_sums, ('gx', 'gy'), 0, 0, tiled=True)  25.2 us
    pallas_call x2, Pallas kernels, mix(): pl.pallas_call(functools.partial(mix_kernel, adjoint, mode_len, step_len)...  18 us
    pallas_call x1, Pallas kernels, shards(): pl.pallas_call(functools.partial(weight_kernel, mode_len, step_len), name...  12.2 us
    all_gather x1, waiting for transfers between devices, shards(): gathered_g = lax.all_gather(spec_g, 'dp', axis=0, tiled=False)  12 us
  transfers between devices with their start and end apart: 5, of which 4 were waited for; matrix products, arithmetic and copies ran while one was open for 0% of the time, Pallas kernels for 6%

profile of v1, /device:TPU:0, one launch (start us, length us, event | category | flops | bytes accessed | tf_op | source)
XLA Modules:
  0.0 338.7 jit_solution(9272158755871504420)
XLA Ops:
  8.0 0.0 all-gather.9.cloned.1.call-start
  8.0 1.3 dynamic-slice_bitcast_fusion.1
  9.3 32.5 %analyze_field.1 = bf16[8,32,16,128]{3,2,1,0:T(8,128)(2,1)} custom-call(bf16[32,64,32,128]{3,2,1,0:T(8,128)(2,1)} %bitcast.14, bf16[512,2048]{1,0:T(8,128)(2,1)} %constant.58.clone.high_ref, bf16[512,2048]{1,0:T(8,128)(2,1)} %constant.59.clone.low_ref, bf16[64,256]{1,0:T(8,128)(2,1)} %constant.66.clone.depth_ref, f32[1,512]{1,0:T(1,128)} %get-tuple-element.16.cos_ref, ...), custom_call_target="tpu_custom_call" | custom-call | flops 17179869184 | bytes 16777216 | tf_op jit(solution)/shard_map/analyze_field/pallas_call | solution.py:356
  41.8 34.1 %all_to_all.10.recv_ref = bf16[8,32,16,128]{3,2,1,0:T(8,128)(2,1)} all-to-all(bf16[8,32,16,128]{3,2,1,0:T(8,128)(2,1)} %analyze_field.1), channel_id=1, replica_groups=mesh['dp'=4,'gx'=2,'gy'=4] {'gx','gy'}, dimensions={0} | all-to-all | bytes 2097152 | tf_op jit(solution)/shard_map/all_to_all | solution.py:400
  75.9 8.2 %mix_forward.1 = (f32[32,16,128]{2,1,0:T(8,128)}, bf16[32,16,128]{2,1,0:T(8,128)(2,1)}) custom-call(bf16[8,32,16,128]{3,2,1,0:T(8,128)(2,1)} %all_to_all.10.recv_ref, f32[4,16,16,2,1024]{4,3,2,1,0:T(2,128)} %weight_ref.3, bf16[64,1024]{1,0:T(8,128)(2,1)} %constant.62.clone.spread_ref.spread_u_ref, bf16[256,128]{1,0:T(8,128)(2,1)} %constant.64.clone.gather_ref), custom_call_target="tpu_custom_call" | custom-call | flops 3200000000 | bytes 8388608 | tf_op jit(solution)/shard_map/mix_forward/pallas_call | solution.py:373
  84.1 0.0 all-gather.9.cloned.1.call-update
  84.1 37.6 %all-gather.9.cloned.1.call-done = bf16[256,16,128]{2,1,0:T(8,128)(2,1)} async-done(((bf16[32,16,128]{2,1,0:T(8,128)(2,1)}), bf16[256,16,128]{2,1,0:T(8,128)(2,1)}) %all-gather.9.cloned.1.call-update) | async-done | bytes 1048592 | tf_op jit(solution)/shard_map/all_gather | solution.py:403
  121.7 83.5 %activate.1 = (bf16[32,64,32,128]{3,2,1,0:T(8,128)(2,1)}, bf16[8,32,16,128]{3,2,1,0:T(8,128)(2,1)}) custom-call(bf16[8,32,16,128]{3,2,1,0:T(8,128)(2,1)} %bitcast.19, bf16[32,64,32,128]{3,2,1,0:T(8,128)(2,1)} %bitcast.15, bf16[2048,512]{1,0:T(8,128)(2,1)} %constant.60.clone.back_high_ref.high_ref, bf16[2048,512]{1,0:T(8,128)(2,1)} %constant.61.clone.back_low_ref.low_ref, ...), custom_call_target="tpu_custom_call" | custom-call | flops 51539607552 | bytes 33554432 | tf_op jit(solution)/shard_map/activate/pallas_call | solution.py:356
  205.2 3.6 %all-to-all-start.1 = ((bf16[8,32,16,128]{3,2,1,0:T(8,128)(2,1)}), bf16[8,32,16,128]{3,2,1,0:T(8,128)(2,1)S(1)}, u32[]{:S(2)}, u32[]{:S(2)}) async-start(bf16[8,32,16,128]{3,2,1,0:T(8,128)(2,1)} %get-tuple-element.11), calls=%async_computation.1 | async-start | bytes 2097152 | tf_op jit(solution)/shard_map/all_to_all | solution.py:400
  208.8 0.0 all-gather.13.cloned.1.call-start
  208.8 0.5 all-gather.13.cloned.1.call-update
  209.3 0.0 all-gather.15.cloned.1.call-start
  209.4 25.2 %all-to-all-done.1.recv_ref = bf16[8,32,16,128]{3,2,1,0:T(8,128)(2,1)S(1)} async-done(((bf16[8,32,16,128]{3,2,1,0:T(8,128)(2,1)}), bf16[8,32,16,128]{3,2,1,0:T(8,128)(2,1)S(1)}, u32[]{:S(2)}, u32[]{:S(2)}) %all-to-all-start.1) | async-done | bytes 1048608 | tf_op jit(solution)/shard_map/all_to_all | solution.py:400
  234.6 0.0 copy-start
  234.6 1.0 copy-done
  235.6 9.7 %mix_adjoint.1 = (f32[32,16,128]{2,1,0:T(8,128)}, bf16[32,16,128]{2,1,0:T(8,128)(2,1)}) custom-call(bf16[8,32,16,128]{3,2,1,0:T(8,128)(2,1)} %copy-done, f32[4,16,16,2,1024]{4,3,2,1,0:T(2,128)} %weight_ref.3, bf16[64,1024]{1,0:T(8,128)(2,1)} %constant.63.clone.spread_ref.spread_g_ref, bf16[2048,128]{1,0:T(8,128)(2,1)} %constant.65.clone.gather_ref), custom_call_target="tpu_custom_call" | custom-call | flops 3200000000 | bytes 8388608 | tf_op jit(solution)/shard_map/mix_adjoint/pallas_call | solution.py:373
  245.3 0.0 all-gather.15.cloned.1.call-update
  245.3 0.0 all-gather.11.cloned.1.call-start
  245.4 0.5 all-gather.11.cloned.1.call-update
  245.9 1.3 dynamic-slice_bitcast_fusion.pick_ref
  247.3 0.0 all-gather.13.cloned.1.call-done
  247.3 12.0 %all-gather.15.cloned.1.call-done = f32[128,16,128]{2,1,0:T(8,128)} async-done(((f32[32,16,128]{2,1,0:T(8,128)}), f32[128,16,128]{2,1,0:T(8,128)}) %all-gather.15.cloned.1.call-update) | async-done | bytes 1048592 | tf_op jit(solution)/shard_map/all_gather | solution.py:452
  259.3 12.2 %weight_terms.1 = f32[4,16,4,2,1024]{4,3,2,1,0:T(2,128)} custom-call(f32[2048,128]{1,0:T(8,128)} %bitcast.16, f32[2048,128]{1,0:T(8,128)} %bitcast.18, bf16[32,256]{1,0:T(8,128)(2,1)} %dynamic-slice_bitcast_fusion.pick_ref, bf16[64,1024]{1,0:T(8,128)(2,1)} %constant.62.clone.spread_ref.spread_u_ref, bf16[64,1024]{1,0:T(8,128)(2,1)} %constant.63.clone.spread_ref.spread_g_ref), custom_call_target="tpu_custom_call" | custom-call | flops 3200000000 | bytes 32000000 | tf_op jit(solution)/shard_map/weight_terms/pallas_call | solution.py:475
  271.5 30.2 %all-gather.11.cloned.1.call-done = bf16[256,16,128]{2,1,0:T(8,128)(2,1)} async-done(((bf16[32,16,128]{2,1,0:T(8,128)(2,1)}), bf16[256,16,128]{2,1,0:T(8,128)(2,1)}) %all-gather.11.cloned.1.call-update) | async-done | bytes 1048592 | tf_op jit(solution)/shard_map/all_gather | solution.py:403
  301.7 29.3 %synthesize_grad.1 = bf16[32,64,32,128]{3,2,1,0:T(8,128)(2,1)} custom-call(bf16[8,32,16,128]{3,2,1,0:T(8,128)(2,1)} %bitcast.17, bf16[2048,512]{1,0:T(8,128)(2,1)} %constant.60.clone.back_high_ref.high_ref, bf16[2048,512]{1,0:T(8,128)(2,1)} %constant.61.clone.back_low_ref.low_ref, bf16[128,192]{1,0:T(8,128)(2,1)} %constant.69.clone.depth_ref, ...), custom_call_target="tpu_custom_call" | custom-call | flops 17179869184 | bytes 16777216 | tf_op jit(solution)/shard_map/synthesize_grad/pallas_call | solution.py:356
Async XLA Ops:
  8.0 113.7 %all-gather.9.cloned.1.call-start = ((), (), s32[]{:S(2)}) async-start(), calls=%async_computation.2 | async-start | bytes 1179648 | tf_op jit(solution)/shard_map/all_gather | solution.py:403
  205.2 29.4 %all-to-all-start.1 = ((bf16[8,32,16,128]{3,2,1,0:T(8,128)(2,1)}), bf16[8,32,16,128]{3,2,1,0:T(8,128)(2,1)S(1)}, u32[]{:S(2)}, u32[]{:S(2)}) async-start(bf16[8,32,16,128]{3,2,1,0:T(8,128)(2,1)} %get-tuple-element.11), calls=%async_computation.1 | async-start | bytes 2097152 | tf_op jit(solution)/shard_map/all_to_all | solution.py:400
  208.8 38.5 %all-gather.13.cloned.1.call-start = ((), (), s32[]{:S(2)}) async-start(), calls=%async_computation.4 | async-start | bytes 1310720 | tf_op jit(solution)/shard_map/all_gather | solution.py:425
  209.3 50.0 %all-gather.15.cloned.1.call-start = ((), (), s32[]{:S(2)}) async-start(), calls=%async_computation.5 | async-start | bytes 1310720 | tf_op jit(solution)/shard_map/all_gather | solution.py:452
  234.6 1.0 copy-start
  245.3 56.4 %all-gather.11.cloned.1.call-start = ((), (), s32[]{:S(2)}) async-start(), calls=%async_computation.3 | async-start | bytes 1179648 | tf_op jit(solution)/shard_map/all_gather | solution.py:403
Sparse Core Ops, SparseCore 0:
  84.2 37.4 all-gather.8
Sparse Core Ops, SparseCore 1:
  211.4 17.8 all-gather.12
  245.4 13.8 all-gather.14
  261.3 40.4 all-gather.10

commit v2 on v1

v2 whole, which is shorter than its diff:
```python
import functools
import math

import jax
import jax.numpy as jnp
import ml_dtypes
import numpy as np
from jax import lax
from jax.experimental import pallas as pl
from jax.experimental.pallas import tpu as pltpu
from jax.sharding import PartitionSpec as P

CHANNELS = 32
NX = 128
NY = 128
NZ = 128
MX = 16
MY = 16
MZ = 32
SAMPLES = 4
PAIR = 2
CHUNKS = 2
PLANE_GAIN = 1.66526
VMEM_BYTES = 56 * 1024 * 1024

NT = (((1,), (1,)), ((), ()))
NN = (((1,), (0,)), ((), ()))


def f32_dot(left_op, right_op, dims=NN):
    return lax.dot_general(left_op, right_op, dims, preferred_element_type=jnp.float32)


def mode_list(length, count):
    half_ids = np.arange(count // 2)
    return np.concatenate([half_ids, length - count // 2 + half_ids])


def split_pair(table):
    high = table.astype(np.float32).astype(ml_dtypes.bfloat16)
    low = (table - high.astype(np.float64)).astype(np.float32).astype(ml_dtypes.bfloat16)
    return high, low


def depth_scales():
    return np.where(np.arange(MZ) == 0, 1.0, 2.0) / float(NX * NY * NZ)


def plane_angles(x_cells, y_cells, blocks):
    kx = mode_list(NX, MX)
    ky = mode_list(NY, MY)
    turns_x = (kx[:, None] * x_cells[None, :] % NX) / NX
    turns_y = (ky[:, None] * y_cells[None, :] % NY) / NY
    turns = turns_x[:, None, :, None] + turns_y[None, :, None, :]
    turns = turns.reshape(blocks, MX // blocks * MY, x_cells.size * y_cells.size)
    return 2.0 * math.pi * turns


def plane_table(x_len, y_len, blocks):
    angles = plane_angles(np.arange(x_len), np.arange(y_len), blocks)
    table = np.stack([np.cos(angles), -np.sin(angles)], axis=1)
    table = PLANE_GAIN * table.reshape(2 * MX * MY, x_len * y_len)
    return table.astype(np.float32).astype(ml_dtypes.bfloat16)


def plane_fit():
    exact = np.cos(2.0 * math.pi * np.arange(NX) / NX)
    rounded = (PLANE_GAIN * exact).astype(np.float32).astype(ml_dtypes.bfloat16)
    return (rounded.astype(np.float64) * exact).sum() / (exact * exact).sum()


def shift_tables(x_len, y_len, x_parts, y_parts):
    angles = plane_angles(np.arange(x_parts) * x_len, np.arange(y_parts) * y_len, y_parts)
    angles = np.moveaxis(angles, 2, 0)
    cosine = np.stack([np.cos(angles), np.cos(angles)], axis=2)
    signed = np.stack([np.sin(angles), -np.sin(angles)], axis=2)
    shape = (x_parts * y_parts, 1, 2 * MX * MY)
    cosine, signed = cosine / plane_fit(), signed / plane_fit()
    return cosine.reshape(shape).astype(np.float32), signed.reshape(shape).astype(np.float32)


def depth_angles():
    turns = (np.arange(MZ)[:, None] * np.arange(NZ)[None, :] % NZ) / NZ
    return 2.0 * math.pi * turns


def analysis_table(scale_vec):
    angles = depth_angles()
    table = np.concatenate([np.cos(angles), np.sin(angles)]) * np.tile(scale_vec, 2)[:, None]
    table = table.astype(np.float32).astype(ml_dtypes.bfloat16)
    return np.concatenate([table, table], axis=1)


def synthesis_table(scale_vec):
    angles = depth_angles()
    table = np.concatenate([np.cos(angles), np.sin(angles)]) * np.tile(scale_vec, 2)[:, None]
    high, low = split_pair(table.T)
    return np.concatenate([high, high, low], axis=1)


def spread_input():
    one = np.repeat(np.eye(CHANNELS), CHANNELS, axis=1)
    return np.concatenate([one, one]).astype(ml_dtypes.bfloat16)


def spread_output():
    one = np.tile(np.eye(CHANNELS), (1, CHANNELS))
    return np.concatenate([one, one]).astype(ml_dtypes.bfloat16)


def halves(value):
    high = value.astype(jnp.bfloat16)
    low = (value - high.astype(jnp.float32)).astype(jnp.bfloat16)
    return high, low


def swap_parts(value):
    width = value.shape[1]
    blocks = [
        pltpu.roll(value[:, at : at + 128], 64, 1) for at in range(0, width, 128)
    ]
    return jnp.concatenate(blocks, axis=1)


def part_signs(width):
    lane_ids = lax.broadcasted_iota(jnp.int32, (1, width), 1)
    return jnp.where(lane_ids % 128 < 64, 1.0, -1.0).astype(jnp.float32)


def analyze_pair(grids, plane_ref, depth_ref, cos_ref, sin_ref, out_ref, x_parts, y_parts):
    plane = f32_dot(plane_ref[...], grids)
    signs = part_signs(plane.shape[0])
    mode_len = MZ // x_parts
    for chan in range(PAIR):
        high, low = halves(plane[:, chan * NZ : (chan + 1) * NZ])
        both = f32_dot(depth_ref[...], jnp.concatenate([high, low], axis=1), NT)
        spectrum = both[:MZ] + signs * swap_parts(both[MZ:])
        spectrum = spectrum * cos_ref[...] + swap_parts(spectrum) * sin_ref[...]
        for gx in range(x_parts):
            for gy in range(y_parts):
                out_ref[gx * y_parts + gy, chan] = spectrum[
                    gx * mode_len : (gx + 1) * mode_len, gy * 128 : (gy + 1) * 128
                ].astype(jnp.bfloat16)


def depth_fields(spec_ref, depth_ref, cos_ref, sin_ref, x_parts, y_parts):
    fields = []
    for chan in range(PAIR):
        rows = [
            jnp.concatenate(
                [spec_ref[gx * y_parts + gy, chan].astype(jnp.float32) for gy in range(y_parts)],
                axis=1,
            )
            for gx in range(x_parts)
        ]
        spectrum = jnp.concatenate(rows, axis=0)
        spectrum = spectrum * cos_ref[...] - swap_parts(spectrum) * sin_ref[...]
        turned = -part_signs(spectrum.shape[1]) * swap_parts(spectrum)
        high, low = halves(jnp.concatenate([spectrum, turned], axis=0))
        fields.append(
            f32_dot(depth_ref[...], jnp.concatenate([high, low, high], axis=0)).astype(jnp.bfloat16)
        )
    return jnp.concatenate(fields, axis=0)


def gelu_parts(pre_act):
    size = jnp.abs(pre_act)
    bell = jnp.exp(pre_act * pre_act * -0.5)
    turn = pl.reciprocal(1.0 + (0.3275911 * 0.7071067811865476) * size, approx=False)
    poly = 0.5 * 1.061405429 * turn - 0.5 * 1.453152027
    poly = poly * turn + 0.5 * 1.421413741
    poly = poly * turn - 0.5 * 0.284496736
    poly = poly * turn + 0.5 * 0.254829592
    tail = poly * turn * bell
    value = jnp.maximum(pre_act, 0.0) - size * tail
    normal_cdf = jnp.where(pre_act > 0.0, 1.0 - tail, tail)
    return value, normal_cdf + pre_act * bell * 0.3989422804014327


def analyze_kernel(x_parts, y_parts, grid_ref, plane_ref, depth_ref, cos_ref, sin_ref, out_ref):
    cells = grid_ref.shape[1] * grid_ref.shape[2]
    grids = jnp.concatenate(
        [grid_ref[chan].reshape(cells, NZ) for chan in range(PAIR)], axis=1
    )
    analyze_pair(grids, plane_ref, depth_ref, cos_ref, sin_ref, out_ref, x_parts, y_parts)


def activate_kernel(
    x_parts,
    y_parts,
    spec_ref,
    cot_ref,
    back_ref,
    back_depth_ref,
    plane_ref,
    depth_ref,
    cos_ref,
    sin_ref,
    *rest,
):
    value_ref, out_ref, grad_ref = rest[-3:]
    fields = depth_fields(spec_ref, back_depth_ref, cos_ref, sin_ref, x_parts, y_parts)
    x_len, y_len = cot_ref.shape[1], cot_ref.shape[2]
    step = min(8, x_len)
    for x_at in range(0, x_len, step):
        rows = slice(x_at * y_len, (x_at + step) * y_len)
        pre_act = f32_dot(back_ref[rows], fields, NT)
        for chan in range(PAIR):
            lanes = slice(chan * NZ, (chan + 1) * NZ)
            value, slope = gelu_parts(pre_act[:, lanes])
            value_ref[chan, x_at : x_at + step] = value.astype(jnp.bfloat16).reshape(step, y_len, NZ)
            cotangent = cot_ref[chan, x_at : x_at + step].reshape(step * y_len, NZ)
            grad_ref[rows, lanes] = (cotangent.astype(jnp.float32) * slope).astype(jnp.bfloat16)
    analyze_pair(
        grad_ref[...], plane_ref, depth_ref, cos_ref, sin_ref, out_ref, x_parts, y_parts
    )


def synthesize_kernel(
    x_parts, y_parts, spec_ref, back_ref, depth_ref, cos_ref, sin_ref, *rest
):
    out_ref = rest[-1]
    fields = depth_fields(spec_ref, depth_ref, cos_ref, sin_ref, x_parts, y_parts)
    x_len, y_len = out_ref.shape[1], out_ref.shape[2]
    step = min(8, x_len)
    for x_at in range(0, x_len, step):
        rows = slice(x_at * y_len, (x_at + step) * y_len)
        grid = f32_dot(back_ref[rows], fields, NT)
        for chan in range(PAIR):
            out_ref[chan, x_at : x_at + step] = (
                grid[:, chan * NZ : (chan + 1) * NZ].astype(jnp.bfloat16).reshape(step, y_len, NZ)
            )


def mode_rows(value, spread_ref):
    high = value.astype(jnp.bfloat16).astype(jnp.float32)
    both = jnp.concatenate([high, value - high], axis=0)
    return f32_dot(both.T.astype(jnp.bfloat16), spread_ref[...])


def mix_kernel(adjoint, mode_len, step_len, *refs):
    recv_refs, refs = refs[:CHUNKS], refs[CHUNKS:]
    weight_ref, spread_ref, gather_ref, share_ref, *refs = refs
    kept_ref, refs = (refs[0], refs[1:]) if adjoint else (None, refs)
    send_ref, out_refs = refs[0], refs[1 : 1 + CHUNKS]
    taken_ref, mixed_ref = refs[1 + CHUNKS :]
    chunk_len = CHANNELS // CHUNKS
    step_at = pl.program_id(0)

    @pl.when(step_at == 0)
    def _():
        for chunk, recv_ref in enumerate(recv_refs):
            total = recv_ref[0].astype(jnp.float32)
            for source in range(1, recv_ref.shape[0]):
                total = total + recv_ref[source].astype(jnp.float32)
            rows = chunk_len * mode_len
            taken_ref[chunk * rows : (chunk + 1) * rows] = total.reshape(rows, 128)

    half = 64
    inputs = []
    for at in range(step_len):
        mode_at = step_at * step_len + at
        here = pl.ds(mode_at, CHANNELS, stride=mode_len) if mode_len > 1 else slice(None)
        taken = taken_ref[here, :]
        inputs.append(taken)
        spread = mode_rows(taken, spread_ref)
        real_in, imag_in = spread[:half], spread[half:]
        w_real = weight_ref[:, at, :, 0, :].reshape(half, CHANNELS * CHANNELS)
        w_imag = weight_ref[:, at, :, 1, :].reshape(half, CHANNELS * CHANNELS)
        if adjoint:
            real_part = real_in * w_real + imag_in * w_imag
            imag_part = imag_in * w_real - real_in * w_imag
            terms = jnp.concatenate([real_part, imag_part], axis=0)
        else:
            real_part = real_in * w_real - imag_in * w_imag
            imag_part = imag_in * w_real + real_in * w_imag
            terms = jnp.concatenate([real_part, imag_part], axis=0)
            width = terms.shape[1]
            while width > 128:
                width //= 2
                terms = terms[:, :width] + terms[:, width:]
        high, low = halves(terms)
        mixed = f32_dot(jnp.concatenate([high, low], axis=1), gather_ref[...])
        mixed_ref[here, :] = mixed.T[:CHANNELS]

    high, low = halves(jnp.concatenate(inputs, axis=1))
    shared = f32_dot(jnp.concatenate([high, low], axis=0), share_ref[...])
    shared = shared[:CHANNELS] + shared[CHANNELS:]
    lanes = send_ref.shape[-1]
    for rank in range(send_ref.shape[0]):
        part = shared[:, rank * lanes : (rank + 1) * lanes]
        if adjoint:
            send_ref[rank, 0, 0] = kept_ref[rank, 0]
            send_ref[rank, 0, 1] = part
        else:
            send_ref[rank, 0] = part

    @pl.when(step_at == pl.num_programs(0) - 1)
    def _():
        rows = chunk_len * mode_len
        for chunk, out_ref in enumerate(out_refs):
            part = mixed_ref[chunk * rows : (chunk + 1) * rows]
            out_ref[...] = part.reshape(out_ref.shape).astype(jnp.bfloat16)


def weight_kernel(terms_ref, spread_u_ref, spread_g_ref, out_ref):
    kx_len, step_len, row_len = out_ref.shape[:3]
    half = kx_len * row_len
    real_part, imag_part = 0.0, 0.0
    for sample in range(terms_ref.shape[0]):
        shape = (step_len, 2, half, CHANNELS * CHANNELS)
        spread_u = mode_rows(terms_ref[sample, 0, 0], spread_u_ref).reshape(shape)
        spread_g = mode_rows(terms_ref[sample, 0, 1], spread_g_ref).reshape(shape)
        u_real, u_imag = spread_u[:, 0], spread_u[:, 1]
        g_real, g_imag = spread_g[:, 0], spread_g[:, 1]
        real_part = real_part + (u_real * g_real + u_imag * g_imag)
        imag_part = imag_part + (u_real * g_imag - u_imag * g_real)
    for at in range(step_len):
        for kx in range(kx_len):
            rows = slice(kx * row_len, (kx + 1) * row_len)
            out_ref[kx, at, :, 0, :] = real_part[at, rows]
            out_ref[kx, at, :, 1, :] = imag_part[at, rows]


def whole_spec(array):
    zeros = (0,) * array.ndim
    return pl.BlockSpec(array.shape, lambda *at: zeros)


def params():
    return pltpu.CompilerParams(vmem_limit_bytes=VMEM_BYTES)


def cost(flops, bytes_accessed):
    return pl.CostEstimate(
        flops=int(flops), bytes_accessed=int(bytes_accessed), transcendentals=0
    )


def share_table(step_len, kx_len, row_len, share_len):
    ids = np.arange(step_len * 2 * kx_len * row_len)
    ids = ids.reshape(step_len * 2 * kx_len, row_len // share_len, share_len)
    ids = np.moveaxis(ids, 1, 0).reshape(-1)
    return (np.arange(ids.size)[:, None] == ids[None, :]).astype(ml_dtypes.bfloat16)


def shards(x_parts, y_parts, field, cotangent, spectral_weight):
    chan_len, x_len, y_len = field.shape[1:4]
    kx_len, mode_len, row_len = spectral_weight.shape[:3]
    parts = x_parts * y_parts
    dp_len = lax.axis_size("dp")
    share_len = row_len // dp_len
    step_len = min(4, mode_len)
    chunk_len = chan_len // CHUNKS
    chunk_steps = chunk_len // PAIR

    plane = plane_table(x_len, y_len, y_parts)
    back = jnp.asarray(plane.T.copy())
    plane = jnp.asarray(plane)
    forward_plain = jnp.asarray(analysis_table(np.ones(MZ)))
    forward_scaled = jnp.asarray(analysis_table(depth_scales()))
    back_scaled = jnp.asarray(synthesis_table(depth_scales()))
    back_plain = jnp.asarray(synthesis_table(np.ones(MZ)))
    cosines, sines = shift_tables(x_len, y_len, x_parts, y_parts)
    place = lax.axis_index("gx") * y_parts + lax.axis_index("gy")
    shift_cos = lax.dynamic_index_in_dim(jnp.asarray(cosines), place, 0, False)
    shift_sin = lax.dynamic_index_in_dim(jnp.asarray(sines), place, 0, False)

    pair_spec = pl.BlockSpec((parts, PAIR, mode_len, 128), lambda at: (0, at, 0, 0))
    grid_shape = jax.ShapeDtypeStruct((chan_len, x_len, y_len, NZ), jnp.bfloat16)
    spec_shape = jax.ShapeDtypeStruct((parts, chunk_len, mode_len, 128), jnp.bfloat16)
    grid_bytes = chunk_len * x_len * y_len * NZ * 2
    plane_flops = 2 * 2 * MX * MY * x_len * y_len * NZ * chunk_len * 2

    def pair_grid(chunk):
        return pl.BlockSpec(
            (PAIR, x_len, y_len, NZ), lambda at: (at + chunk * chunk_steps, 0, 0, 0)
        )

    def tables_of(*arrays):
        return [whole_spec(array) for array in arrays]

    def call(body, name, operands, specs, earlier, out_shapes, out_specs, scratch, flops, moved):
        aliases = {}
        if earlier is not None:
            aliases = {len(operands): 0}
            operands = (*operands, earlier)
            specs = [*specs, pl.BlockSpec(memory_space=pl.ANY)]
        return pl.pallas_call(
            functools.partial(body, x_parts, y_parts),
            name=name,
            grid=(chunk_steps,),
            in_specs=specs,
            out_specs=out_specs,
            out_shape=out_shapes,
            scratch_shapes=scratch,
            input_output_aliases=aliases,
            compiler_params=params(),
            cost_estimate=cost(flops, moved),
        )(*operands)

    def mix(name, received, spread, gather, kept):
        adjoint = kept is not None
        steps = mode_len // step_len
        lanes = step_len * 2 * kx_len * share_len
        small = (chan_len * mode_len, 128)
        operands = [*received, spectral_weight, spread, gather, share]
        specs = [
            *tables_of(*received),
            pl.BlockSpec(
                (kx_len, step_len, row_len, 2, chan_len * chan_len), lambda at: (0, at, 0, 0, 0)
            ),
            *tables_of(spread, gather, share),
        ]
        one_send = pl.BlockSpec((dp_len, 1, chan_len, lanes), lambda at: (0, at, 0, 0))
        if adjoint:
            operands.append(kept)
            specs.append(one_send)
            send_shape = (dp_len, steps, 2, chan_len, lanes)
            send_spec = pl.BlockSpec((dp_len, 1, 2, chan_len, lanes), lambda at: (0, at, 0, 0, 0))
        else:
            send_shape = (dp_len, steps, chan_len, lanes)
            send_spec = one_send
        chunk_shape = (chunk_len, mode_len, 128)
        return pl.pallas_call(
            functools.partial(mix_kernel, adjoint, mode_len, step_len),
            name=name,
            grid=(steps,),
            in_specs=specs,
            out_specs=[send_spec]
            + [pl.BlockSpec(chunk_shape, lambda at: (0, 0, 0)) for _ in range(CHUNKS)],
            out_shape=[jax.ShapeDtypeStruct(send_shape, jnp.float32)]
            + [jax.ShapeDtypeStruct(chunk_shape, jnp.bfloat16) for _ in range(CHUNKS)],
            scratch_shapes=[pltpu.VMEM(small, jnp.float32), pltpu.VMEM(small, jnp.float32)],
            compiler_params=params(),
            cost_estimate=cost(mode_len * 2e8, spectral_weight.size * 4),
        )(*operands)

    def exchange(partial_sums):
        return lax.all_to_all(partial_sums, ("gx", "gy"), 0, 0, tiled=True)

    def collect(spectrum):
        return lax.all_gather(spectrum, ("gx", "gy"), axis=0, tiled=False)

    share = jnp.asarray(share_table(step_len, kx_len, row_len, share_len))
    spread_in, spread_out = jnp.asarray(spread_input()), jnp.asarray(spread_output())
    onto_out = np.zeros((128, 128))
    onto_out[np.arange(128), np.arange(128) % CHANNELS] = 1.0
    onto_out = jnp.asarray(np.concatenate([onto_out, onto_out]).astype(ml_dtypes.bfloat16))
    onto_in = np.zeros((chan_len * chan_len, 128))
    onto_in[np.arange(chan_len * chan_len), np.arange(chan_len * chan_len) // CHANNELS] = 1.0
    onto_in = jnp.asarray(np.concatenate([onto_in, onto_in]).astype(ml_dtypes.bfloat16))

    received = []
    tables = (plane, forward_plain, shift_cos, shift_sin)
    for chunk in range(CHUNKS):
        partial_u = call(
            analyze_kernel,
            "analyze_field",
            (field[0], *tables),
            [pair_grid(chunk), *tables_of(*tables)],
            None,
            spec_shape,
            pair_spec,
            [],
            plane_flops,
            grid_bytes,
        )
        received.append(exchange(partial_u))
    send_u, *spec_v = mix("mix_forward", received, spread_in, onto_out, None)

    received, out_grid = [], None
    gathered = [collect(spectrum) for spectrum in spec_v]
    tables = (back, back_scaled, plane, forward_scaled, shift_cos, shift_sin)
    for chunk in range(CHUNKS):
        out_grid, partial_g = call(
            activate_kernel,
            "activate",
            (gathered[chunk], cotangent[0], *tables),
            [pair_spec, pair_grid(chunk), *tables_of(*tables)],
            out_grid,
            [grid_shape, spec_shape],
            [pair_grid(chunk), pair_spec],
            [pltpu.VMEM((x_len * y_len, PAIR * NZ), jnp.bfloat16)],
            4 * plane_flops,
            2 * grid_bytes,
        )
        received.append(exchange(partial_g))
    send_terms, *spec_du = mix("mix_adjoint", received, spread_out, onto_in, send_u)

    gathered = [collect(spectrum) for spectrum in spec_du]
    terms = lax.all_to_all(send_terms, "dp", 0, 0, tiled=True)
    lanes = terms.shape[-1]
    weight_grad = pl.pallas_call(
        weight_kernel,
        name="weight_terms",
        grid=(mode_len // step_len,),
        in_specs=[
            pl.BlockSpec((dp_len, 1, 2, chan_len, lanes), lambda at: (0, at, 0, 0, 0)),
            *tables_of(spread_in, spread_out),
        ],
        out_specs=pl.BlockSpec(
            (kx_len, step_len, share_len, 2, chan_len * chan_len), lambda at: (0, at, 0, 0, 0)
        ),
        out_shape=jax.ShapeDtypeStruct(
            (kx_len, mode_len, share_len, 2, chan_len * chan_len), jnp.float32
        ),
        compiler_params=params(),
        cost_estimate=cost(mode_len * 2e8, mode_len * 2e6),
    )(terms, spread_in, spread_out)

    grad_grid = None
    tables = (back, back_plain, shift_cos, shift_sin)
    for chunk in range(CHUNKS):
        grad_grid = call(
            synthesize_kernel,
            "synthesize_grad",
            (gathered[chunk], *tables),
            [pair_spec, *tables_of(*tables)],
            grad_grid,
            grid_shape,
            pair_grid(chunk),
            [],
            plane_flops,
            grid_bytes,
        )
    return (out_grid[None], grad_grid[None], weight_grad)


def solution(mesh):
    placed = (
        P("dp", None, "gx", "gy", None),
        P("dp", None, "gx", "gy", None),
        P("gy", "gx", None, None, None),
    )
    return jax.shard_map(
        functools.partial(shards, mesh.shape["gx"], mesh.shape["gy"]),
        mesh=mesh,
        in_specs=placed,
        out_specs=(
            P("dp", None, "gx", "gy", None),
            P("dp", None, "gx", "gy", None),
            P("gy", "gx", "dp", None, None),
        ),
        check_vma=False,
    )
```

time: 339 us -> 335 us (0.988)
  blocking collectives: 34.1 us -> 174 us
  waiting for transfers between devices: 106 us -> 2.51 us
  Pallas kernels: 175 us -> 141 us
  between operations: 15.7 us -> 0.68 us
  starting transfers between devices: 3.73 us -> 14.2 us
    all_gather x0 -> x4, blocking collectives: none -> 138 us  [collect(): return lax.all_gather(spectrum, ('gx', 'gy'), axis=0, tiled=False)]
    all_gather x4 -> x0, waiting for transfers between devices: 79.8 us -> none  [the longest x2 67.8 us: collect(): return lax.all_gather(spectrum, ('gx', 'gy'), axis=0, tiled=False)]
    pallas_call x3 -> x6, Pallas kernels: 145 us -> 117 us  [call(): pl.pallas_call(functools.partial(body, x_parts, y_parts), name=name, grid...]
    all_to_all x1 -> x2, waiting for transfers between devices: 25.2 us -> 2.51 us  [exchange(): return lax.all_to_all(partial_sums, ('gx', 'gy'), 0, 0, tiled=True)]
    all_to_all x1 -> x2, starting transfers between devices: 3.56 us -> 10.8 us  [exchange(): return lax.all_to_all(partial_sums, ('gx', 'gy'), 0, 0, tiled=True)]
    pallas_call x1, Pallas kernels: 12.2 us -> 5.74 us  [shards(): pl.pallas_call(weight_kernel, name='weight_terms', grid=(mode_len // step...]
    all_to_all x0 -> x1, starting transfers between devices: none -> 3.47 us  [shards(): terms = lax.all_to_all(send_terms, 'dp', 0, 0, tiled=True)]
    all_to_all x1 -> x2, blocking collectives: 34.1 us -> 36 us  [exchange(): return lax.all_to_all(partial_sums, ('gx', 'gy'), 0, 0, tiled=True)]
  transfers between devices with their start and end apart: 5 -> 3, of which waited for: 4 -> 1; matrix products, arithmetic and copies ran while one was open for 0% -> 0% of each run, Pallas kernels for 6% -> 21%
where the time goes in v2:
time: 335 us; the launch traced here: 334 us
  blocking collectives  174 us (52%)
  Pallas kernels  141 us (42%)
  starting transfers between devices  14.2 us (4%)
    all_gather x4, blocking collectives, collect(): return lax.all_gather(spectrum, ('gx', 'gy'), axis=0, tiled=False)  138 us
    pallas_call x6, Pallas kernels, call(): pl.pallas_call(functools.partial(body, x_parts, y_parts), name=name, grid...  117 us
    all_to_all x2, blocking collectives, exchange(): return lax.all_to_all(partial_sums, ('gx', 'gy'), 0, 0, tiled=True)  36 us
    pallas_call x2, Pallas kernels, mix(): pl.pallas_call(functools.partial(mix_kernel, adjoint, mode_len, step_len)...  18.6 us
    all_to_all x2, starting transfers between devices, exchange(): return lax.all_to_all(partial_sums, ('gx', 'gy'), 0, 0, tiled=True)  10.8 us
  transfers between devices with their start and end apart: 3, of which 1 were waited for; matrix products, arithmetic and copies ran while one was open for 0% of the time, Pallas kernels for 21%

profile of v2, /device:TPU:0, one launch (start us, length us, event | category | flops | bytes accessed | tf_op | source)
XLA Modules:
  0.0 333.9 jit_solution(10272551930859220423)
XLA Ops:
  0.6 1.3 dynamic-slice_bitcast_fusion
  1.9 12.9 %analyze_field.2 = bf16[8,16,16,128]{3,2,1,0:T(8,128)(2,1)} custom-call(bf16[32,64,32,128]{3,2,1,0:T(8,128)(2,1)} %bitcast.17, bf16[512,2048]{1,0:T(8,128)(2,1)} %constant.46.clone.plane_ref, bf16[64,256]{1,0:T(8,128)(2,1)} %constant.47.clone.depth_ref, f32[1,512]{1,0:T(1,128)} %get-tuple-element.24.cos_ref, f32[1,512]{1,0:T(1,128)} %get-tuple-element.23.sin_ref), custom_call_target="tpu_custom_call" | custom-call | flops 8589934592 | bytes 8388608 | tf_op jit(solution)/shard_map/analyze_field/pallas_call | solution.py:389
  14.9 7.3 %all-to-all-start = ((bf16[8,16,16,128]{3,2,1,0:T(8,128)(2,1)}), bf16[8,16,16,128]{3,2,1,0:T(8,128)(2,1)S(1)}, u32[]{:S(2)}, u32[]{:S(2)}) async-start(bf16[8,16,16,128]{3,2,1,0:T(8,128)(2,1)} %analyze_field.2), calls=%async_computation | async-start | bytes 1048576 | tf_op jit(solution)/shard_map/all_to_all | solution.py:440
  22.1 12.9 %analyze_field.3 = bf16[8,16,16,128]{3,2,1,0:T(8,128)(2,1)} custom-call(bf16[32,64,32,128]{3,2,1,0:T(8,128)(2,1)} %bitcast.18, bf16[512,2048]{1,0:T(8,128)(2,1)} %constant.46.clone.plane_ref, bf16[64,256]{1,0:T(8,128)(2,1)} %constant.47.clone.depth_ref, f32[1,512]{1,0:T(1,128)} %get-tuple-element.24.cos_ref, f32[1,512]{1,0:T(1,128)} %get-tuple-element.23.sin_ref), custom_call_target="tpu_custom_call" | custom-call | flops 8589934592 | bytes 8388608 | tf_op jit(solution)/shard_map/analyze_field/pallas_call | solution.py:389
  35.0 2.5 all-to-all-done.refs_0_
  37.5 0.0 copy-start.2
  37.5 18.4 %all_to_all.25.refs_1_ = bf16[8,16,16,128]{3,2,1,0:T(8,128)(2,1)} all-to-all(bf16[8,16,16,128]{3,2,1,0:T(8,128)(2,1)} %analyze_field.3), channel_id=1, replica_groups=mesh['dp'=4,'gx'=2,'gy'=4] {'gx','gy'}, dimensions={0} | all-to-all | bytes 1048576 | tf_op jit(solution)/shard_map/all_to_all | solution.py:440
  55.9 0.0 copy-done.2
  55.9 8.5 %mix_forward.1 = (f32[4,4,32,128]{3,2,1,0:T(8,128)}, bf16[16,16,128]{2,1,0:T(8,128)(2,1)}, bf16[16,16,128]{2,1,0:T(8,128)(2,1)}) custom-call(bf16[8,16,16,128]{3,2,1,0:T(8,128)(2,1)} %copy-done.2, bf16[8,16,16,128]{3,2,1,0:T(8,128)(2,1)} %all_to_all.25.refs_1_, f32[4,16,16,2,1024]{4,3,2,1,0:T(2,128)} %refs_2_.3, ...), custom_call_target="tpu_custom_call" | custom-call | flops 3200000000 | bytes 8388608 | tf_op jit(solution)/shard_map/mix_forward/pallas_call | solution.py:425
  64.4 34.7 %all-gather = bf16[128,16,128]{2,1,0:T(8,128)(2,1)} all-gather(bf16[16,16,128]{2,1,0:T(8,128)(2,1)} %get-tuple-element.13), channel_id=2, replica_groups=mesh['dp'=4,'gx'=2,'gy'=4] {'gx','gy'}, dimensions={0}, use_global_device_ids=true | all-gather | bytes 589824 | tf_op jit(solution)/shard_map/all_gather | solution.py:443
  99.1 34.5 %all-gather.1 = bf16[128,16,128]{2,1,0:T(8,128)(2,1)} all-gather(bf16[16,16,128]{2,1,0:T(8,128)(2,1)} %get-tuple-element.14), channel_id=3, replica_groups=mesh['dp'=4,'gx'=2,'gy'=4] {'gx','gy'}, dimensions={0}, use_global_device_ids=true | all-gather | bytes 589824 | tf_op jit(solution)/shard_map/all_gather | solution.py:443
  133.6 33.9 %activate.2 = (bf16[32,64,32,128]{3,2,1,0:T(8,128)(2,1)}, bf16[8,16,16,128]{3,2,1,0:T(8,128)(2,1)}) custom-call(bf16[8,16,16,128]{3,2,1,0:T(8,128)(2,1)} %bitcast.16, bf16[32,64,32,128]{3,2,1,0:T(8,128)(2,1)} %bitcast.19, bf16[2048,512]{1,0:T(8,128)(2,1)} %constant.45.clone.back_ref, bf16[128,192]{1,0:T(8,128)(2,1)} %constant.49.clone.back_depth_ref, ...), custom_call_target="tpu_custom_call" | custom-call | flops 34359738368 | bytes 16777216 | tf_op jit(solution)/shard_map/activate/pallas_call | solution.py:389
  167.5 3.5 %all-to-all-start.2 = ((bf16[8,16,16,128]{3,2,1,0:T(8,128)(2,1)}), bf16[8,16,16,128]{3,2,1,0:T(8,128)(2,1)S(1)}, u32[]{:S(2)}, u32[]{:S(2)}) async-start(bf16[8,16,16,128]{3,2,1,0:T(8,128)(2,1)} %get-tuple-element.17), calls=%async_computation.2 | async-start | bytes 1048576 | tf_op jit(solution)/shard_map/all_to_all | solution.py:440
  171.0 34.1 %activate.3 = (bf16[32,64,32,128]{3,2,1,0:T(8,128)(2,1)}, bf16[8,16,16,128]{3,2,1,0:T(8,128)(2,1)}) custom-call(bf16[8,16,16,128]{3,2,1,0:T(8,128)(2,1)} %bitcast.14, bf16[32,64,32,128]{3,2,1,0:T(8,128)(2,1)} %bitcast.20, bf16[2048,512]{1,0:T(8,128)(2,1)} %constant.45.clone.back_ref, ...), custom_call_target="tpu_custom_call", output_to_operand_aliasing={{0}: (8, {})} | custom-call | flops 34359738368 | bytes 16777216 | tf_op jit(solution)/shard_map/activate/pallas_call | solution.py:389
  205.1 0.0 all-to-all-done.2.refs_0_
  205.1 0.0 copy-start
  205.2 17.6 %all_to_all.26.refs_1_ = bf16[8,16,16,128]{3,2,1,0:T(8,128)(2,1)} all-to-all(bf16[8,16,16,128]{3,2,1,0:T(8,128)(2,1)} %get-tuple-element.18), channel_id=1, replica_groups=mesh['dp'=4,'gx'=2,'gy'=4] {'gx','gy'}, dimensions={0} | all-to-all | bytes 1048576 | tf_op jit(solution)/shard_map/all_to_all | solution.py:440
  222.7 0.0 copy-done
  222.7 10.1 %mix_adjoint.1 = (f32[4,4,2,32,128]{4,3,2,1,0:T(8,128)}, bf16[16,16,128]{2,1,0:T(8,128)(2,1)}, bf16[16,16,128]{2,1,0:T(8,128)(2,1)}) custom-call(bf16[8,16,16,128]{3,2,1,0:T(8,128)(2,1)} %copy-done, bf16[8,16,16,128]{3,2,1,0:T(8,128)(2,1)} %all_to_all.26.refs_1_, f32[4,16,16,2,1024]{4,3,2,1,0:T(2,128)} %refs_2_.3, ...), custom_call_target="tpu_custom_call" | custom-call | flops 3200000000 | bytes 8388608 | tf_op jit(solution)/shard_map/mix_adjoint/pallas_call | solution.py:425
  232.8 34.5 %all-gather.2 = bf16[128,16,128]{2,1,0:T(8,128)(2,1)} all-gather(bf16[16,16,128]{2,1,0:T(8,128)(2,1)} %get-tuple-element.20), channel_id=4, replica_groups=mesh['dp'=4,'gx'=2,'gy'=4] {'gx','gy'}, dimensions={0}, use_global_device_ids=true | all-gather | bytes 589824 | tf_op jit(solution)/shard_map/all_gather | solution.py:443
  267.3 33.9 %all-gather.3 = bf16[128,16,128]{2,1,0:T(8,128)(2,1)} all-gather(bf16[16,16,128]{2,1,0:T(8,128)(2,1)} %get-tuple-element.21), channel_id=5, replica_groups=mesh['dp'=4,'gx'=2,'gy'=4] {'gx','gy'}, dimensions={0}, use_global_device_ids=true | all-gather | bytes 589824 | tf_op jit(solution)/shard_map/all_gather | solution.py:443
  301.2 3.5 %all-to-all-start.4 = ((f32[4,4,2,32,128]{4,3,2,1,0:T(8,128)}), f32[4,4,2,32,128]{4,3,2,1,0:T(8,128)S(1)}, u32[]{:S(2)}, u32[]{:S(2)}) async-start(f32[4,4,2,32,128]{4,3,2,1,0:T(8,128)} %get-tuple-element.22), calls=%async_computation.4 | async-start | bytes 1048576 | tf_op jit(solution)/shard_map/all_to_all | solution.py:492
  304.6 11.4 %synthesize_grad.2.rest_0_ = bf16[32,64,32,128]{3,2,1,0:T(8,128)(2,1)} custom-call(bf16[8,16,16,128]{3,2,1,0:T(8,128)(2,1)} %bitcast.15, bf16[2048,512]{1,0:T(8,128)(2,1)} %constant.45.clone.back_ref, bf16[128,192]{1,0:T(8,128)(2,1)} %constant.50.clone.depth_ref, f32[1,512]{1,0:T(1,128)} %get-tuple-element.24.cos_ref, f32[1,512]{1,0:T(1,128)} %get-tuple-element.23.sin_ref), custom_call_target="tpu_custom_call" | custom-call | flops 8589934592 | bytes 8388608 | tf_op jit(solution)/shard_map/synthesize_grad/pallas_call | solution.py:389
  316.0 11.4 %synthesize_grad.3 = bf16[32,64,32,128]{3,2,1,0:T(8,128)(2,1)} custom-call(bf16[8,16,16,128]{3,2,1,0:T(8,128)(2,1)} %bitcast.13, bf16[2048,512]{1,0:T(8,128)(2,1)} %constant.45.clone.back_ref, bf16[128,192]{1,0:T(8,128)(2,1)} %constant.50.clone.depth_ref, f32[1,512]{1,0:T(1,128)} %get-tuple-element.24.cos_ref, ...), custom_call_target="tpu_custom_call", output_to_operand_aliasing={{}: (5, {})} | custom-call | flops 8589934592 | bytes 8388608 | tf_op jit(solution)/shard_map/synthesize_grad/pallas_call | solution.py:389
  327.4 0.0 all-to-all-done.4.terms_ref
  327.4 0.0 copy-start.1
  327.4 0.8 copy-done.1
  328.2 5.7 %weight_terms.1 = f32[4,16,4,2,1024]{4,3,2,1,0:T(2,128)} custom-call(f32[4,4,2,32,128]{4,3,2,1,0:T(8,128)} %copy-done.1, bf16[64,1024]{1,0:T(8,128)(2,1)} %constant.54.clone.refs_3_.spread_u_ref, bf16[64,1024]{1,0:T(8,128)(2,1)} %constant.55.clone.refs_3_.spread_g_ref), custom_call_target="tpu_custom_call" | custom-call | flops 3200000000 | bytes 32000000 | tf_op jit(solution)/shard_map/weight_terms/pallas_call | solution.py:494
Async XLA Ops:
  14.9 22.7 %all-to-all-start = ((bf16[8,16,16,128]{3,2,1,0:T(8,128)(2,1)}), bf16[8,16,16,128]{3,2,1,0:T(8,128)(2,1)S(1)}, u32[]{:S(2)}, u32[]{:S(2)}) async-start(bf16[8,16,16,128]{3,2,1,0:T(8,128)(2,1)} %analyze_field.2), calls=%async_computation | async-start | bytes 1048576 | tf_op jit(solution)/shard_map/all_to_all | solution.py:440
  37.5 18.4 %copy-start.2 = (bf16[8,16,16,128]{3,2,1,0:T(8,128)(2,1)}, bf16[8,16,16,128]{3,2,1,0:T(8,128)(2,1)S(1)}, u32[]{:S(2)}) copy-start(bf16[8,16,16,128]{3,2,1,0:T(8,128)(2,1)S(1)} %all-to-all-done.refs_0_) | copy-start | bytes 1572868
  167.5 37.6 %all-to-all-start.2 = ((bf16[8,16,16,128]{3,2,1,0:T(8,128)(2,1)}), bf16[8,16,16,128]{3,2,1,0:T(8,128)(2,1)S(1)}, u32[]{:S(2)}, u32[]{:S(2)}) async-start(bf16[8,16,16,128]{3,2,1,0:T(8,128)(2,1)} %get-tuple-element.17), calls=%async_computation.2 | async-start | bytes 1048576 | tf_op jit(solution)/shard_map/all_to_all | solution.py:440
  205.1 17.6 %copy-start = (bf16[8,16,16,128]{3,2,1,0:T(8,128)(2,1)}, bf16[8,16,16,128]{3,2,1,0:T(8,128)(2,1)S(1)}, u32[]{:S(2)}) copy-start(bf16[8,16,16,128]{3,2,1,0:T(8,128)(2,1)S(1)} %all-to-all-done.2.refs_0_) | copy-start | bytes 1572868
  301.2 26.2 %all-to-all-start.4 = ((f32[4,4,2,32,128]{4,3,2,1,0:T(8,128)}), f32[4,4,2,32,128]{4,3,2,1,0:T(8,128)S(1)}, u32[]{:S(2)}, u32[]{:S(2)}) async-start(f32[4,4,2,32,128]{4,3,2,1,0:T(8,128)} %get-tuple-element.22), calls=%async_computation.4 | async-start | bytes 1048576 | tf_op jit(solution)/shard_map/all_to_all | solution.py:492
  327.4 0.8 copy-start.1

commit v3 on v2

--- a/solution.py
+++ b/solution.py
@@ -19,7 +19,9 @@
 MZ = 32
 SAMPLES = 4
 PAIR = 2
-CHUNKS = 2
+ANALYZE_CHUNKS = (8, 12, 12)
+ACTIVATE_CHUNKS = (8, 16, 8)
+SYNTHESIZE_CHUNKS = (8, 16, 8)
 PLANE_GAIN = 1.66526
 VMEM_BYTES = 56 * 1024 * 1024
 
@@ -238,32 +240,34 @@
     return f32_dot(both.T.astype(jnp.bfloat16), spread_ref[...])
 
 
-def mix_kernel(adjoint, mode_len, step_len, *refs):
-    recv_refs, refs = refs[:CHUNKS], refs[CHUNKS:]
+def spans(chunks):
+    ends = np.cumsum(chunks)
+    return [(int(end) - size, int(end)) for size, end in zip(chunks, ends)]
+
+
+def mix_kernel(adjoint, mode_len, step_len, taken, given, *refs):
+    recv_refs, refs = refs[: len(taken)], refs[len(taken) :]
     weight_ref, spread_ref, gather_ref, share_ref, *refs = refs
     kept_ref, refs = (refs[0], refs[1:]) if adjoint else (None, refs)
-    send_ref, out_refs = refs[0], refs[1 : 1 + CHUNKS]
-    taken_ref, mixed_ref = refs[1 + CHUNKS :]
-    chunk_len = CHANNELS // CHUNKS
+    send_ref, *out_refs, taken_ref, mixed_ref = refs
     step_at = pl.program_id(0)
 
     @pl.when(step_at == 0)
     def _():
-        for chunk, recv_ref in enumerate(recv_refs):
+        for (start, stop), recv_ref in zip(spans(taken), recv_refs):
             total = recv_ref[0].astype(jnp.float32)
             for source in range(1, recv_ref.shape[0]):
                 total = total + recv_ref[source].astype(jnp.float32)
-            rows = chunk_len * mode_len
-            taken_ref[chunk * rows : (chunk + 1) * rows] = total.reshape(rows, 128)
+            rows = slice(start * mode_len, stop * mode_len)
+            taken_ref[rows] = total.reshape((stop - start) * mode_len, 128)
 
     half = 64
     inputs = []
     for at in range(step_len):
         mode_at = step_at * step_len + at
         here = pl.ds(mode_at, CHANNELS, stride=mode_len) if mode_len > 1 else slice(None)
-        taken = taken_ref[here, :]
-        inputs.append(taken)
-        spread = mode_rows(taken, spread_ref)
+        inputs.append(taken_ref[here, :])
+        spread = mode_rows(inputs[-1], spread_ref)
         real_in, imag_in = spread[:half], spread[half:]
         w_real = weight_ref[:, at, :, 0, :].reshape(half, CHANNELS * CHANNELS)
         w_imag = weight_ref[:, at, :, 1, :].reshape(half, CHANNELS * CHANNELS)
@@ -297,10 +301,11 @@
 
     @pl.when(step_at == pl.num_programs(0) - 1)
     def _():
-        rows = chunk_len * mode_len
-        for chunk, out_ref in enumerate(out_refs):
-            part = mixed_ref[chunk * rows : (chunk + 1) * rows]
-            out_ref[...] = part.reshape(out_ref.shape).astype(jnp.bfloat16)
+        for (start, stop), out_ref in zip(spans(given), out_refs):
+            part = mixed_ref[start * mode_len : stop * mode_len]
+            part = part.reshape(out_ref.shape[1:]).astype(jnp.bfloat16)
+            for target in range(out_ref.shape[0]):
+                out_ref[target] = part
 
 
 def weight_kernel(terms_ref, spread_u_ref, spread_g_ref, out_ref):
@@ -351,8 +356,6 @@
     dp_len = lax.axis_size("dp")
     share_len = row_len // dp_len
     step_len = min(4, mode_len)
-    chunk_len = chan_len // CHUNKS
-    chunk_steps = chunk_len // PAIR
 
     plane = plane_table(x_len, y_len, y_parts)
     back = jnp.asarray(plane.T.copy())
@@ -368,19 +371,23 @@
 
     pair_spec = pl.BlockSpec((parts, PAIR, mode_len, 128), lambda at: (0, at, 0, 0))
     grid_shape = jax.ShapeDtypeStruct((chan_len, x_len, y_len, NZ), jnp.bfloat16)
-    spec_shape = jax.ShapeDtypeStruct((parts, chunk_len, mode_len, 128), jnp.bfloat16)
-    grid_bytes = chunk_len * x_len * y_len * NZ * 2
-    plane_flops = 2 * 2 * MX * MY * x_len * y_len * NZ * chunk_len * 2
-
-    def pair_grid(chunk):
+    grid_bytes = x_len * y_len * NZ * 2
+    plane_flops = 2 * 2 * MX * MY * x_len * y_len * NZ * 2
+
+    def spec_shape(size):
+        return jax.ShapeDtypeStruct((parts, size, mode_len, 128), jnp.bfloat16)
+
+    def pair_grid(start):
         return pl.BlockSpec(
-            (PAIR, x_len, y_len, NZ), lambda at: (at + chunk * chunk_steps, 0, 0, 0)
+            (PAIR, x_len, y_len, NZ), lambda at: (at + start // PAIR, 0, 0, 0)
         )
 
     def tables_of(*arrays):
         return [whole_spec(array) for array in arrays]
 
-    def call(body, name, operands, specs, earlier, out_shapes, out_specs, scratch, flops, moved):
+    def call(
+        body, name, size, operands, specs, earlier, out_shapes, out_specs, scratch, flops, moved
+    ):
         aliases = {}
         if earlier is not None:
             aliases = {len(operands): 0}
@@ -389,17 +396,17 @@
         return pl.pallas_call(
             functools.partial(body, x_parts, y_parts),
             name=name,
-            grid=(chunk_steps,),
+            grid=(size // PAIR,),
             in_specs=specs,
             out_specs=out_specs,
             out_shape=out_shapes,
             scratch_shapes=scratch,
             input_output_aliases=aliases,
             compiler_params=params(),
-            cost_estimate=cost(flops, moved),
+            cost_estimate=cost(flops * size, moved * size),
         )(*operands)
 
-    def mix(name, received, spread, gather, kept):
+    def mix(name, received, spread, gather, kept, taken, given):
         adjoint = kept is not None
         steps = mode_len // step_len
         lanes = step_len * 2 * kx_len * share_len
@@ -421,26 +428,23 @@
         else:
             send_shape = (dp_len, steps, chan_len, lanes)
             send_spec = one_send
-        chunk_shape = (chunk_len, mode_len, 128)
+        whole = [spec_shape(size) for size in given]
         return pl.pallas_call(
-            functools.partial(mix_kernel, adjoint, mode_len, step_len),
+            functools.partial(mix_kernel, adjoint, mode_len, step_len, taken, given),
             name=name,
             grid=(steps,),
             in_specs=specs,
             out_specs=[send_spec]
-            + [pl.BlockSpec(chunk_shape, lambda at: (0, 0, 0)) for _ in range(CHUNKS)],
+            + tables_of(*whole),
             out_shape=[jax.ShapeDtypeStruct(send_shape, jnp.float32)]
-            + [jax.ShapeDtypeStruct(chunk_shape, jnp.bfloat16) for _ in range(CHUNKS)],
+            + whole,
             scratch_shapes=[pltpu.VMEM(small, jnp.float32), pltpu.VMEM(small, jnp.float32)],
             compiler_params=params(),
             cost_estimate=cost(mode_len * 2e8, spectral_weight.size * 4),
         )(*operands)
 
-    def exchange(partial_sums):
-        return lax.all_to_all(partial_sums, ("gx", "gy"), 0, 0, tiled=True)
-
-    def collect(spectrum):
-        return lax.all_gather(spectrum, ("gx", "gy"), axis=0, tiled=False)
+    def exchange(blocks):
+        return lax.all_to_all(blocks, ("gx", "gy"), 0, 0, tiled=True)
 
     share = jnp.asarray(share_table(step_len, kx_len, row_len, share_len))
     spread_in, spread_out = jnp.asarray(spread_input()), jnp.asarray(spread_output())
@@ -453,42 +457,48 @@
 
     received = []
     tables = (plane, forward_plain, shift_cos, shift_sin)
-    for chunk in range(CHUNKS):
+    for start, stop in spans(ANALYZE_CHUNKS):
         partial_u = call(
             analyze_kernel,
             "analyze_field",
+            stop - start,
             (field[0], *tables),
-            [pair_grid(chunk), *tables_of(*tables)],
+            [pair_grid(start), *tables_of(*tables)],
             None,
-            spec_shape,
+            spec_shape(stop - start),
             pair_spec,
             [],
             plane_flops,
             grid_bytes,
         )
         received.append(exchange(partial_u))
-    send_u, *spec_v = mix("mix_forward", received, spread_in, onto_out, None)
+    send_u, *spec_v = mix(
+        "mix_forward", received, spread_in, onto_out, None, ANALYZE_CHUNKS, ACTIVATE_CHUNKS
+    )
 
     received, out_grid = [], None
-    gathered = [collect(spectrum) for spectrum in spec_v]
+    gathered = [exchange(copies) for copies in spec_v]
     tables = (back, back_scaled, plane, forward_scaled, shift_cos, shift_sin)
-    for chunk in range(CHUNKS):
+    for chunk, (start, stop) in enumerate(spans(ACTIVATE_CHUNKS)):
         out_grid, partial_g = call(
             activate_kernel,
             "activate",
+            stop - start,
             (gathered[chunk], cotangent[0], *tables),
-            [pair_spec, pair_grid(chunk), *tables_of(*tables)],
+            [pair_spec, pair_grid(start), *tables_of(*tables)],
             out_grid,
-            [grid_shape, spec_shape],
-            [pair_grid(chunk), pair_spec],
+            [grid_shape, spec_shape(stop - start)],
+            [pair_grid(start), pair_spec],
             [pltpu.VMEM((x_len * y_len, PAIR * NZ), jnp.bfloat16)],
             4 * plane_flops,
             2 * grid_bytes,
         )
         received.append(exchange(partial_g))
-    send_terms, *spec_du = mix("mix_adjoint", received, spread_out, onto_in, send_u)
-
-    gathered = [collect(spectrum) for spectrum in spec_du]
+    send_terms, *spec_du = mix(
+        "mix_adjoint", received, spread_out, onto_in, send_u, ACTIVATE_CHUNKS, SYNTHESIZE_CHUNKS
+    )
+
+    gathered = [exchange(copies) for copies in spec_du]
     terms = lax.all_to_all(send_terms, "dp", 0, 0, tiled=True)
     lanes = terms.shape[-1]
     weight_grad = pl.pallas_call(
@@ -511,15 +521,16 @@
 
     grad_grid = None
     tables = (back, back_plain, shift_cos, shift_sin)
-    for chunk in range(CHUNKS):
+    for chunk, (start, stop) in enumerate(spans(SYNTHESIZE_CHUNKS)):
         grad_grid = call(
             synthesize_kernel,
             "synthesize_grad",
+            stop - start,
             (gathered[chunk], *tables),
             [pair_spec, *tables_of(*tables)],
             grad_grid,
             grid_shape,
-            pair_grid(chunk),
+            pair_grid(start),
             [],
             plane_flops,
             grid_bytes,

time: 335 us -> 279 us (0.83)
  blocking collectives: 174 us -> 84.3 us
  starting transfers between devices: 14.2 us -> 37.1 us
  Pallas kernels: 141 us -> 150 us
    all_gather x4 -> x0, blocking collectives: 138 us -> none  [collect(): return lax.all_gather(spectrum, ('gx', 'gy'), axis=0, tiled=False)]
    all_to_all x2 -> x6, blocking collectives: 36 us -> 84.3 us  [the longest x5 71.2 us: exchange(): return lax.all_to_all(blocks, ('gx', 'gy'), 0, 0, tiled=True)]
    all_to_all x3 -> x7, starting transfers between devices: 14.2 us -> 37.1 us  [exchange(): return lax.all_to_all(blocks, ('gx', 'gy'), 0, 0, tiled=True)]
    pallas_call x6 -> x9, Pallas kernels: 117 us -> 125 us  [call(): pl.pallas_call(functools.partial(body, x_parts, y_parts), name=name, grid...]
  transfers between devices with their start and end apart: 3 -> 7, of which waited for: 1 -> 2; matrix products, arithmetic and copies ran while one was open for 0% -> 0% of each run, Pallas kernels for 21% -> 42%
where the time goes in v3:
time: 279 us; the launch traced here: 277 us
  Pallas kernels  150 us (54%)
  blocking collectives  84.3 us (30%)
  starting transfers between devices  37.1 us (13%)
    pallas_call x9, Pallas kernels, call(): pl.pallas_call(functools.partial(body, x_parts, y_parts), name=name, grid...  125 us
    all_to_all x5, blocking collectives, exchange(): return lax.all_to_all(blocks, ('gx', 'gy'), 0, 0, tiled=True)  71.2 us
    all_to_all x7, starting transfers between devices, exchange(): return lax.all_to_all(blocks, ('gx', 'gy'), 0, 0, tiled=True)  37.1 us
    pallas_call x2, Pallas kernels, mix(): pl.pallas_call(functools.partial(mix_kernel, adjoint, mode_len, step_len,...  19.3 us
    all_to_all x1, blocking collectives, shards(): terms = lax.all_to_all(send_terms, 'dp', 0, 0, tiled=True)  13.1 us
    pallas_call x1, Pallas kernels, shards(): pl.pallas_call(weight_kernel, name='weight_terms', grid=(mode_len // step...  5.76 us
  transfers between devices with their start and end apart: 7, of which 2 were waited for; matrix products, arithmetic and copies ran while one was open for 0% of the time, Pallas kernels for 42%

profile of v3, /device:TPU:0, one launch (start us, length us, event | category | flops | bytes accessed | tf_op | source)
XLA Modules:
  0.0 277.0 jit_solution(7522340488548871308)
XLA Ops:
  0.6 1.3 dynamic-slice_bitcast_fusion
  1.9 7.7 %analyze_field.3 = bf16[8,8,16,128]{3,2,1,0:T(8,128)(2,1)} custom-call(bf16[32,64,32,128]{3,2,1,0:T(8,128)(2,1)} %bitcast.9, bf16[512,2048]{1,0:T(8,128)(2,1)} %constant.46.clone.plane_ref, bf16[64,256]{1,0:T(8,128)(2,1)} %constant.47.clone.depth_ref, f32[1,512]{1,0:T(1,128)} %get-tuple-element.32.cos_ref, f32[1,512]{1,0:T(1,128)} %get-tuple-element.31.sin_ref), custom_call_target="tpu_custom_call" | custom-call | flops 4294967296 | bytes 4194304 | tf_op jit(solution)/shard_map/analyze_field/pallas_call | solution.py:396
  9.7 7.3 %all-to-all-start = ((bf16[8,8,16,128]{3,2,1,0:T(8,128)(2,1)}), bf16[8,8,16,128]{3,2,1,0:T(8,128)(2,1)S(1)}, u32[]{:S(2)}, u32[]{:S(2)}) async-start(bf16[8,8,16,128]{3,2,1,0:T(8,128)(2,1)} %analyze_field.3), calls=%async_computation | async-start | bytes 524288 | tf_op jit(solution)/shard_map/all_to_all | solution.py:447
  16.9 10.3 %analyze_field.4 = bf16[8,12,16,128]{3,2,1,0:T(8,128)(2,1)} custom-call(bf16[32,64,32,128]{3,2,1,0:T(8,128)(2,1)} %bitcast.10, bf16[512,2048]{1,0:T(8,128)(2,1)} %constant.46.clone.plane_ref, bf16[64,256]{1,0:T(8,128)(2,1)} %constant.47.clone.depth_ref, f32[1,512]{1,0:T(1,128)} %get-tuple-element.32.cos_ref, f32[1,512]{1,0:T(1,128)} %get-tuple-element.31.sin_ref), custom_call_target="tpu_custom_call" | custom-call | flops 6442450944 | bytes 6291456 | tf_op jit(solution)/shard_map/analyze_field/pallas_call | solution.py:396
  27.3 0.0 all-to-all-done.refs_0_
  27.3 0.0 copy-start.6
  27.3 6.0 %all-to-all-start.1 = ((bf16[8,12,16,128]{3,2,1,0:T(8,128)(2,1)}), bf16[8,12,16,128]{3,2,1,0:T(8,128)(2,1)S(1)}, u32[]{:S(2)}, u32[]{:S(2)}) async-start(bf16[8,12,16,128]{3,2,1,0:T(8,128)(2,1)} %analyze_field.4), calls=%async_computation.1 | async-start | bytes 786432 | tf_op jit(solution)/shard_map/all_to_all | solution.py:447
  33.2 10.3 %analyze_field.5 = bf16[8,12,16,128]{3,2,1,0:T(8,128)(2,1)} custom-call(bf16[32,64,32,128]{3,2,1,0:T(8,128)(2,1)} %bitcast.11, bf16[512,2048]{1,0:T(8,128)(2,1)} %constant.46.clone.plane_ref, bf16[64,256]{1,0:T(8,128)(2,1)} %constant.47.clone.depth_ref, f32[1,512]{1,0:T(1,128)} %get-tuple-element.32.cos_ref, f32[1,512]{1,0:T(1,128)} %get-tuple-element.31.sin_ref), custom_call_target="tpu_custom_call" | custom-call | flops 6442450944 | bytes 6291456 | tf_op jit(solution)/shard_map/analyze_field/pallas_call | solution.py:396
  43.5 1.7 all-to-all-done.1.refs_1_
  45.3 0.0 copy-start.4
  45.3 15.8 %all_to_all.65.refs_2_ = bf16[8,12,16,128]{3,2,1,0:T(8,128)(2,1)} all-to-all(bf16[8,12,16,128]{3,2,1,0:T(8,128)(2,1)} %analyze_field.5), channel_id=1, replica_groups=mesh['dp'=4,'gx'=2,'gy'=4] {'gx','gy'}, dimensions={0} | all-to-all | bytes 786432 | tf_op jit(solution)/shard_map/all_to_all | solution.py:447
  61.1 0.0 copy-done.6
  61.1 0.0 copy-done.4
  61.1 8.8 %mix_forward.1 = (f32[4,4,32,128]{3,2,1,0:T(8,128)}, bf16[8,8,16,128]{3,2,1,0:T(8,128)(2,1)}, bf16[8,16,16,128]{3,2,1,0:T(8,128)(2,1)}, bf16[8,8,16,128]{3,2,1,0:T(8,128)(2,1)}) custom-call(bf16[8,8,16,128]{3,2,1,0:T(8,128)(2,1)} %copy-done.6, bf16[8,12,16,128]{3,2,1,0:T(8,128)(2,1)} %copy-done.4, bf16[8,12,16,128]{3,2,1,0:T(8,128)(2,1)} %all_to_all.65.refs_2_, ...), custom_call_target="tpu_custom_call" | custom-call | flops 3200000000 | bytes 8388608 | tf_op jit(solution)/shard_map/mix_forward/pallas_call | solution.py:432
  70.0 12.6 %all_to_all.66.spec_ref = bf16[8,8,16,128]{3,2,1,0:T(8,128)(2,1)} all-to-all(bf16[8,8,16,128]{3,2,1,0:T(8,128)(2,1)} %get-tuple-element.19), channel_id=1, replica_groups=mesh['dp'=4,'gx'=2,'gy'=4] {'gx','gy'}, dimensions={0} | all-to-all | bytes 524288 | tf_op jit(solution)/shard_map/all_to_all | solution.py:447
  82.6 3.5 %all-to-all-start.4 = ((bf16[8,16,16,128]{3,2,1,0:T(8,128)(2,1)}), bf16[8,16,16,128]{3,2,1,0:T(8,128)(2,1)S(1)}, u32[]{:S(2)}, u32[]{:S(2)}) async-start(bf16[8,16,16,128]{3,2,1,0:T(8,128)(2,1)} %get-tuple-element.18), calls=%async_computation.4 | async-start | bytes 1048576 | tf_op jit(solution)/shard_map/all_to_all | solution.py:447
  86.1 18.6 %activate.3 = (bf16[32,64,32,128]{3,2,1,0:T(8,128)(2,1)}, bf16[8,8,16,128]{3,2,1,0:T(8,128)(2,1)}) custom-call(bf16[8,8,16,128]{3,2,1,0:T(8,128)(2,1)} %all_to_all.66.spec_ref, bf16[32,64,32,128]{3,2,1,0:T(8,128)(2,1)} %bitcast.12, bf16[2048,512]{1,0:T(8,128)(2,1)} %constant.45.clone.back_ref, bf16[128,192]{1,0:T(8,128)(2,1)} %constant.49.clone.back_depth_ref, ...), custom_call_target="tpu_custom_call" | custom-call | flops 17179869184 | bytes 8388608 | tf_op jit(solution)/shard_map/activate/pallas_call | solution.py:396
  104.6 0.0 all-to-all-done.4.spec_ref
  104.7 0.0 copy-start.3
  104.7 5.9 %all-to-all-start.3 = ((bf16[8,8,16,128]{3,2,1,0:T(8,128)(2,1)}), bf16[8,8,16,128]{3,2,1,0:T(8,128)(2,1)S(1)}, u32[]{:S(2)}, u32[]{:S(2)}) async-start(bf16[8,8,16,128]{3,2,1,0:T(8,128)(2,1)} %get-tuple-element.17), calls=%async_computation.3 | async-start | bytes 524288 | tf_op jit(solution)/shard_map/all_to_all | solution.py:447
  110.6 0.0 copy-done.3
  110.6 34.1 %activate.4 = (bf16[32,64,32,128]{3,2,1,0:T(8,128)(2,1)}, bf16[8,16,16,128]{3,2,1,0:T(8,128)(2,1)}) custom-call(bf16[8,16,16,128]{3,2,1,0:T(8,128)(2,1)} %copy-done.3, bf16[32,64,32,128]{3,2,1,0:T(8,128)(2,1)} %bitcast.13, bf16[2048,512]{1,0:T(8,128)(2,1)} %constant.45.clone.back_ref, ...), custom_call_target="tpu_custom_call", output_to_operand_aliasing={{0}: (8, {})} | custom-call | flops 34359738368 | bytes 16777216 | tf_op jit(solution)/shard_map/activate/pallas_call | solution.py:396
  144.7 0.0 all-to-all-done.3.spec_ref
  144.7 0.0 copy-start.7
  144.7 6.0 %all-to-all-start.6 = ((bf16[8,8,16,128]{3,2,1,0:T(8,128)(2,1)}), bf16[8,8,16,128]{3,2,1,0:T(8,128)(2,1)S(1)}, u32[]{:S(2)}, u32[]{:S(2)}) async-start(bf16[8,8,16,128]{3,2,1,0:T(8,128)(2,1)} %get-tuple-element.23), calls=%async_computation.6 | async-start | bytes 524288 | tf_op jit(solution)/shard_map/all_to_all | solution.py:447
  150.7 0.0 copy-done.7
  150.7 0.0 copy-start.2
  150.7 18.7 %activate.5 = (bf16[32,64,32,128]{3,2,1,0:T(8,128)(2,1)}, bf16[8,8,16,128]{3,2,1,0:T(8,128)(2,1)}) custom-call(bf16[8,8,16,128]{3,2,1,0:T(8,128)(2,1)} %copy-done.7, bf16[32,64,32,128]{3,2,1,0:T(8,128)(2,1)} %bitcast.14, bf16[2048,512]{1,0:T(8,128)(2,1)} %constant.45.clone.back_ref, ...), custom_call_target="tpu_custom_call", output_to_operand_aliasing={{0}: (8, {})} | custom-call | flops 17179869184 | bytes 8388608 | tf_op jit(solution)/shard_map/activate/pallas_call | solution.py:396
  169.4 0.0 all-to-all-done.6.refs_0_
  169.5 0.0 copy-start.5
  169.5 14.7 %all_to_all.67.refs_2_ = bf16[8,8,16,128]{3,2,1,0:T(8,128)(2,1)} all-to-all(bf16[8,8,16,128]{3,2,1,0:T(8,128)(2,1)} %get-tuple-element.25), channel_id=1, replica_groups=mesh['dp'=4,'gx'=2,'gy'=4] {'gx','gy'}, dimensions={0} | all-to-all | bytes 524288 | tf_op jit(solution)/shard_map/all_to_all | solution.py:447
  184.2 0.0 copy-done.2
  184.2 14.3 %all_to_all.68.refs_1_ = bf16[8,16,16,128]{3,2,1,0:T(8,128)(2,1)} all-to-all(bf16[8,16,16,128]{3,2,1,0:T(8,128)(2,1)S(1)} %copy-done.2), channel_id=1, replica_groups=mesh['dp'=4,'gx'=2,'gy'=4] {'gx','gy'}, dimensions={0} | all-to-all | bytes 1048576 | tf_op jit(solution)/shard_map/all_to_all | solution.py:447
  198.4 0.0 copy-done.5
  198.4 10.5 %mix_adjoint.1 = (f32[4,4,2,32,128]{4,3,2,1,0:T(8,128)}, bf16[8,8,16,128]{3,2,1,0:T(8,128)(2,1)}, bf16[8,16,16,128]{3,2,1,0:T(8,128)(2,1)}, bf16[8,8,16,128]{3,2,1,0:T(8,128)(2,1)}) custom-call(bf16[8,8,16,128]{3,2,1,0:T(8,128)(2,1)} %copy-done.5, bf16[8,16,16,128]{3,2,1,0:T(8,128)(2,1)} %all_to_all.68.refs_1_, bf16[8,8,16,128]{3,2,1,0:T(8,128)(2,1)} %all_to_all.67.refs_2_, ...), custom_call_target="tpu_custom_call" | custom-call | flops 3200000000 | bytes 8388608 | tf_op jit(solution)/shard_map/mix_adjoint/pallas_call | solution.py:432
  208.9 13.1 %all_to_all.69.terms_ref = f32[4,4,2,32,128]{4,3,2,1,0:T(8,128)} all-to-all(f32[4,4,2,32,128]{4,3,2,1,0:T(8,128)} %get-tuple-element.30), channel_id=1, replica_groups=mesh['dp'=4,'gx'=2,'gy'=4] {'dp'}, dimensions={0} | all-to-all | bytes 1048576 | tf_op jit(solution)/shard_map/all_to_all | solution.py:502
  222.0 13.8 %all_to_all.70.spec_ref = bf16[8,8,16,128]{3,2,1,0:T(8,128)(2,1)} all-to-all(bf16[8,8,16,128]{3,2,1,0:T(8,128)(2,1)} %get-tuple-element.29), channel_id=1, replica_groups=mesh['dp'=4,'gx'=2,'gy'=4] {'gx','gy'}, dimensions={0} | all-to-all | bytes 524288 | tf_op jit(solution)/shard_map/all_to_all | solution.py:447
  235.8 3.5 %all-to-all-start.10 = ((bf16[8,16,16,128]{3,2,1,0:T(8,128)(2,1)}), bf16[8,16,16,128]{3,2,1,0:T(8,128)(2,1)S(1)}, u32[]{:S(2)}, u32[]{:S(2)}) async-start(bf16[8,16,16,128]{3,2,1,0:T(8,128)(2,1)} %get-tuple-element.28), calls=%async_computation.10 | async-start | bytes 1048576 | tf_op jit(solution)/shard_map/all_to_all | solution.py:447
  239.3 5.8 %weight_terms.1 = f32[4,16,4,2,1024]{4,3,2,1,0:T(2,128)} custom-call(f32[4,4,2,32,128]{4,3,2,1,0:T(8,128)} %all_to_all.69.terms_ref, bf16[64,1024]{1,0:T(8,128)(2,1)} %constant.54.clone.refs_4_.spread_u_ref, bf16[64,1024]{1,0:T(8,128)(2,1)} %constant.55.clone.refs_4_.spread_g_ref), custom_call_target="tpu_custom_call" | custom-call | flops 3200000000 | bytes 32000000 | tf_op jit(solution)/shard_map/weight_terms/pallas_call | solution.py:504
  245.0 7.0 %synthesize_grad.3.rest_0_ = bf16[32,64,32,128]{3,2,1,0:T(8,128)(2,1)} custom-call(bf16[8,8,16,128]{3,2,1,0:T(8,128)(2,1)} %all_to_all.70.spec_ref, bf16[2048,512]{1,0:T(8,128)(2,1)} %constant.45.clone.back_ref, bf16[128,192]{1,0:T(8,128)(2,1)} %constant.50.clone.depth_ref, f32[1,512]{1,0:T(1,128)} %get-tuple-element.32.cos_ref, ...), custom_call_target="tpu_custom_call" | custom-call | flops 4294967296 | bytes 4194304 | tf_op jit(solution)/shard_map/synthesize_grad/pallas_call | solution.py:396
  252.0 1.1 all-to-all-done.10.spec_ref
  253.1 0.0 copy-start
  253.1 4.9 %all-to-all-start.9 = ((bf16[8,8,16,128]{3,2,1,0:T(8,128)(2,1)}), bf16[8,8,16,128]{3,2,1,0:T(8,128)(2,1)S(1)}, u32[]{:S(2)}, u32[]{:S(2)}) async-start(bf16[8,8,16,128]{3,2,1,0:T(8,128)(2,1)} %get-tuple-element.27), calls=%async_computation.9 | async-start | bytes 524288 | tf_op jit(solution)/shard_map/all_to_all | solution.py:447
  257.9 0.0 copy-done
  257.9 11.4 %synthesize_grad.4.rest_0_ = bf16[32,64,32,128]{3,2,1,0:T(8,128)(2,1)} custom-call(bf16[8,16,16,128]{3,2,1,0:T(8,128)(2,1)} %copy-done, bf16[2048,512]{1,0:T(8,128)(2,1)} %constant.45.clone.back_ref, bf16[128,192]{1,0:T(8,128)(2,1)} %constant.50.clone.depth_ref, f32[1,512]{1,0:T(1,128)} %get-tuple-element.32.cos_ref, ...), custom_call_target="tpu_custom_call", output_to_operand_aliasing={{}: (5, {})} | custom-call | flops 8589934592 | bytes 8388608 | tf_op jit(solution)/shard_map/synthesize_grad/pallas_call | solution.py:396
  269.3 0.0 all-to-all-done.9.spec_ref
  269.3 0.0 copy-start.1
  269.3 0.7 copy-done.1
  270.0 7.0 %synthesize_grad.5 = bf16[32,64,32,128]{3,2,1,0:T(8,128)(2,1)} custom-call(bf16[8,8,16,128]{3,2,1,0:T(8,128)(2,1)} %copy-done.1, bf16[2048,512]{1,0:T(8,128)(2,1)} %constant.45.clone.back_ref, bf16[128,192]{1,0:T(8,128)(2,1)} %constant.50.clone.depth_ref, f32[1,512]{1,0:T(1,128)} %get-tuple-element.32.cos_ref, ...), custom_call_target="tpu_custom_call", output_to_operand_aliasing={{}: (5, {})} | custom-call | flops 4294967296 | bytes 4194304 | tf_op jit(solution)/shard_map/synthesize_grad/pallas_call | solution.py:396
Async XLA Ops:
  9.7 17.6 %all-to-all-start = ((bf16[8,8,16,128]{3,2,1,0:T(8,128)(2,1)}), bf16[8,8,16,128]{3,2,1,0:T(8,128)(2,1)S(1)}, u32[]{:S(2)}, u32[]{:S(2)}) async-start(bf16[8,8,16,128]{3,2,1,0:T(8,128)(2,1)} %analyze_field.3), calls=%async_computation | async-start | bytes 524288 | tf_op jit(solution)/shard_map/all_to_all | solution.py:447
  27.3 33.8 %copy-start.6 = (bf16[8,8,16,128]{3,2,1,0:T(8,128)(2,1)}, bf16[8,8,16,128]{3,2,1,0:T(8,128)(2,1)S(1)}, u32[]{:S(2)}) copy-start(bf16[8,8,16,128]{3,2,1,0:T(8,128)(2,1)S(1)} %all-to-all-done.refs_0_) | copy-start | bytes 786436
  27.3 18.0 %all-to-all-start.1 = ((bf16[8,12,16,128]{3,2,1,0:T(8,128)(2,1)}), bf16[8,12,16,128]{3,2,1,0:T(8,128)(2,1)S(1)}, u32[]{:S(2)}, u32[]{:S(2)}) async-start(bf16[8,12,16,128]{3,2,1,0:T(8,128)(2,1)} %analyze_field.4), calls=%async_computation.1 | async-start | bytes 786432 | tf_op jit(solution)/shard_map/all_to_all | solution.py:447
  45.3 15.9 %copy-start.4 = (bf16[8,12,16,128]{3,2,1,0:T(8,128)(2,1)}, bf16[8,12,16,128]{3,2,1,0:T(8,128)(2,1)S(1)}, u32[]{:S(2)}) copy-start(bf16[8,12,16,128]{3,2,1,0:T(8,128)(2,1)S(1)} %all-to-all-done.1.refs_1_) | copy-start | bytes 1179652
  82.6 22.1 %all-to-all-start.4 = ((bf16[8,16,16,128]{3,2,1,0:T(8,128)(2,1)}), bf16[8,16,16,128]{3,2,1,0:T(8,128)(2,1)S(1)}, u32[]{:S(2)}, u32[]{:S(2)}) async-start(bf16[8,16,16,128]{3,2,1,0:T(8,128)(2,1)} %get-tuple-element.18), calls=%async_computation.4 | async-start | bytes 1048576 | tf_op jit(solution)/shard_map/all_to_all | solution.py:447
  104.7 5.9 %copy-start.3 = (bf16[8,16,16,128]{3,2,1,0:T(8,128)(2,1)}, bf16[8,16,16,128]{3,2,1,0:T(8,128)(2,1)S(1)}, u32[]{:S(2)}) copy-start(bf16[8,16,16,128]{3,2,1,0:T(8,128)(2,1)S(1)} %all-to-all-done.4.spec_ref) | copy-start | bytes 1572868
  104.7 40.0 %all-to-all-start.3 = ((bf16[8,8,16,128]{3,2,1,0:T(8,128)(2,1)}), bf16[8,8,16,128]{3,2,1,0:T(8,128)(2,1)S(1)}, u32[]{:S(2)}, u32[]{:S(2)}) async-start(bf16[8,8,16,128]{3,2,1,0:T(8,128)(2,1)} %get-tuple-element.17), calls=%async_computation.3 | async-start | bytes 524288 | tf_op jit(solution)/shard_map/all_to_all | solution.py:447
  144.7 6.0 %copy-start.7 = (bf16[8,8,16,128]{3,2,1,0:T(8,128)(2,1)}, bf16[8,8,16,128]{3,2,1,0:T(8,128)(2,1)S(1)}, u32[]{:S(2)}) copy-start(bf16[8,8,16,128]{3,2,1,0:T(8,128)(2,1)S(1)} %all-to-all-done.3.spec_ref) | copy-start | bytes 786436
  144.7 24.7 %all-to-all-start.6 = ((bf16[8,8,16,128]{3,2,1,0:T(8,128)(2,1)}), bf16[8,8,16,128]{3,2,1,0:T(8,128)(2,1)S(1)}, u32[]{:S(2)}, u32[]{:S(2)}) async-start(bf16[8,8,16,128]{3,2,1,0:T(8,128)(2,1)} %get-tuple-element.23), calls=%async_computation.6 | async-start | bytes 524288 | tf_op jit(solution)/shard_map/all_to_all | solution.py:447
  150.7 33.5 %copy-start.2 = (bf16[8,16,16,128]{3,2,1,0:T(8,128)(2,1)S(1)}, bf16[8,16,16,128]{3,2,1,0:T(8,128)(2,1)}, u32[]{:S(2)}) copy-start(bf16[8,16,16,128]{3,2,1,0:T(8,128)(2,1)} %get-tuple-element.24) | copy-start | bytes 1572868
  169.5 29.0 %copy-start.5 = (bf16[8,8,16,128]{3,2,1,0:T(8,128)(2,1)}, bf16[8,8,16,128]{3,2,1,0:T(8,128)(2,1)S(1)}, u32[]{:S(2)}) copy-start(bf16[8,8,16,128]{3,2,1,0:T(8,128)(2,1)S(1)} %all-to-all-done.6.refs_0_) | copy-start | bytes 786436
  235.8 17.3 %all-to-all-start.10 = ((bf16[8,16,16,128]{3,2,1,0:T(8,128)(2,1)}), bf16[8,16,16,128]{3,2,1,0:T(8,128)(2,1)S(1)}, u32[]{:S(2)}, u32[]{:S(2)}) async-start(bf16[8,16,16,128]{3,2,1,0:T(8,128)(2,1)} %get-tuple-element.28), calls=%async_computation.10 | async-start | bytes 1048576 | tf_op jit(solution)/shard_map/all_to_all | solution.py:447
  253.1 4.9 %copy-start = (bf16[8,16,16,128]{3,2,1,0:T(8,128)(2,1)}, bf16[8,16,16,128]{3,2,1,0:T(8,128)(2,1)S(1)}, u32[]{:S(2)}) copy-start(bf16[8,16,16,128]{3,2,1,0:T(8,128)(2,1)S(1)} %all-to-all-done.10.spec_ref) | copy-start | bytes 1572868
  253.1 16.3 %all-to-all-start.9 = ((bf16[8,8,16,128]{3,2,1,0:T(8,128)(2,1)}), bf16[8,8,16,128]{3,2,1,0:T(8,128)(2,1)S(1)}, u32[]{:S(2)}, u32[]{:S(2)}) async-start(bf16[8,8,16,128]{3,2,1,0:T(8,128)(2,1)} %get-tuple-element.27), calls=%async_computation.9 | async-start | bytes 524288 | tf_op jit(solution)/shard_map/all_to_all | solution.py:447
  269.3 0.7 copy-start.1

commit v4 on v3

--- a/solution.py
+++ b/solution.py
@@ -19,13 +19,12 @@
 MZ = 32
 SAMPLES = 4
 PAIR = 2
-ANALYZE_CHUNKS = (8, 12, 12)
-ACTIVATE_CHUNKS = (8, 16, 8)
-SYNTHESIZE_CHUNKS = (8, 16, 8)
+ANALYZE_CHUNKS = (16, 16)
+ACTIVATE_CHUNKS = (16, 16)
+SYNTHESIZE_CHUNKS = (16, 16)
 PLANE_GAIN = 1.66526
 VMEM_BYTES = 56 * 1024 * 1024
 
-NT = (((1,), (1,)), ((), ()))
 NN = (((1,), (0,)), ((), ()))
 
 
@@ -89,8 +88,9 @@
 def analysis_table(scale_vec):
     angles = depth_angles()
     table = np.concatenate([np.cos(angles), np.sin(angles)]) * np.tile(scale_vec, 2)[:, None]
-    table = table.astype(np.float32).astype(ml_dtypes.bfloat16)
-    return np.concatenate([table, table], axis=1)
+    table = np.concatenate([table, table], axis=1).T
+    blocks = np.kron(np.eye(PAIR), table)
+    return blocks.astype(np.float32).astype(ml_dtypes.bfloat16)
 
 
 def synthesis_table(scale_vec):
@@ -133,10 +133,11 @@
     plane = f32_dot(plane_ref[...], grids)
     signs = part_signs(plane.shape[0])
     mode_len = MZ // x_parts
+    sides = [half for chan in range(PAIR) for half in halves(plane[:, chan * NZ : (chan + 1) * NZ])]
+    both = f32_dot(jnp.concatenate(sides, axis=1), depth_ref[...]).T
     for chan in range(PAIR):
-        high, low = halves(plane[:, chan * NZ : (chan + 1) * NZ])
-        both = f32_dot(depth_ref[...], jnp.concatenate([high, low], axis=1), NT)
-        spectrum = both[:MZ] + signs * swap_parts(both[MZ:])
+        top = 2 * MZ * chan
+        spectrum = both[top : top + MZ] + signs * swap_parts(both[top + MZ : top + 2 * MZ])
         spectrum = spectrum * cos_ref[...] + swap_parts(spectrum) * sin_ref[...]
         for gx in range(x_parts):
             for gy in range(y_parts):
@@ -160,9 +161,9 @@
         turned = -part_signs(spectrum.shape[1]) * swap_parts(spectrum)
         high, low = halves(jnp.concatenate([spectrum, turned], axis=0))
         fields.append(
-            f32_dot(depth_ref[...], jnp.concatenate([high, low, high], axis=0)).astype(jnp.bfloat16)
+            f32_dot(depth_ref[...], jnp.concatenate([high, low, high], axis=0)).T
         )
-    return jnp.concatenate(fields, axis=0)
+    return jnp.concatenate(fields, axis=1).astype(jnp.bfloat16)
 
 
 def gelu_parts(pre_act):
@@ -206,7 +207,7 @@
     step = min(8, x_len)
     for x_at in range(0, x_len, step):
         rows = slice(x_at * y_len, (x_at + step) * y_len)
-        pre_act = f32_dot(back_ref[rows], fields, NT)
+        pre_act = f32_dot(back_ref[rows], fields)
         for chan in range(PAIR):
             lanes = slice(chan * NZ, (chan + 1) * NZ)
             value, slope = gelu_parts(pre_act[:, lanes])
@@ -227,7 +228,7 @@
     step = min(8, x_len)
     for x_at in range(0, x_len, step):
         rows = slice(x_at * y_len, (x_at + step) * y_len)
-        grid = f32_dot(back_ref[rows], fields, NT)
+        grid = f32_dot(back_ref[rows], fields)
         for chan in range(PAIR):
             out_ref[chan, x_at : x_at + step] = (
                 grid[:, chan * NZ : (chan + 1) * NZ].astype(jnp.bfloat16).reshape(step, y_len, NZ)
@@ -248,7 +249,6 @@
 def mix_kernel(adjoint, mode_len, step_len, taken, given, *refs):
     recv_refs, refs = refs[: len(taken)], refs[len(taken) :]
     weight_ref, spread_ref, gather_ref, share_ref, *refs = refs
-    kept_ref, refs = (refs[0], refs[1:]) if adjoint else (None, refs)
     send_ref, *out_refs, taken_ref, mixed_ref = refs
     step_at = pl.program_id(0)
 
@@ -292,12 +292,7 @@
     shared = shared[:CHANNELS] + shared[CHANNELS:]
     lanes = send_ref.shape[-1]
     for rank in range(send_ref.shape[0]):
-        part = shared[:, rank * lanes : (rank + 1) * lanes]
-        if adjoint:
-            send_ref[rank, 0, 0] = kept_ref[rank, 0]
-            send_ref[rank, 0, 1] = part
-        else:
-            send_ref[rank, 0] = part
+        send_ref[rank, 0] = shared[:, rank * lanes : (rank + 1) * lanes]
 
     @pl.when(step_at == pl.num_programs(0) - 1)
     def _():
@@ -308,14 +303,14 @@
                 out_ref[target] = part
 
 
-def weight_kernel(terms_ref, spread_u_ref, spread_g_ref, out_ref):
+def weight_kernel(rank_ref, u_ref, g_ref, spread_u_ref, spread_g_ref, out_ref):
     kx_len, step_len, row_len = out_ref.shape[:3]
     half = kx_len * row_len
     real_part, imag_part = 0.0, 0.0
-    for sample in range(terms_ref.shape[0]):
+    for sample in range(u_ref.shape[0]):
         shape = (step_len, 2, half, CHANNELS * CHANNELS)
-        spread_u = mode_rows(terms_ref[sample, 0, 0], spread_u_ref).reshape(shape)
-        spread_g = mode_rows(terms_ref[sample, 0, 1], spread_g_ref).reshape(shape)
+        spread_u = mode_rows(u_ref[sample, 0, 0], spread_u_ref).reshape(shape)
+        spread_g = mode_rows(g_ref[sample, 0, 0], spread_g_ref).reshape(shape)
         u_real, u_imag = spread_u[:, 0], spread_u[:, 1]
         g_real, g_imag = spread_g[:, 0], spread_g[:, 1]
         real_part = real_part + (u_real * g_real + u_imag * g_imag)
@@ -406,8 +401,7 @@
             cost_estimate=cost(flops * size, moved * size),
         )(*operands)
 
-    def mix(name, received, spread, gather, kept, taken, given):
-        adjoint = kept is not None
+    def mix(name, received, spread, gather, adjoint, taken, given):
         steps = mode_len // step_len
         lanes = step_len * 2 * kx_len * share_len
         small = (chan_len * mode_len, 128)
@@ -419,15 +413,8 @@
             ),
             *tables_of(spread, gather, share),
         ]
-        one_send = pl.BlockSpec((dp_len, 1, chan_len, lanes), lambda at: (0, at, 0, 0))
-        if adjoint:
-            operands.append(kept)
-            specs.append(one_send)
-            send_shape = (dp_len, steps, 2, chan_len, lanes)
-            send_spec = pl.BlockSpec((dp_len, 1, 2, chan_len, lanes), lambda at: (0, at, 0, 0, 0))
-        else:
-            send_shape = (dp_len, steps, chan_len, lanes)
-            send_spec = one_send
+        send_shape = (dp_len, steps, chan_len, lanes)
+        send_spec = pl.BlockSpec((dp_len, 1, chan_len, lanes), lambda at: (0, at, 0, 0))
         whole = [spec_shape(size) for size in given]
         return pl.pallas_call(
             functools.partial(mix_kernel, adjoint, mode_len, step_len, taken, given),
@@ -473,9 +460,10 @@
         )
         received.append(exchange(partial_u))
     send_u, *spec_v = mix(
-        "mix_forward", received, spread_in, onto_out, None, ANALYZE_CHUNKS, ACTIVATE_CHUNKS
-    )
-
+        "mix_forward", received, spread_in, onto_out, False, ANALYZE_CHUNKS, ACTIVATE_CHUNKS
+    )
+
+    all_u = lax.all_gather(send_u, "dp", axis=0, tiled=False)
     received, out_grid = [], None
     gathered = [exchange(copies) for copies in spec_v]
     tables = (back, back_scaled, plane, forward_scaled, shift_cos, shift_sin)
@@ -494,30 +482,34 @@
             2 * grid_bytes,
         )
         received.append(exchange(partial_g))
-    send_terms, *spec_du = mix(
-        "mix_adjoint", received, spread_out, onto_in, send_u, ACTIVATE_CHUNKS, SYNTHESIZE_CHUNKS
+    send_g, *spec_du = mix(
+        "mix_adjoint", received, spread_out, onto_in, True, ACTIVATE_CHUNKS, SYNTHESIZE_CHUNKS
     )
 
     gathered = [exchange(copies) for copies in spec_du]
-    terms = lax.all_to_all(send_terms, "dp", 0, 0, tiled=True)
-    lanes = terms.shape[-1]
+    all_g = lax.all_gather(send_g, "dp", axis=0, tiled=False)
+    lanes = all_g.shape[-1]
+    terms_spec = pl.BlockSpec(
+        (dp_len, 1, 1, chan_len, lanes), lambda at, rank: (0, rank[0], at, 0, 0)
+    )
     weight_grad = pl.pallas_call(
         weight_kernel,
         name="weight_terms",
-        grid=(mode_len // step_len,),
-        in_specs=[
-            pl.BlockSpec((dp_len, 1, 2, chan_len, lanes), lambda at: (0, at, 0, 0, 0)),
-            *tables_of(spread_in, spread_out),
-        ],
-        out_specs=pl.BlockSpec(
-            (kx_len, step_len, share_len, 2, chan_len * chan_len), lambda at: (0, at, 0, 0, 0)
+        grid_spec=pltpu.PrefetchScalarGridSpec(
+            num_scalar_prefetch=1,
+            grid=(mode_len // step_len,),
+            in_specs=[terms_spec, terms_spec, *tables_of(spread_in, spread_out)],
+            out_specs=pl.BlockSpec(
+                (kx_len, step_len, share_len, 2, chan_len * chan_len),
+                lambda at, rank: (0, at, 0, 0, 0),
+            ),
         ),
         out_shape=jax.ShapeDtypeStruct(
             (kx_len, mode_len, share_len, 2, chan_len * chan_len), jnp.float32
         ),
         compiler_params=params(),
         cost_estimate=cost(mode_len * 2e8, mode_len * 2e6),
-    )(terms, spread_in, spread_out)
+    )(lax.axis_index("dp").astype(jnp.int32).reshape(1), all_u, all_g, spread_in, spread_out)
 
     grad_grid = None
     tables = (back, back_plain, shift_cos, shift_sin)

time: 279 us -> 257 us (0.921)
  blocking collectives: 84.3 us -> 51.4 us
  between operations: 0.73 us -> 14.1 us
  waiting for transfers between devices: 2.77 us -> 13.7 us
  starting transfers between devices: 37.1 us -> 26.5 us
  Pallas kernels: 150 us -> 147 us
    all_to_all x5 -> x3, blocking collectives: 71.2 us -> 51.4 us  [exchange(): return lax.all_to_all(blocks, ('gx', 'gy'), 0, 0, tiled=True)]
    all_to_all x1 -> x0, blocking collectives: 13.1 us -> none  [shards(): terms = lax.all_to_all(send_terms, 'dp', 0, 0, tiled=True)]
    all_to_all x7 -> x5, starting transfers between devices: 37.1 us -> 26.2 us  [exchange(): return lax.all_to_all(blocks, ('gx', 'gy'), 0, 0, tiled=True)]
    all_to_all x7 -> x5, waiting for transfers between devices: 2.77 us -> 12.6 us  [exchange(): return lax.all_to_all(blocks, ('gx', 'gy'), 0, 0, tiled=True)]
    pallas_call x9 -> x6, Pallas kernels: 125 us -> 122 us  [call(): pl.pallas_call(functools.partial(body, x_parts, y_parts), name=name, grid...]
  transfers between devices with their start and end apart: 7 -> 7, of which waited for: 2 -> 2; matrix products, arithmetic and copies ran while one was open for 0% -> 0% of each run, Pallas kernels for 42% -> 46%
where the time goes in v4:
time: 257 us; the launch traced here: 255 us
  Pallas kernels  147 us (57%)
  blocking collectives  51.4 us (20%)
  starting transfers between devices  26.5 us (10%)
  between operations  14.1 us (5%)
  waiting for transfers between devices  13.7 us (5%)
  local copies, waits for them, and re-layouts  2.9 us (1%)
    pallas_call x6, Pallas kernels, call(): pl.pallas_call(functools.partial(body, x_parts, y_parts), name=name, grid...  122 us
    all_to_all x3, blocking collectives, exchange(): return lax.all_to_all(blocks, ('gx', 'gy'), 0, 0, tiled=True)  51.4 us
    all_to_all x5, starting transfers between devices, exchange(): return lax.all_to_all(blocks, ('gx', 'gy'), 0, 0, tiled=True)  26.2 us
    pallas_call x2, Pallas kernels, mix(): pl.pallas_call(functools.partial(mix_kernel, adjoint, mode_len, step_len,...  19.2 us
    all_to_all x5, waiting for transfers between devices, exchange(): return lax.all_to_all(blocks, ('gx', 'gy'), 0, 0, tiled=True)  12.6 us
    pallas_call x1, Pallas kernels, shards(): pl.pallas_call(weight_kernel, name='weight_terms', grid_spec=pltpu.Prefet...  5.75 us
  transfers between devices with their start and end apart: 7, of which 2 were waited for; matrix products, arithmetic and copies ran while one was open for 0% of the time, Pallas kernels for 46%

profile of v4, /device:TPU:0, one launch (start us, length us, event | category | flops | bytes accessed | tf_op | source)
XLA Modules:
  0.0 255.4 jit_solution(14605080994580693214)
XLA Ops:
  7.2 1.3 dynamic-slice_bitcast_fusion
  8.5 13.6 %analyze_field.2 = bf16[8,16,16,128]{3,2,1,0:T(8,128)(2,1)} custom-call(bf16[32,64,32,128]{3,2,1,0:T(8,128)(2,1)} %bitcast.12, bf16[512,2048]{1,0:T(8,128)(2,1)} %constant.49.clone.plane_ref, bf16[512,128]{1,0:T(8,128)(2,1)} %constant.50.clone.depth_ref, f32[1,512]{1,0:T(1,128)} %get-tuple-element.24.cos_ref, f32[1,512]{1,0:T(1,128)} %get-tuple-element.23.sin_ref), custom_call_target="tpu_custom_call" | custom-call | flops 8589934592 | bytes 8388608 | tf_op jit(solution)/shard_map/analyze_field/pallas_call | solution.py:391
  22.0 7.3 %all-to-all-start = ((bf16[8,16,16,128]{3,2,1,0:T(8,128)(2,1)}), bf16[8,16,16,128]{3,2,1,0:T(8,128)(2,1)S(1)}, u32[]{:S(2)}, u32[]{:S(2)}) async-start(bf16[8,16,16,128]{3,2,1,0:T(8,128)(2,1)} %analyze_field.2), calls=%async_computation | async-start | bytes 1048576 | tf_op jit(solution)/shard_map/all_to_all | solution.py:434
  29.3 13.6 %analyze_field.3 = bf16[8,16,16,128]{3,2,1,0:T(8,128)(2,1)} custom-call(bf16[32,64,32,128]{3,2,1,0:T(8,128)(2,1)} %bitcast.13, bf16[512,2048]{1,0:T(8,128)(2,1)} %constant.49.clone.plane_ref, bf16[512,128]{1,0:T(8,128)(2,1)} %constant.50.clone.depth_ref, f32[1,512]{1,0:T(1,128)} %get-tuple-element.24.cos_ref, f32[1,512]{1,0:T(1,128)} %get-tuple-element.23.sin_ref), custom_call_target="tpu_custom_call" | custom-call | flops 8589934592 | bytes 8388608 | tf_op jit(solution)/shard_map/analyze_field/pallas_call | solution.py:391
  42.9 1.8 all-to-all-done.refs_0_
  44.7 0.0 copy-start.4
  44.7 19.1 %all_to_all.40.refs_1_ = bf16[8,16,16,128]{3,2,1,0:T(8,128)(2,1)} all-to-all(bf16[8,16,16,128]{3,2,1,0:T(8,128)(2,1)} %analyze_field.3), channel_id=1, replica_groups=mesh['dp'=4,'gx'=2,'gy'=4] {'gx','gy'}, dimensions={0} | all-to-all | bytes 1048576 | tf_op jit(solution)/shard_map/all_to_all | solution.py:434
  63.8 0.0 copy-done.4
  63.8 8.9 %mix_forward.1 = (f32[4,4,32,128]{3,2,1,0:T(8,128)}, bf16[8,16,16,128]{3,2,1,0:T(8,128)(2,1)}, bf16[8,16,16,128]{3,2,1,0:T(8,128)(2,1)}) custom-call(bf16[8,16,16,128]{3,2,1,0:T(8,128)(2,1)} %copy-done.4, bf16[8,16,16,128]{3,2,1,0:T(8,128)(2,1)} %all_to_all.40.refs_1_, f32[4,16,16,2,1024]{4,3,2,1,0:T(2,128)} %refs_2_.3, ...), custom_call_target="tpu_custom_call" | custom-call | flops 3200000000 | bytes 8388608 | tf_op jit(solution)/shard_map/mix_forward/pallas_call | solution.py:419
  72.7 17.0 %all_to_all.41.spec_ref = bf16[8,16,16,128]{3,2,1,0:T(8,128)(2,1)} all-to-all(bf16[8,16,16,128]{3,2,1,0:T(8,128)(2,1)} %get-tuple-element.14), channel_id=1, replica_groups=mesh['dp'=4,'gx'=2,'gy'=4] {'gx','gy'}, dimensions={0} | all-to-all | bytes 1048576 | tf_op jit(solution)/shard_map/all_to_all | solution.py:434
  89.7 3.5 %all-to-all-start.2 = ((bf16[8,16,16,128]{3,2,1,0:T(8,128)(2,1)}), bf16[8,16,16,128]{3,2,1,0:T(8,128)(2,1)S(1)}, u32[]{:S(2)}, u32[]{:S(2)}) async-start(bf16[8,16,16,128]{3,2,1,0:T(8,128)(2,1)} %get-tuple-element.13), calls=%async_computation.2 | async-start | bytes 1048576 | tf_op jit(solution)/shard_map/all_to_all | solution.py:434
  93.2 35.2 %activate.2 = (bf16[32,64,32,128]{3,2,1,0:T(8,128)(2,1)}, bf16[8,16,16,128]{3,2,1,0:T(8,128)(2,1)}) custom-call(bf16[8,16,16,128]{3,2,1,0:T(8,128)(2,1)} %all_to_all.41.spec_ref, bf16[32,64,32,128]{3,2,1,0:T(8,128)(2,1)} %bitcast.14, bf16[2048,512]{1,0:T(8,128)(2,1)} %constant.48.clone.back_ref, bf16[128,192]{1,0:T(8,128)(2,1)} %constant.52.clone.back_depth_ref, ...), custom_call_target="tpu_custom_call" | custom-call | flops 34359738368 | bytes 16777216 | tf_op jit(solution)/shard_map/activate/pallas_call | solution.py:391
  128.4 0.0 all-to-all-done.2.spec_ref
  128.4 0.0 copy-start.3
  128.4 5.9 %all-to-all-start.4 = ((bf16[8,16,16,128]{3,2,1,0:T(8,128)(2,1)}), bf16[8,16,16,128]{3,2,1,0:T(8,128)(2,1)S(1)}, u32[]{:S(2)}, u32[]{:S(2)}) async-start(bf16[8,16,16,128]{3,2,1,0:T(8,128)(2,1)} %get-tuple-element.17), calls=%async_computation.4 | async-start | bytes 1048576 | tf_op jit(solution)/shard_map/all_to_all | solution.py:434
  134.3 0.0 copy-done.3
  134.3 35.3 %activate.3 = (bf16[32,64,32,128]{3,2,1,0:T(8,128)(2,1)}, bf16[8,16,16,128]{3,2,1,0:T(8,128)(2,1)}) custom-call(bf16[8,16,16,128]{3,2,1,0:T(8,128)(2,1)} %copy-done.3, bf16[32,64,32,128]{3,2,1,0:T(8,128)(2,1)} %bitcast.15, bf16[2048,512]{1,0:T(8,128)(2,1)} %constant.48.clone.back_ref, ...), custom_call_target="tpu_custom_call", output_to_operand_aliasing={{0}: (8, {})} | custom-call | flops 34359738368 | bytes 16777216 | tf_op jit(solution)/shard_map/activate/pallas_call | solution.py:391
  169.7 0.0 all-to-all-done.4.refs_0_
  169.7 0.0 copy-start.1
  169.7 6.0 %all-to-all-start.5 = ((bf16[8,16,16,128]{3,2,1,0:T(8,128)(2,1)}), bf16[8,16,16,128]{3,2,1,0:T(8,128)(2,1)S(1)}, u32[]{:S(2)}, u32[]{:S(2)}) async-start(bf16[8,16,16,128]{3,2,1,0:T(8,128)(2,1)} %get-tuple-element.18), calls=%async_computation.5 | async-start | bytes 1048576 | tf_op jit(solution)/shard_map/all_to_all | solution.py:434
  175.7 0.2 all-gather.5.cloned.1.call-start
  175.9 0.5 all-gather.5.cloned.1.call-update
  176.4 10.7 %all-to-all-done.5.refs_1_ = bf16[8,16,16,128]{3,2,1,0:T(8,128)(2,1)S(1)} async-done(((bf16[8,16,16,128]{3,2,1,0:T(8,128)(2,1)}), bf16[8,16,16,128]{3,2,1,0:T(8,128)(2,1)S(1)}, u32[]{:S(2)}, u32[]{:S(2)}) %all-to-all-start.5) | async-done | bytes 524320 | tf_op jit(solution)/shard_map/all_to_all | solution.py:434
  187.2 0.0 copy-done.1
  187.2 0.0 copy-start.2
  187.2 0.8 copy-done.2
  187.9 10.4 %mix_adjoint.1 = (f32[4,4,32,128]{3,2,1,0:T(8,128)}, bf16[8,16,16,128]{3,2,1,0:T(8,128)(2,1)}, bf16[8,16,16,128]{3,2,1,0:T(8,128)(2,1)}) custom-call(bf16[8,16,16,128]{3,2,1,0:T(8,128)(2,1)} %copy-done.1, bf16[8,16,16,128]{3,2,1,0:T(8,128)(2,1)} %copy-done.2, f32[4,16,16,2,1024]{4,3,2,1,0:T(2,128)} %refs_2_.3, ...), custom_call_target="tpu_custom_call" | custom-call | flops 3200000000 | bytes 8388608 | tf_op jit(solution)/shard_map/mix_adjoint/pallas_call | solution.py:419
  198.3 15.3 %all_to_all.42.spec_ref = bf16[8,16,16,128]{3,2,1,0:T(8,128)(2,1)} all-to-all(bf16[8,16,16,128]{3,2,1,0:T(8,128)(2,1)} %get-tuple-element.20), channel_id=1, replica_groups=mesh['dp'=4,'gx'=2,'gy'=4] {'gx','gy'}, dimensions={0} | all-to-all | bytes 1048576 | tf_op jit(solution)/shard_map/all_to_all | solution.py:434
  213.6 3.5 %all-to-all-start.6 = ((bf16[8,16,16,128]{3,2,1,0:T(8,128)(2,1)}), bf16[8,16,16,128]{3,2,1,0:T(8,128)(2,1)S(1)}, u32[]{:S(2)}, u32[]{:S(2)}) async-start(bf16[8,16,16,128]{3,2,1,0:T(8,128)(2,1)} %get-tuple-element.19), calls=%async_computation.6 | async-start | bytes 1048576 | tf_op jit(solution)/shard_map/all_to_all | solution.py:434
  217.1 0.0 all-gather.7.cloned.1.call-start
  217.2 0.7 all-gather.7.cloned.1.call-update
  217.9 12.1 %synthesize_grad.2.rest_0_ = bf16[32,64,32,128]{3,2,1,0:T(8,128)(2,1)} custom-call(bf16[8,16,16,128]{3,2,1,0:T(8,128)(2,1)} %all_to_all.42.spec_ref, bf16[2048,512]{1,0:T(8,128)(2,1)} %constant.48.clone.back_ref, bf16[128,192]{1,0:T(8,128)(2,1)} %constant.53.clone.depth_ref, f32[1,512]{1,0:T(1,128)} %get-tuple-element.24.cos_ref, ...), custom_call_target="tpu_custom_call" | custom-call | flops 8589934592 | bytes 8388608 | tf_op jit(solution)/shard_map/synthesize_grad/pallas_call | solution.py:391
  229.9 0.0 all-to-all-done.6.spec_ref
  229.9 0.0 copy-start
  230.0 0.8 copy-done
  230.7 12.0 %synthesize_grad.3 = bf16[32,64,32,128]{3,2,1,0:T(8,128)(2,1)} custom-call(bf16[8,16,16,128]{3,2,1,0:T(8,128)(2,1)} %copy-done, bf16[2048,512]{1,0:T(8,128)(2,1)} %constant.48.clone.back_ref, bf16[128,192]{1,0:T(8,128)(2,1)} %constant.53.clone.depth_ref, f32[1,512]{1,0:T(1,128)} %get-tuple-element.24.cos_ref, ...), custom_call_target="tpu_custom_call", output_to_operand_aliasing={{}: (5, {})} | custom-call | flops 8589934592 | bytes 8388608 | tf_op jit(solution)/shard_map/synthesize_grad/pallas_call | solution.py:391
  242.8 0.0 all-gather.5.cloned.1.call-done
  242.8 0.0 all-gather.7.cloned.1.call-done
  242.8 5.8 %weight_terms.1 = f32[4,16,4,2,1024]{4,3,2,1,0:T(2,128)} custom-call(s32[1]{0:T(128)} %bitcast.6.rank_ref, f32[4,4,4,32,128]{4,3,2,1,0:T(8,128)} %bitcast.16, f32[4,4,4,32,128]{4,3,2,1,0:T(8,128)} %bitcast.17, bf16[64,1024]{1,0:T(8,128)(2,1)} %constant.57.clone.refs_3_.spread_u_ref, bf16[64,1024]{1,0:T(8,128)(2,1)} %constant.58.clone.refs_3_.spread_g_ref), custom_call_target="tpu_custom_call" | custom-call | flops 3200000000 | bytes 32000000 | tf_op jit(solution)/shard_map/weight_terms/pallas_call | solution.py:495
Async XLA Ops:
  22.0 22.7 %all-to-all-start = ((bf16[8,16,16,128]{3,2,1,0:T(8,128)(2,1)}), bf16[8,16,16,128]{3,2,1,0:T(8,128)(2,1)S(1)}, u32[]{:S(2)}, u32[]{:S(2)}) async-start(bf16[8,16,16,128]{3,2,1,0:T(8,128)(2,1)} %analyze_field.2), calls=%async_computation | async-start | bytes 1048576 | tf_op jit(solution)/shard_map/all_to_all | solution.py:434
  44.7 19.1 %copy-start.4 = (bf16[8,16,16,128]{3,2,1,0:T(8,128)(2,1)}, bf16[8,16,16,128]{3,2,1,0:T(8,128)(2,1)S(1)}, u32[]{:S(2)}) copy-start(bf16[8,16,16,128]{3,2,1,0:T(8,128)(2,1)S(1)} %all-to-all-done.refs_0_) | copy-start | bytes 1572868
  89.7 38.7 %all-to-all-start.2 = ((bf16[8,16,16,128]{3,2,1,0:T(8,128)(2,1)}), bf16[8,16,16,128]{3,2,1,0:T(8,128)(2,1)S(1)}, u32[]{:S(2)}, u32[]{:S(2)}) async-start(bf16[8,16,16,128]{3,2,1,0:T(8,128)(2,1)} %get-tuple-element.13), calls=%async_computation.2 | async-start | bytes 1048576 | tf_op jit(solution)/shard_map/all_to_all | solution.py:434
  128.4 6.0 %copy-start.3 = (bf16[8,16,16,128]{3,2,1,0:T(8,128)(2,1)}, bf16[8,16,16,128]{3,2,1,0:T(8,128)(2,1)S(1)}, u32[]{:S(2)}) copy-start(bf16[8,16,16,128]{3,2,1,0:T(8,128)(2,1)S(1)} %all-to-all-done.2.spec_ref) | copy-start | bytes 1572868
  128.4 41.3 %all-to-all-start.4 = ((bf16[8,16,16,128]{3,2,1,0:T(8,128)(2,1)}), bf16[8,16,16,128]{3,2,1,0:T(8,128)(2,1)S(1)}, u32[]{:S(2)}, u32[]{:S(2)}) async-start(bf16[8,16,16,128]{3,2,1,0:T(8,128)(2,1)} %get-tuple-element.17), calls=%async_computation.4 | async-start | bytes 1048576 | tf_op jit(solution)/shard_map/all_to_all | solution.py:434
  169.7 17.5 %copy-start.1 = (bf16[8,16,16,128]{3,2,1,0:T(8,128)(2,1)}, bf16[8,16,16,128]{3,2,1,0:T(8,128)(2,1)S(1)}, u32[]{:S(2)}) copy-start(bf16[8,16,16,128]{3,2,1,0:T(8,128)(2,1)S(1)} %all-to-all-done.4.refs_0_) | copy-start | bytes 1572868
  169.7 17.5 %all-to-all-start.5 = ((bf16[8,16,16,128]{3,2,1,0:T(8,128)(2,1)}), bf16[8,16,16,128]{3,2,1,0:T(8,128)(2,1)S(1)}, u32[]{:S(2)}, u32[]{:S(2)}) async-start(bf16[8,16,16,128]{3,2,1,0:T(8,128)(2,1)} %get-tuple-element.18), calls=%async_computation.5 | async-start | bytes 1048576 | tf_op jit(solution)/shard_map/all_to_all | solution.py:434
  175.7 67.1 %all-gather.5.cloned.1.call-start = ((), (), s32[]{:S(2)}) async-start(), calls=%async_computation.8 | async-start | bytes 1310720 | tf_op jit(solution)/shard_map/all_gather | solution.py:466
  187.2 0.8 copy-start.2
  213.6 16.3 %all-to-all-start.6 = ((bf16[8,16,16,128]{3,2,1,0:T(8,128)(2,1)}), bf16[8,16,16,128]{3,2,1,0:T(8,128)(2,1)S(1)}, u32[]{:S(2)}, u32[]{:S(2)}) async-start(bf16[8,16,16,128]{3,2,1,0:T(8,128)(2,1)} %get-tuple-element.19), calls=%async_computation.6 | async-start | bytes 1048576 | tf_op jit(solution)/shard_map/all_to_all | solution.py:434
  217.1 25.6 %all-gather.7.cloned.1.call-start = ((), (), s32[]{:S(2)}) async-start(), calls=%async_computation.9 | async-start | bytes 1310720 | tf_op jit(solution)/shard_map/all_gather | solution.py:490
  229.9 0.8 copy-start
Sparse Core Ops, SparseCore 0:
  178.1 18.1 all-gather.4
  219.5 18.1 all-gather.6

commit v5 on v4

--- a/solution.py
+++ b/solution.py
@@ -26,6 +26,7 @@
 VMEM_BYTES = 56 * 1024 * 1024
 
 NN = (((1,), (0,)), ((), ()))
+NT = (((1,), (1,)), ((), ()))
 
 
 def f32_dot(left_op, right_op, dims=NN):
@@ -88,9 +89,8 @@
 def analysis_table(scale_vec):
     angles = depth_angles()
     table = np.concatenate([np.cos(angles), np.sin(angles)]) * np.tile(scale_vec, 2)[:, None]
-    table = np.concatenate([table, table], axis=1).T
-    blocks = np.kron(np.eye(PAIR), table)
-    return blocks.astype(np.float32).astype(ml_dtypes.bfloat16)
+    table = table.astype(np.float32).astype(ml_dtypes.bfloat16)
+    return np.concatenate([table, table], axis=1)
 
 
 def synthesis_table(scale_vec):
@@ -129,26 +129,24 @@
     return jnp.where(lane_ids % 128 < 64, 1.0, -1.0).astype(jnp.float32)
 
 
-def analyze_pair(grids, plane_ref, depth_ref, cos_ref, sin_ref, out_ref, x_parts, y_parts):
-    plane = f32_dot(plane_ref[...], grids)
+def finish_pair(plane, depth_ref, cos_ref, sin_ref, out_ref, first, x_parts, y_parts):
     signs = part_signs(plane.shape[0])
     mode_len = MZ // x_parts
-    sides = [half for chan in range(PAIR) for half in halves(plane[:, chan * NZ : (chan + 1) * NZ])]
-    both = f32_dot(jnp.concatenate(sides, axis=1), depth_ref[...]).T
     for chan in range(PAIR):
-        top = 2 * MZ * chan
-        spectrum = both[top : top + MZ] + signs * swap_parts(both[top + MZ : top + 2 * MZ])
+        sides = jnp.concatenate(halves(plane[:, chan * NZ : (chan + 1) * NZ]), axis=1)
+        both = f32_dot(depth_ref[...], sides, NT)
+        spectrum = both[:MZ] + signs * swap_parts(both[MZ:])
         spectrum = spectrum * cos_ref[...] + swap_parts(spectrum) * sin_ref[...]
         for gx in range(x_parts):
             for gy in range(y_parts):
-                out_ref[gx * y_parts + gy, chan] = spectrum[
+                out_ref[gx * y_parts + gy, first + chan] = spectrum[
                     gx * mode_len : (gx + 1) * mode_len, gy * 128 : (gy + 1) * 128
                 ].astype(jnp.bfloat16)
 
 
-def depth_fields(spec_ref, depth_ref, cos_ref, sin_ref, x_parts, y_parts):
+def depth_fields(spec_ref, depth_ref, cos_ref, sin_ref, x_parts, y_parts, first=0):
     fields = []
-    for chan in range(PAIR):
+    for chan in range(first, first + PAIR):
         rows = [
             jnp.concatenate(
                 [spec_ref[gx * y_parts + gy, chan].astype(jnp.float32) for gy in range(y_parts)],
@@ -161,9 +159,9 @@
         turned = -part_signs(spectrum.shape[1]) * swap_parts(spectrum)
         high, low = halves(jnp.concatenate([spectrum, turned], axis=0))
         fields.append(
-            f32_dot(depth_ref[...], jnp.concatenate([high, low, high], axis=0)).T
+            f32_dot(depth_ref[...], jnp.concatenate([high, low, high], axis=0)).astype(jnp.bfloat16)
         )
-    return jnp.concatenate(fields, axis=1).astype(jnp.bfloat16)
+    return jnp.concatenate(fields, axis=0)
 
 
 def gelu_parts(pre_act):
@@ -180,12 +178,39 @@
     return value, normal_cdf + pre_act * bell * 0.3989422804014327
 
 
-def analyze_kernel(x_parts, y_parts, grid_ref, plane_ref, depth_ref, cos_ref, sin_ref, out_ref):
+def lagged(steps, first, second):
+    step_at = pl.program_id(0)
+
+    @pl.when(step_at == 0)
+    def _():
+        first(step_at, None)
+
+    @pl.when((step_at > 0) & (step_at < steps))
+    def _():
+        first(step_at, second)
+
+    @pl.when(step_at == steps)
+    def _():
+        second(step_at - 1)
+
+
+def analyze_kernel(
+    x_parts, y_parts, grid_ref, plane_ref, depth_ref, cos_ref, sin_ref, out_ref, sums_ref
+):
     cells = grid_ref.shape[1] * grid_ref.shape[2]
-    grids = jnp.concatenate(
-        [grid_ref[chan].reshape(cells, NZ) for chan in range(PAIR)], axis=1
-    )
-    analyze_pair(grids, plane_ref, depth_ref, cos_ref, sin_ref, out_ref, x_parts, y_parts)
+
+    def second(step_at):
+        finish_pair(
+            sums_ref[...], depth_ref, cos_ref, sin_ref, out_ref, step_at * PAIR, x_parts, y_parts
+        )
+
+    def first(step_at, earlier):
+        if earlier is not None:
+            earlier(step_at - 1)
+        grids = [grid_ref[chan].reshape(cells, NZ) for chan in range(PAIR)]
+        sums_ref[...] = f32_dot(plane_ref[...], jnp.concatenate(grids, axis=1))
+
+    lagged(pl.num_programs(0) - 1, first, second)
 
 
 def activate_kernel(
@@ -201,38 +226,79 @@
     sin_ref,
     *rest,
 ):
-    value_ref, out_ref, grad_ref = rest[-3:]
-    fields = depth_fields(spec_ref, back_depth_ref, cos_ref, sin_ref, x_parts, y_parts)
+    value_ref, out_ref, early_ref, late_ref = rest[-4:]
     x_len, y_len = cot_ref.shape[1], cot_ref.shape[2]
+    block = min(16, x_len)
     step = min(8, x_len)
-    for x_at in range(0, x_len, step):
+
+    def activate(fields, new_ref, chan_at, x_at):
         rows = slice(x_at * y_len, (x_at + step) * y_len)
-        pre_act = f32_dot(back_ref[rows], fields)
+        pre_act = f32_dot(back_ref[rows], fields, NT)
         for chan in range(PAIR):
             lanes = slice(chan * NZ, (chan + 1) * NZ)
             value, slope = gelu_parts(pre_act[:, lanes])
-            value_ref[chan, x_at : x_at + step] = value.astype(jnp.bfloat16).reshape(step, y_len, NZ)
-            cotangent = cot_ref[chan, x_at : x_at + step].reshape(step * y_len, NZ)
-            grad_ref[rows, lanes] = (cotangent.astype(jnp.float32) * slope).astype(jnp.bfloat16)
-    analyze_pair(
-        grad_ref[...], plane_ref, depth_ref, cos_ref, sin_ref, out_ref, x_parts, y_parts
-    )
+            here = (chan_at + chan, slice(x_at, x_at + step))
+            value_ref[here] = value.astype(jnp.bfloat16).reshape(step, y_len, NZ)
+            cotangent = cot_ref[here].reshape(step * y_len, NZ).astype(jnp.float32)
+            new_ref[rows, lanes] = (cotangent * slope).astype(jnp.bfloat16)
+
+    def stage(fields, new_ref, chan_at, old_ref, old_first):
+        sums = None
+        for x_at in range(0, x_len, block):
+            if old_ref is not None:
+                rows = slice(x_at * y_len, (x_at + block) * y_len)
+                part = f32_dot(plane_ref[:, rows], old_ref[rows])
+                sums = part if sums is None else sums + part
+            if fields is not None:
+                for at in range(x_at, x_at + block, step):
+                    activate(fields, new_ref, chan_at, at)
+        if old_ref is not None:
+            finish_pair(
+                sums, depth_ref, cos_ref, sin_ref, out_ref, old_first, x_parts, y_parts
+            )
+
+    def second(step_at):
+        stage(None, None, None, late_ref, (2 * step_at + 1) * PAIR)
+
+    def first(step_at, earlier):
+        fields = [
+            depth_fields(spec_ref, back_depth_ref, cos_ref, sin_ref, x_parts, y_parts, first)
+            for first in (0, PAIR)
+        ]
+        if earlier is None:
+            stage(fields[0], early_ref, 0, None, None)
+        else:
+            stage(fields[0], early_ref, 0, late_ref, (2 * step_at - 1) * PAIR)
+        stage(fields[1], late_ref, PAIR, early_ref, 2 * step_at * PAIR)
+
+    lagged(pl.num_programs(0) - 1, first, second)
 
 
 def synthesize_kernel(
     x_parts, y_parts, spec_ref, back_ref, depth_ref, cos_ref, sin_ref, *rest
 ):
-    out_ref = rest[-1]
-    fields = depth_fields(spec_ref, depth_ref, cos_ref, sin_ref, x_parts, y_parts)
+    out_ref, fields_ref = rest[-2:]
     x_len, y_len = out_ref.shape[1], out_ref.shape[2]
     step = min(8, x_len)
-    for x_at in range(0, x_len, step):
-        rows = slice(x_at * y_len, (x_at + step) * y_len)
-        grid = f32_dot(back_ref[rows], fields)
-        for chan in range(PAIR):
-            out_ref[chan, x_at : x_at + step] = (
-                grid[:, chan * NZ : (chan + 1) * NZ].astype(jnp.bfloat16).reshape(step, y_len, NZ)
-            )
+
+    def second(step_at):
+        for x_at in range(0, x_len, step):
+            rows = slice(x_at * y_len, (x_at + step) * y_len)
+            grid = f32_dot(back_ref[rows], fields_ref[...], NT)
+            for chan in range(PAIR):
+                out_ref[chan, x_at : x_at + step] = (
+                    grid[:, chan * NZ : (chan + 1) * NZ]
+                    .astype(jnp.bfloat16)
+                    .reshape(step, y_len, NZ)
+                )
+
+    def first(step_at, earlier):
+        fields = depth_fields(spec_ref, depth_ref, cos_ref, sin_ref, x_parts, y_parts)
+        if earlier is not None:
+            earlier(step_at - 1)
+        fields_ref[...] = fields
+
+    lagged(pl.num_programs(0) - 1, first, second)
 
 
 def mode_rows(value, spread_ref):
@@ -364,7 +430,6 @@
     shift_cos = lax.dynamic_index_in_dim(jnp.asarray(cosines), place, 0, False)
     shift_sin = lax.dynamic_index_in_dim(jnp.asarray(sines), place, 0, False)
 
-    pair_spec = pl.BlockSpec((parts, PAIR, mode_len, 128), lambda at: (0, at, 0, 0))
     grid_shape = jax.ShapeDtypeStruct((chan_len, x_len, y_len, NZ), jnp.bfloat16)
     grid_bytes = x_len * y_len * NZ * 2
     plane_flops = 2 * 2 * MX * MY * x_len * y_len * NZ * 2
@@ -372,16 +437,24 @@
     def spec_shape(size):
         return jax.ShapeDtypeStruct((parts, size, mode_len, 128), jnp.bfloat16)
 
-    def pair_grid(start):
+    def spec_blocks(size, width):
+        last = size // width - 1
         return pl.BlockSpec(
-            (PAIR, x_len, y_len, NZ), lambda at: (at + start // PAIR, 0, 0, 0)
+            (parts, width, mode_len, 128), lambda at: (0, jnp.minimum(at, last), 0, 0)
+        )
+
+    def grid_blocks(start, size, width, lag=0):
+        last = size // width - 1
+        return pl.BlockSpec(
+            (width, x_len, y_len, NZ),
+            lambda at: (jnp.clip(at - lag, 0, last) + start // width, 0, 0, 0),
         )
 
     def tables_of(*arrays):
         return [whole_spec(array) for array in arrays]
 
     def call(
-        body, name, size, operands, specs, earlier, out_shapes, out_specs, scratch, flops, moved
+        body, name, size, width, operands, specs, earlier, out_shapes, out_specs, scratch, flops, moved
     ):
         aliases = {}
         if earlier is not None:
@@ -391,7 +464,7 @@
         return pl.pallas_call(
             functools.partial(body, x_parts, y_parts),
             name=name,
-            grid=(size // PAIR,),
+            grid=(size // width + 1,),
             in_specs=specs,
             out_specs=out_specs,
             out_shape=out_shapes,
@@ -449,12 +522,13 @@
             analyze_kernel,
             "analyze_field",
             stop - start,
+            PAIR,
             (field[0], *tables),
-            [pair_grid(start), *tables_of(*tables)],
+            [grid_blocks(start, stop - start, PAIR), *tables_of(*tables)],
             None,
             spec_shape(stop - start),
-            pair_spec,
-            [],
+            whole_spec(spec_shape(stop - start)),
+            [pltpu.VMEM((2 * MX * MY, PAIR * NZ), jnp.float32)],
             plane_flops,
             grid_bytes,
         )
@@ -472,12 +546,17 @@
             activate_kernel,
             "activate",
             stop - start,
+            2 * PAIR,
             (gathered[chunk], cotangent[0], *tables),
-            [pair_spec, pair_grid(start), *tables_of(*tables)],
+            [
+                spec_blocks(stop - start, 2 * PAIR),
+                grid_blocks(start, stop - start, 2 * PAIR),
+                *tables_of(*tables),
+            ],
             out_grid,
             [grid_shape, spec_shape(stop - start)],
-            [pair_grid(start), pair_spec],
-            [pltpu.VMEM((x_len * y_len, PAIR * NZ), jnp.bfloat16)],
+            [grid_blocks(start, stop - start, 2 * PAIR), whole_spec(spec_shape(stop - start))],
+            [pltpu.VMEM((x_len * y_len, PAIR * NZ), jnp.bfloat16) for _ in range(2)],
             4 * plane_flops,
             2 * grid_bytes,
         )
@@ -518,12 +597,13 @@
             synthesize_kernel,
             "synthesize_grad",
             stop - start,
+            PAIR,
             (gathered[chunk], *tables),
-            [pair_spec, *tables_of(*tables)],
+            [spec_blocks(stop - start, PAIR), *tables_of(*tables)],
             grad_grid,
             grid_shape,
-            pair_grid(start),
-            [],
+            grid_blocks(start, stop - start, PAIR, 1),
+            [pltpu.VMEM((PAIR * NZ, 2 * MX * MY), jnp.bfloat16)],
             plane_flops,
             grid_bytes,
         )

time: 257 us -> 239 us (0.930)
  Pallas kernels: 147 us -> 128 us
    pallas_call x6, Pallas kernels: 122 us -> 103 us  [call(): pl.pallas_call(functools.partial(body, x_parts, y_parts), name=name, grid...]
  transfers between devices with their start and end apart: 7 -> 7, of which waited for: 2 -> 2; matrix products, arithmetic and copies ran while one was open for 0% -> 0% of each run, Pallas kernels for 46% -> 43%
where the time goes in v5:
time: 239 us; the launch traced here: 238 us
  Pallas kernels  128 us (54%)
  blocking collectives  50.5 us (21%)
  starting transfers between devices  26.5 us (11%)
  waiting for transfers between devices  15.8 us (7%)
  between operations  14.1 us (6%)
  local copies, waits for them, and re-layouts  2.9 us (1%)
    pallas_call x6, Pallas kernels, call(): pl.pallas_call(functools.partial(body, x_parts, y_parts), name=name, grid...  103 us
    all_to_all x3, blocking collectives, exchange(): return lax.all_to_all(blocks, ('gx', 'gy'), 0, 0, tiled=True)  50.5 us
    all_to_all x5, starting transfers between devices, exchange(): return lax.all_to_all(blocks, ('gx', 'gy'), 0, 0, tiled=True)  26.2 us
    pallas_call x2, Pallas kernels, mix(): pl.pallas_call(functools.partial(mix_kernel, adjoint, mode_len, step_len,...  19.2 us
    all_to_all x5, waiting for transfers between devices, exchange(): return lax.all_to_all(blocks, ('gx', 'gy'), 0, 0, tiled=True)  14.7 us
    pallas_call x1, Pallas kernels, shards(): pl.pallas_call(weight_kernel, name='weight_terms', grid_spec=pltpu.Prefet...  5.76 us
  transfers between devices with their start and end apart: 7, of which 2 were waited for; matrix products, arithmetic and copies ran while one was open for 0% of the time, Pallas kernels for 43%

profile of v5, /device:TPU:0, one launch (start us, length us, event | category | flops | bytes accessed | tf_op | source)
XLA Modules:
  0.0 238.0 jit_solution(10461527692957773001)
XLA Ops:
  7.2 1.3 dynamic-slice_bitcast_fusion
  8.5 11.4 %analyze_field.2 = bf16[8,16,16,128]{3,2,1,0:T(8,128)(2,1)} custom-call(bf16[32,64,32,128]{3,2,1,0:T(8,128)(2,1)} %bitcast.12, bf16[512,2048]{1,0:T(8,128)(2,1)} %constant.49.clone.plane_ref, bf16[64,256]{1,0:T(8,128)(2,1)} %constant.50.clone.depth_ref, f32[1,512]{1,0:T(1,128)} %get-tuple-element.24.cos_ref, f32[1,512]{1,0:T(1,128)} %get-tuple-element.23.sin_ref), custom_call_target="tpu_custom_call" | custom-call | flops 8589934592 | bytes 8388608 | tf_op jit(solution)/shard_map/analyze_field/pallas_call | solution.py:464
  19.9 7.3 %all-to-all-start = ((bf16[8,16,16,128]{3,2,1,0:T(8,128)(2,1)}), bf16[8,16,16,128]{3,2,1,0:T(8,128)(2,1)S(1)}, u32[]{:S(2)}, u32[]{:S(2)}) async-start(bf16[8,16,16,128]{3,2,1,0:T(8,128)(2,1)} %analyze_field.2), calls=%async_computation | async-start | bytes 1048576 | tf_op jit(solution)/shard_map/all_to_all | solution.py:507
  27.2 11.4 %analyze_field.3 = bf16[8,16,16,128]{3,2,1,0:T(8,128)(2,1)} custom-call(bf16[32,64,32,128]{3,2,1,0:T(8,128)(2,1)} %bitcast.13, bf16[512,2048]{1,0:T(8,128)(2,1)} %constant.49.clone.plane_ref, bf16[64,256]{1,0:T(8,128)(2,1)} %constant.50.clone.depth_ref, f32[1,512]{1,0:T(1,128)} %get-tuple-element.24.cos_ref, f32[1,512]{1,0:T(1,128)} %get-tuple-element.23.sin_ref), custom_call_target="tpu_custom_call" | custom-call | flops 8589934592 | bytes 8388608 | tf_op jit(solution)/shard_map/analyze_field/pallas_call | solution.py:464
  38.6 4.0 %all-to-all-done.refs_0_ = bf16[8,16,16,128]{3,2,1,0:T(8,128)(2,1)S(1)} async-done(((bf16[8,16,16,128]{3,2,1,0:T(8,128)(2,1)}), bf16[8,16,16,128]{3,2,1,0:T(8,128)(2,1)S(1)}, u32[]{:S(2)}, u32[]{:S(2)}) %all-to-all-start) | async-done | bytes 524320 | tf_op jit(solution)/shard_map/all_to_all | solution.py:507
  42.5 0.0 copy-start.4
  42.5 18.3 %all_to_all.40.refs_1_ = bf16[8,16,16,128]{3,2,1,0:T(8,128)(2,1)} all-to-all(bf16[8,16,16,128]{3,2,1,0:T(8,128)(2,1)} %analyze_field.3), channel_id=1, replica_groups=mesh['dp'=4,'gx'=2,'gy'=4] {'gx','gy'}, dimensions={0} | all-to-all | bytes 1048576 | tf_op jit(solution)/shard_map/all_to_all | solution.py:507
  60.9 0.0 copy-done.4
  60.9 8.9 %mix_forward.1 = (f32[4,4,32,128]{3,2,1,0:T(8,128)}, bf16[8,16,16,128]{3,2,1,0:T(8,128)(2,1)}, bf16[8,16,16,128]{3,2,1,0:T(8,128)(2,1)}) custom-call(bf16[8,16,16,128]{3,2,1,0:T(8,128)(2,1)} %copy-done.4, bf16[8,16,16,128]{3,2,1,0:T(8,128)(2,1)} %all_to_all.40.refs_1_, f32[4,16,16,2,1024]{4,3,2,1,0:T(2,128)} %refs_2_.3, ...), custom_call_target="tpu_custom_call" | custom-call | flops 3200000000 | bytes 8388608 | tf_op jit(solution)/shard_map/mix_forward/pallas_call | solution.py:492
  69.7 16.9 %all_to_all.41.spec_ref = bf16[8,16,16,128]{3,2,1,0:T(8,128)(2,1)} all-to-all(bf16[8,16,16,128]{3,2,1,0:T(8,128)(2,1)} %get-tuple-element.14), channel_id=1, replica_groups=mesh['dp'=4,'gx'=2,'gy'=4] {'gx','gy'}, dimensions={0} | all-to-all | bytes 1048576 | tf_op jit(solution)/shard_map/all_to_all | solution.py:507
  86.7 3.7 %all-to-all-start.2 = ((bf16[8,16,16,128]{3,2,1,0:T(8,128)(2,1)}), bf16[8,16,16,128]{3,2,1,0:T(8,128)(2,1)S(1)}, u32[]{:S(2)}, u32[]{:S(2)}) async-start(bf16[8,16,16,128]{3,2,1,0:T(8,128)(2,1)} %get-tuple-element.13), calls=%async_computation.2 | async-start | bytes 1048576 | tf_op jit(solution)/shard_map/all_to_all | solution.py:507
  90.3 28.9 %activate.2 = (bf16[32,64,32,128]{3,2,1,0:T(8,128)(2,1)}, bf16[8,16,16,128]{3,2,1,0:T(8,128)(2,1)}) custom-call(bf16[8,16,16,128]{3,2,1,0:T(8,128)(2,1)} %all_to_all.41.spec_ref, bf16[32,64,32,128]{3,2,1,0:T(8,128)(2,1)} %bitcast.14, bf16[2048,512]{1,0:T(8,128)(2,1)} %constant.48.clone.back_ref, bf16[128,192]{1,0:T(8,128)(2,1)} %constant.52.clone.back_depth_ref, ...), custom_call_target="tpu_custom_call" | custom-call | flops 34359738368 | bytes 16777216 | tf_op jit(solution)/shard_map/activate/pallas_call | solution.py:464
  119.3 0.0 all-to-all-done.2.spec_ref
  119.3 0.0 copy-start.3
  119.3 5.8 %all-to-all-start.4 = ((bf16[8,16,16,128]{3,2,1,0:T(8,128)(2,1)}), bf16[8,16,16,128]{3,2,1,0:T(8,128)(2,1)S(1)}, u32[]{:S(2)}, u32[]{:S(2)}) async-start(bf16[8,16,16,128]{3,2,1,0:T(8,128)(2,1)} %get-tuple-element.17), calls=%async_computation.4 | async-start | bytes 1048576 | tf_op jit(solution)/shard_map/all_to_all | solution.py:507
  125.1 0.0 copy-done.3
  125.1 29.0 %activate.3 = (bf16[32,64,32,128]{3,2,1,0:T(8,128)(2,1)}, bf16[8,16,16,128]{3,2,1,0:T(8,128)(2,1)}) custom-call(bf16[8,16,16,128]{3,2,1,0:T(8,128)(2,1)} %copy-done.3, bf16[32,64,32,128]{3,2,1,0:T(8,128)(2,1)} %bitcast.15, bf16[2048,512]{1,0:T(8,128)(2,1)} %constant.48.clone.back_ref, ...), custom_call_target="tpu_custom_call", output_to_operand_aliasing={{0}: (8, {})} | custom-call | flops 34359738368 | bytes 16777216 | tf_op jit(solution)/shard_map/activate/pallas_call | solution.py:464
  154.0 0.0 all-to-all-done.4.refs_0_
  154.0 0.0 copy-start.1
  154.0 6.0 %all-to-all-start.5 = ((bf16[8,16,16,128]{3,2,1,0:T(8,128)(2,1)}), bf16[8,16,16,128]{3,2,1,0:T(8,128)(2,1)S(1)}, u32[]{:S(2)}, u32[]{:S(2)}) async-start(bf16[8,16,16,128]{3,2,1,0:T(8,128)(2,1)} %get-tuple-element.18), calls=%async_computation.5 | async-start | bytes 1048576 | tf_op jit(solution)/shard_map/all_to_all | solution.py:507
  160.0 0.3 all-gather.5.cloned.1.call-start
  160.3 0.4 all-gather.5.cloned.1.call-update
  160.8 10.7 %all-to-all-done.5.refs_1_ = bf16[8,16,16,128]{3,2,1,0:T(8,128)(2,1)S(1)} async-done(((bf16[8,16,16,128]{3,2,1,0:T(8,128)(2,1)}), bf16[8,16,16,128]{3,2,1,0:T(8,128)(2,1)S(1)}, u32[]{:S(2)}, u32[]{:S(2)}) %all-to-all-start.5) | async-done | bytes 524320 | tf_op jit(solution)/shard_map/all_to_all | solution.py:507
  171.5 0.0 copy-done.1
  171.5 0.0 copy-start.2
  171.5 0.8 copy-done.2
  172.3 10.4 %mix_adjoint.1 = (f32[4,4,32,128]{3,2,1,0:T(8,128)}, bf16[8,16,16,128]{3,2,1,0:T(8,128)(2,1)}, bf16[8,16,16,128]{3,2,1,0:T(8,128)(2,1)}) custom-call(bf16[8,16,16,128]{3,2,1,0:T(8,128)(2,1)} %copy-done.1, bf16[8,16,16,128]{3,2,1,0:T(8,128)(2,1)} %copy-done.2, f32[4,16,16,2,1024]{4,3,2,1,0:T(2,128)} %refs_2_.3, ...), custom_call_target="tpu_custom_call" | custom-call | flops 3200000000 | bytes 8388608 | tf_op jit(solution)/shard_map/mix_adjoint/pallas_call | solution.py:492
  182.7 15.3 %all_to_all.42.spec_ref = bf16[8,16,16,128]{3,2,1,0:T(8,128)(2,1)} all-to-all(bf16[8,16,16,128]{3,2,1,0:T(8,128)(2,1)} %get-tuple-element.20), channel_id=1, replica_groups=mesh['dp'=4,'gx'=2,'gy'=4] {'gx','gy'}, dimensions={0} | all-to-all | bytes 1048576 | tf_op jit(solution)/shard_map/all_to_all | solution.py:507
  198.0 3.5 %all-to-all-start.6 = ((bf16[8,16,16,128]{3,2,1,0:T(8,128)(2,1)}), bf16[8,16,16,128]{3,2,1,0:T(8,128)(2,1)S(1)}, u32[]{:S(2)}, u32[]{:S(2)}) async-start(bf16[8,16,16,128]{3,2,1,0:T(8,128)(2,1)} %get-tuple-element.19), calls=%async_computation.6 | async-start | bytes 1048576 | tf_op jit(solution)/shard_map/all_to_all | solution.py:507
  201.5 0.0 all-gather.7.cloned.1.call-start
  201.5 0.7 all-gather.7.cloned.1.call-update
  202.2 11.2 %synthesize_grad.2.rest_0_ = bf16[32,64,32,128]{3,2,1,0:T(8,128)(2,1)} custom-call(bf16[8,16,16,128]{3,2,1,0:T(8,128)(2,1)} %all_to_all.42.spec_ref, bf16[2048,512]{1,0:T(8,128)(2,1)} %constant.48.clone.back_ref, bf16[128,192]{1,0:T(8,128)(2,1)} %constant.53.clone.depth_ref, f32[1,512]{1,0:T(1,128)} %get-tuple-element.24.cos_ref, ...), custom_call_target="tpu_custom_call" | custom-call | flops 8589934592 | bytes 8388608 | tf_op jit(solution)/shard_map/synthesize_grad/pallas_call | solution.py:464
  213.4 0.0 all-to-all-done.6.spec_ref
  213.4 0.0 copy-start
  213.4 0.8 copy-done
  214.2 11.1 %synthesize_grad.3 = bf16[32,64,32,128]{3,2,1,0:T(8,128)(2,1)} custom-call(bf16[8,16,16,128]{3,2,1,0:T(8,128)(2,1)} %copy-done, bf16[2048,512]{1,0:T(8,128)(2,1)} %constant.48.clone.back_ref, bf16[128,192]{1,0:T(8,128)(2,1)} %constant.53.clone.depth_ref, f32[1,512]{1,0:T(1,128)} %get-tuple-element.24.cos_ref, ...), custom_call_target="tpu_custom_call", output_to_operand_aliasing={{}: (5, {})} | custom-call | flops 8589934592 | bytes 8388608 | tf_op jit(solution)/shard_map/synthesize_grad/pallas_call | solution.py:464
  225.4 0.0 all-gather.5.cloned.1.call-done
  225.4 0.0 all-gather.7.cloned.1.call-done
  225.4 5.8 %weight_terms.1 = f32[4,16,4,2,1024]{4,3,2,1,0:T(2,128)} custom-call(s32[1]{0:T(128)} %bitcast.6.rank_ref, f32[4,4,4,32,128]{4,3,2,1,0:T(8,128)} %bitcast.16, f32[4,4,4,32,128]{4,3,2,1,0:T(8,128)} %bitcast.17, bf16[64,1024]{1,0:T(8,128)(2,1)} %constant.57.clone.refs_3_.spread_u_ref, bf16[64,1024]{1,0:T(8,128)(2,1)} %constant.58.clone.refs_3_.spread_g_ref), custom_call_target="tpu_custom_call" | custom-call | flops 3200000000 | bytes 32000000 | tf_op jit(solution)/shard_map/weight_terms/pallas_call | solution.py:574
Async XLA Ops:
  19.9 22.7 %all-to-all-start = ((bf16[8,16,16,128]{3,2,1,0:T(8,128)(2,1)}), bf16[8,16,16,128]{3,2,1,0:T(8,128)(2,1)S(1)}, u32[]{:S(2)}, u32[]{:S(2)}) async-start(bf16[8,16,16,128]{3,2,1,0:T(8,128)(2,1)} %analyze_field.2), calls=%async_computation | async-start | bytes 1048576 | tf_op jit(solution)/shard_map/all_to_all | solution.py:507
  42.5 18.3 %copy-start.4 = (bf16[8,16,16,128]{3,2,1,0:T(8,128)(2,1)}, bf16[8,16,16,128]{3,2,1,0:T(8,128)(2,1)S(1)}, u32[]{:S(2)}) copy-start(bf16[8,16,16,128]{3,2,1,0:T(8,128)(2,1)S(1)} %all-to-all-done.refs_0_) | copy-start | bytes 1572868
  86.7 32.6 %all-to-all-start.2 = ((bf16[8,16,16,128]{3,2,1,0:T(8,128)(2,1)}), bf16[8,16,16,128]{3,2,1,0:T(8,128)(2,1)S(1)}, u32[]{:S(2)}, u32[]{:S(2)}) async-start(bf16[8,16,16,128]{3,2,1,0:T(8,128)(2,1)} %get-tuple-element.13), calls=%async_computation.2 | async-start | bytes 1048576 | tf_op jit(solution)/shard_map/all_to_all | solution.py:507
  119.3 5.8 %copy-start.3 = (bf16[8,16,16,128]{3,2,1,0:T(8,128)(2,1)}, bf16[8,16,16,128]{3,2,1,0:T(8,128)(2,1)S(1)}, u32[]{:S(2)}) copy-start(bf16[8,16,16,128]{3,2,1,0:T(8,128)(2,1)S(1)} %all-to-all-done.2.spec_ref) | copy-start | bytes 1572868
  119.3 34.7 %all-to-all-start.4 = ((bf16[8,16,16,128]{3,2,1,0:T(8,128)(2,1)}), bf16[8,16,16,128]{3,2,1,0:T(8,128)(2,1)S(1)}, u32[]{:S(2)}, u32[]{:S(2)}) async-start(bf16[8,16,16,128]{3,2,1,0:T(8,128)(2,1)} %get-tuple-element.17), calls=%async_computation.4 | async-start | bytes 1048576 | tf_op jit(solution)/shard_map/all_to_all | solution.py:507
  154.0 17.5 %copy-start.1 = (bf16[8,16,16,128]{3,2,1,0:T(8,128)(2,1)}, bf16[8,16,16,128]{3,2,1,0:T(8,128)(2,1)S(1)}, u32[]{:S(2)}) copy-start(bf16[8,16,16,128]{3,2,1,0:T(8,128)(2,1)S(1)} %all-to-all-done.4.refs_0_) | copy-start | bytes 1572868
  154.0 17.5 %all-to-all-start.5 = ((bf16[8,16,16,128]{3,2,1,0:T(8,128)(2,1)}), bf16[8,16,16,128]{3,2,1,0:T(8,128)(2,1)S(1)}, u32[]{:S(2)}, u32[]{:S(2)}) async-start(bf16[8,16,16,128]{3,2,1,0:T(8,128)(2,1)} %get-tuple-element.18), calls=%async_computation.5 | async-start | bytes 1048576 | tf_op jit(solution)/shard_map/all_to_all | solution.py:507
  160.0 65.3 %all-gather.5.cloned.1.call-start = ((), (), s32[]{:S(2)}) async-start(), calls=%async_computation.8 | async-start | bytes 1310720 | tf_op jit(solution)/shard_map/all_gather | solution.py:540
  171.5 0.8 copy-start.2
  198.0 15.4 %all-to-all-start.6 = ((bf16[8,16,16,128]{3,2,1,0:T(8,128)(2,1)}), bf16[8,16,16,128]{3,2,1,0:T(8,128)(2,1)S(1)}, u32[]{:S(2)}, u32[]{:S(2)}) async-start(bf16[8,16,16,128]{3,2,1,0:T(8,128)(2,1)} %get-tuple-element.19), calls=%async_computation.6 | async-start | bytes 1048576 | tf_op jit(solution)/shard_map/all_to_all | solution.py:507
  201.5 23.9 %all-gather.7.cloned.1.call-start = ((), (), s32[]{:S(2)}) async-start(), calls=%async_computation.9 | async-start | bytes 1310720 | tf_op jit(solution)/shard_map/all_gather | solution.py:569
  213.4 0.8 copy-start
Sparse Core Ops, SparseCore 0:
  162.4 18.1 all-gather.4
  203.9 18.0 all-gather.6
